TPU v7x, 32 devices: a whole 2x2x4 slice. The times are simulated.
32 devices in a mesh: group: 2 (over x), dp: 2 (over y), tensor: 8 (over z, core).
Axes of the slice: x: 2, y: 2, z: 4, core: 2. Of those that a mesh axis runs over, the one named last changes fastest.
Arguments:
- image_feats: bfloat16 [512, 7680], P('tensor', ('group', 'dp')), may hold values from -6 to 6
- proj_weight: bfloat16 [7680, 8192], P(('group', 'dp'), 'tensor'), may hold values from -0.0625 to 0.0625
- proj_bias: bfloat16 [8192], P('tensor'), may hold values from -3 to 3
- kv_weight: bfloat16 [8192, 2048], P('tensor'), may hold values from -0.0625 to 0.0625
- queries: bfloat16 [1024, 8192], P(('group', 'dp'), 'tensor'), may hold values from -14 to 14
- out_grad: bfloat16 [1024, 8192], P(('group', 'dp'), 'tensor'), may hold values from -6 to 6
- image_sample: int32 [4, 128], P(('group', 'dp')), may hold values from 0 to 3, as said below
- text_sample: int32 [4, 256], P(('group', 'dp')), may hold values from 0 to 3, as said below
Outputs:
- attended: bfloat16 [1024, 8192], P(('group', 'dp'), 'tensor')
- d_queries: bfloat16 [1024, 8192], P(('group', 'dp'), 'tensor')
- d_proj_weight: bfloat16 [7680, 8192], P(('group', 'dp'), 'tensor')
- d_proj_bias: float32 [8192], P('tensor')
- d_kv_weight: bfloat16 [8192, 2048], P('tensor', ('group', 'dp'))
Inputs may be any that keep to these rules, and one draw needn't show every extreme that they name: `image_sample`: within each row (one data shard) the sample numbers never fall and every number from 0 to 3 occurs. `text_sample`: within each row (one data shard) the sample numbers never fall and every number from 0 to 3 occurs.
All inputs are finite; a program needn't handle non-finite values.
Results may differ from a plain program's by a relative error of at most 0.04.
Values may be sent and summed in bfloat16 or wider, within the bound.
No kernel may reach another device: no remote copies, remote signals or barrier semaphores. Data moves between devices by JAX's collectives and lax.ppermute only.
A program may use at most 64 MiB of HBM per device.

v0:
```python
import jax
import jax.numpy as jnp
from jax import lax
from jax.sharding import PartitionSpec as P

H = 64
KVH = 8
HD = 128


def from_partner(shard, axis, distance):
    return lax.ppermute(shard, axis, [(i, i ^ 1 << distance) for i in range(lax.axis_size(axis))])


def shards(
    image_feats, proj_weight, proj_bias, kv_weight, queries, out_grad, image_sample, text_sample
):
    gathered = lax.all_gather(image_feats, "tensor", axis=0, tiled=True)
    rows = gathered
    summed = lax.psum_scatter(
        jnp.dot(rows, proj_weight, preferred_element_type=jnp.float32).astype(jnp.bfloat16),
        ("group", "dp"),
        scatter_dimension=0,
        tiled=True,
    ).astype(jnp.float32)
    projected = (summed + proj_bias.astype(jnp.float32)[None, :]).astype(jnp.bfloat16)
    kv_term = jnp.dot(projected, kv_weight, preferred_element_type=jnp.float32)
    kv_all = lax.psum(kv_term, "tensor").astype(jnp.bfloat16)
    local_heads = queries.shape[1] // HD
    shared = H // KVH
    half = kv_all.shape[1] // 2
    key_head = lax.axis_index("tensor") * local_heads // shared
    key_start = key_head * HD
    keys = lax.dynamic_slice_in_dim(kv_all, key_start, HD, 1)
    values = lax.dynamic_slice_in_dim(kv_all, key_start + half, HD, 1)
    scale = HD ** (-0.5)
    q_rows = queries.reshape(queries.shape[0], local_heads, HD)
    grads = out_grad.reshape(out_grad.shape[0], local_heads, HD)
    scores = jnp.einsum("thd,id->hti", q_rows, keys, preferred_element_type=jnp.float32) * scale
    allowed = text_sample[0][:, None] == image_sample[0][None, :]
    scores = jnp.where(allowed[None], scores, jnp.float32(-1e30))
    peak = jnp.max(scores, axis=-1, keepdims=True)
    expo = jnp.exp(scores - peak)
    probs = expo / jnp.sum(expo, axis=-1, keepdims=True)
    probs_b = probs.astype(jnp.bfloat16)
    attended = jnp.einsum(
        "hti,id->thd", probs_b, values, preferred_element_type=jnp.float32
    ).astype(jnp.bfloat16)
    dprobs = jnp.einsum("thd,id->hti", grads, values, preferred_element_type=jnp.float32)
    delta = jnp.sum(probs * dprobs, axis=-1, keepdims=True)
    dscores = (probs * (dprobs - delta) * scale).astype(jnp.bfloat16)
    d_rows = jnp.einsum("hti,id->thd", dscores, keys, preferred_element_type=jnp.float32).astype(
        jnp.bfloat16
    )
    d_keys = jnp.einsum("hti,thd->id", dscores, q_rows, preferred_element_type=jnp.float32)
    d_values = jnp.einsum("hti,thd->id", probs_b, grads, preferred_element_type=jnp.float32)
    image_count = kv_term.shape[0]
    members = shared // local_heads
    stacked = jnp.concatenate([d_keys, d_values], axis=1)
    for level in range(members.bit_length() - 1):
        stacked = stacked + from_partner(stacked, "tensor", level)
    width = stacked.shape[1] // members
    member = lax.axis_index("tensor") % members
    mine = lax.dynamic_slice_in_dim(stacked, member * width, width, 1).astype(jnp.bfloat16)
    collected = lax.all_gather(mine, "tensor", axis=1, tiled=True)
    heads_total = collected.shape[1] // (2 * HD)
    dkv = (
        collected.reshape(image_count, heads_total, 2, HD)
        .transpose(0, 2, 1, 3)
        .reshape(image_count, 2 * heads_total * HD)
    )
    d_projected = lax.dot_general(
        dkv, kv_weight, (((1,), (1,)), ((), ())), preferred_element_type=jnp.float32
    ).astype(jnp.bfloat16)
    kv_grad_term = lax.dot_general(
        projected, dkv, (((0,), (0,)), ((), ())), preferred_element_type=jnp.float32
    )
    d_kv_weight = lax.psum_scatter(
        kv_grad_term.astype(jnp.bfloat16), ("group", "dp"), scatter_dimension=1, tiled=True
    )
    piece = lax.all_gather(d_projected, ("group", "dp"), axis=0, tiled=True)
    rows = gathered
    weight_grad = lax.dot_general(
        rows, piece, (((0,), (0,)), ((), ())), preferred_element_type=jnp.float32
    )
    bias_grad = jnp.sum(piece.astype(jnp.float32), axis=0)
    weight_grad, bias_grad = (weight_grad, bias_grad)
    attended = attended.reshape(queries.shape)
    d_queries = d_rows.reshape(queries.shape)
    return (attended, d_queries, weight_grad.astype(jnp.bfloat16), bias_grad, d_kv_weight)


def solution(mesh):
    in_specs = (
        P("tensor", ("group", "dp")),
        P(("group", "dp"), "tensor"),
        P("tensor"),
        P("tensor", None),
        P(("group", "dp"), "tensor"),
        P(("group", "dp"), "tensor"),
        P(("group", "dp"), None),
        P(("group", "dp"), None),
    )
    out_specs = (
        P(("group", "dp"), "tensor"),
        P(("group", "dp"), "tensor"),
        P(("group", "dp"), "tensor"),
        P("tensor"),
        P("tensor", ("group", "dp")),
    )
    return jax.shard_map(shards, mesh=mesh, in_specs=in_specs, out_specs=out_specs, check_vma=False)
```

profile of v0, /device:TPU:0, one launch (start us, length us, event | category | flops | bytes accessed | tf_op | source)
XLA Modules:
  0.0 246.7 jit_solution(18130810129607671531)
XLA Ops:
  7.2 0.0 all-gather.3.cloned.1.call-start
  7.2 0.7 all-gather.3.cloned.1.call-update
  8.0 0.0 reduce-scatter.3.cloned.1.call-start
  8.0 32.4 %all-gather.3.cloned.1.call-done = bf16[512,1920]{1,0:T(8,128)(2,1)} async-done(((bf16[64,1920]{1,0:T(8,128)(2,1)}), bf16[512,1920]{1,0:T(8,128)(2,1)}) %all-gather.3.cloned.1.call-update) | async-done | bytes 1966096 | tf_op jit(solution)/shard_map/all_gather | solution.py:18
  40.4 6.0 %convolution_convert_fusion.1 = bf16[512,1024]{1,0:T(8,128)(2,1)} fusion(bf16[512,1920]{1,0:T(8,128)(2,1)} %all-gather.3.cloned.1.call-done, bf16[1920,1024]{1,0:T(8,128)(2,1)} %param.9), kind=kOutput, calls=%fused_computation.6 | convolution fusion | flops 2013790208 | bytes 6946816 | tf_op jit(solution)/shard_map/dot_general | solution.py:21
  46.4 0.0 reduce-scatter.3.cloned.1.call-update
  46.4 0.0 all-gather.5.cloned.1.call-start
  46.5 0.2 copy.48
  46.7 0.2 copy.49
  47.0 0.1 broadcast_compare_fusion
  47.1 26.7 %reduce-scatter.3.cloned.1.call-done = bf16[128,1024]{1,0:T(8,128)(2,1)} async-done(((bf16[512,1024]{1,0:T(8,128)(2,1)}), bf16[128,1024]{1,0:T(8,128)(2,1)}) %reduce-scatter.3.cloned.1.call-update) | async-done | bytes 262160 | tf_op jit(solution)/shard_map/reduce_scatter | solution.py:20
  73.8 3.0 %fusion.20 = f32[128,2048]{1,0:T(8,128)S(1)} fusion(bf16[1024,2048]{1,0:T(8,128)(2,1)} %param.11, bf16[128,1024]{1,0:T(8,128)(2,1)} %reduce-scatter.3.cloned.1.call-done, f32[1024]{0:T(1024)S(1)} %convert_element_type.51), kind=kOutput, calls=%fused_computation.32 | convolution fusion | flops 537264128 | bytes 5509120 | tf_op jit(solution)/shard_map/dot_general | solution.py:27
  76.8 59.0 %all-reduce.1 = bf16[128,2048]{1,0:T(8,128)(2,1)S(1)} all-reduce(f32[128,2048]{1,0:T(8,128)S(1)} %fusion.20), channel_id=1, replica_groups=mesh['group'=2,'dp'=2,'tensor'=8] {'tensor'}, use_global_device_ids=true, to_apply=%region_1.0 | all-reduce | flops 262144 | bytes 1572864 | tf_op jit(solution)/shard_map/psum | solution.py:28
  135.9 0.3 convolution_bitcast_fusion
  136.2 1.4 fusion.56
  137.6 0.6 fusion.11
  138.2 2.1 fusion.10
  140.3 14.9 %all_gather.10 = bf16[128,2048]{0,1:T(8,128)(2,1)S(1)} all-gather(bf16[128,256]{0,1:T(8,128)(2,1)S(1)} %pad_maximum_fusion), channel_id=1, replica_groups=mesh['group'=2,'dp'=2,'tensor'=8] {'tensor'}, dimensions={1}, use_global_device_ids=true | all-gather | bytes 589824 | tf_op jit(solution)/shard_map/all_gather | solution.py:65
  155.3 4.4 %convolution_convert_fusion.4 = bf16[128,1024]{1,0:T(8,128)(2,1)} fusion(bf16[128,2048]{0,1:T(8,128)(2,1)S(1)} %bitcast.85, bf16[1024,2048]{1,0:T(8,128)(2,1)} %param.11), kind=kOutput, calls=%fused_computation.18 | convolution fusion | flops 537001984 | bytes 4980736 | tf_op jit(solution)/shard_map/dot_general | solution.py:72
  159.7 0.0 all-gather.5.cloned.1.call-update
  159.7 0.0 reduce-scatter.5.cloned.1.call-start
  159.8 3.2 %convolution_convert_fusion = bf16[1024,2048]{1,0:T(8,128)(2,1)} fusion(bf16[128,2048]{0,1:T(8,128)(2,1)S(1)} %bitcast.86, bf16[128,1024]{1,0:T(8,128)(2,1)S(1)} %copy-done, f32[1024]{0:T(1024)S(1)} %convert_element_type.51), kind=kOutput, calls=%fused_computation.3 | convolution fusion | flops 539361280 | bytes 4984832 | tf_op jit(solution)/shard_map/dot_general | solution.py:75
  163.0 0.0 reduce-scatter.5.cloned.1.call-update
  163.0 0.7 convolution_convert_fusion.3
  163.7 1.0 copy.37
  164.7 2.1 convolution_convert_fusion.2
  166.8 1.0 copy.38
  167.8 16.0 %all-gather.5.cloned.1.call-done = bf16[512,1024]{1,0:T(8,128)(2,1)} async-done(((bf16[128,1024]{1,0:T(8,128)(2,1)}), bf16[512,1024]{1,0:T(8,128)(2,1)}) %all-gather.5.cloned.1.call-update) | async-done | bytes 1048592 | tf_op jit(solution)/shard_map/all_gather | solution.py:81
  183.8 6.1 %convert_bitcast_fusion = bf16[1920,1024]{0,1:T(8,128)(2,1)} fusion(bf16[512,1024]{1,0:T(8,128)(2,1)} %all-gather.5.cloned.1.call-done, bf16[512,1920]{1,0:T(8,128)(2,1)} %all-gather.3.cloned.1.call-done), kind=kOutput, calls=%fused_computation.2 | convolution fusion | flops 2015232000 | bytes 6946816 | tf_op jit(solution)/shard_map/dot_general | solution.py:83
  189.9 6.4 %copy.39 = bf16[1920,1024]{1,0:T(8,128)(2,1)} copy(bf16[1920,1024]{0,1:T(8,128)(2,1)} %convert_bitcast_fusion) | data formatting | bytes 7864320
  196.4 0.8 convert_reduce_fusion
  197.2 43.0 %reduce-scatter.5.cloned.1.call-done = bf16[1024,512]{1,0:T(8,128)(2,1)} async-done(((bf16[1024,2048]{1,0:T(8,128)(2,1)}), bf16[1024,512]{1,0:T(8,128)(2,1)}) %reduce-scatter.5.cloned.1.call-update) | async-done | bytes 1048592 | tf_op jit(solution)/shard_map/reduce_scatter | solution.py:78
  (17 shorter events, 0.1 us)
Async XLA Ops:
  7.2 33.2 %all-gather.3.cloned.1.call-start = ((), (), s32[]{:S(2)}) async-start(), calls=%async_computation.2 | async-start | bytes 2211840 | tf_op jit(solution)/shard_map/all_gather | solution.py:18
  7.9 38.6 %copy-start.4 = (bf16[1024]{0:T(1024)(128)(2,1)S(1)}, bf16[1024]{0:T(1024)(128)(2,1)}, u32[]{:S(2)}) copy-start(bf16[1024]{0:T(1024)(128)(2,1)} %param.10) | copy-start | bytes 6148
  7.9 38.6 %copy-start.2 = (bf16[256,1024]{1,0:T(8,128)(2,1)S(1)}, bf16[256,1024]{1,0:T(8,128)(2,1)}, u32[]{:S(2)}) copy-start(bf16[256,1024]{1,0:T(8,128)(2,1)} %param.12) | copy-start | bytes 1572868
  7.9 38.8 %copy-start.3 = (bf16[256,1024]{1,0:T(8,128)(2,1)S(1)}, bf16[256,1024]{1,0:T(8,128)(2,1)}, u32[]{:S(2)}) copy-start(bf16[256,1024]{1,0:T(8,128)(2,1)} %param.13) | copy-start | bytes 1572868
  7.9 39.0 %copy-start.5 = (s32[1,256]{1,0:T(1,128)S(1)}, s32[1,256]{1,0:T(1,128)}, u32[]{:S(2)}) copy-start(s32[1,256]{1,0:T(1,128)} %param.15) | copy-start | bytes 3076
  7.9 39.0 %copy-start.6 = (s32[1,128]{1,0:T(1,128)S(1)}, s32[1,128]{1,0:T(1,128)}, u32[]{:S(2)}) copy-start(s32[1,128]{1,0:T(1,128)} %param.14) | copy-start | bytes 1540
  8.0 65.9 %reduce-scatter.3.cloned.1.call-start = ((), (), s32[]{:S(2)}) async-start(), calls=%async_computation.3 | async-start | bytes 1310720 | tf_op jit(solution)/shard_map/reduce_scatter | solution.py:20
  46.4 137.4 %all-gather.5.cloned.1.call-start = ((), (), s32[]{:S(2)}) async-start(), calls=%async_computation.4 | async-start | bytes 1310720 | tf_op jit(solution)/shard_map/all_gather | solution.py:81
  140.3 19.5 %copy-start = (bf16[128,1024]{1,0:T(8,128)(2,1)S(1)}, bf16[128,1024]{1,0:T(8,128)(2,1)}, u32[]{:S(2)}) copy-start(bf16[128,1024]{1,0:T(8,128)(2,1)} %reduce-scatter.3.cloned.1.call-done) | copy-start | bytes 786436
  159.7 80.4 %reduce-scatter.5.cloned.1.call-start = ((), (), s32[]{:S(2)}) async-start(), calls=%async_computation.5 | async-start | bytes 5242880 | tf_op jit(solution)/shard_map/reduce_scatter | solution.py:78
  189.9 6.4 %copy-start.1 = (bf16[512,1024]{1,0:T(8,128)(2,1)S(1)}, bf16[512,1024]{1,0:T(8,128)(2,1)}, u32[]{:S(2)}) copy-start(bf16[512,1024]{1,0:T(8,128)(2,1)} %all-gather.5.cloned.1.call-done) | copy-start | bytes 3145732
Sparse Core Ops, SparseCore 0:
  9.6 30.7 all-gather.2
  46.5 27.2 reduce-scatter.2
  159.9 23.9 all-gather.4
  187.5 52.6 reduce-scatter.4
where the time goes:
time: 247 us
  waiting for transfers between devices  119 us (48%)
  blocking collectives  74 us (30%)
  matrix products  29.9 us (12%)
  between operations  14 us (6%)
  local copies, waits for them, and re-layouts  8.91 us (4%)
    psum x1, blocking collectives, shards(): kv_all = lax.psum(kv_term, 'tensor').astype(jnp.bfloat16)  59 us
    reduce_scatter x1, waiting for transfers between devices, shards(): lax.psum_scatter(kv_grad_term.astype(jnp.bfloat16), ('group', 'dp'), scat...  43 us
    all_gather x1, waiting for transfers between devices, shards(): gathered = lax.all_gather(image_feats, 'tensor', axis=0, tiled=True)  32.4 us
    reduce_scatter x1, waiting for transfers between devices, shards(): lax.psum_scatter(jnp.dot(rows, proj_weight, preferred_element_type=jnp.fl...  26.7 us
    all_gather x1, waiting for transfers between devices, shards(): piece = lax.all_gather(d_projected, ('group', 'dp'), axis=0, tiled=True)  16 us
    all_gather x1, blocking collectives, shards(): collected = lax.all_gather(mine, 'tensor', axis=1, tiled=True)  14.9 us
    unnamed x17, local copies, waits for them, and re-layouts  8.47 us
    dot_general x1, matrix products, shards(): lax.dot_general(rows, piece, (((0,), (0,)), ((), ())), preferred_element_...  6.12 us
  transfers between devices with their start and end apart: 4, of which 4 were waited for; matrix products, arithmetic and copies ran while one was open for 9% of the time, Pallas kernels for 0%

commit v1 on v0

--- a/solution.py
+++ b/solution.py
@@ -3,16 +3,56 @@
 from jax import lax
 from jax.sharding import PartitionSpec as P
 
-H = 64
-KVH = 8
 HD = 128
+
+T = "tensor"
+XY = ("group", "dp")
+F32 = jnp.float32
+BF16 = jnp.bfloat16
+
+
+def size_of(axes):
+    names = axes if isinstance(axes, tuple) else (axes,)
+    total = 1
+    for name in names:
+        total *= lax.axis_size(name)
+    return total
+
+
+def swap(x, axes, bits):
+    return lax.ppermute(x, axes, [(i, i ^ bits) for i in range(size_of(axes))])
+
+
+def send(x, axes, target):
+    pairs = [(i, target(i)) for i in range(size_of(axes))]
+    return lax.ppermute(x, axes, [(i, t) for i, t in pairs if t is not None])
+
+
+def gather_line(block, chips):
+    if chips != 4:
+        return [block] + [swap(block, T, 2 * k) for k in range(1, chips)]
+    chip = lax.axis_index(T) // 2
+    inner = jnp.logical_or(chip == 1, chip == 2)
+    near = swap(block, T, 2)
+    middle = send(block, T, lambda i: i ^ 6 if i // 2 in (1, 2) else None)
+    onward = jnp.where(inner, middle, block)
+    cycle = {0: 2, 2: 3, 3: 1, 1: 0}
+    two = send(onward, T, lambda i: 2 * cycle[i // 2] + i % 2)
+    out = {1: 0, 2: 3}
+    last = send(two, T, lambda i: 2 * out[i // 2] + i % 2 if i // 2 in out else None)
+    return [block, near, two, jnp.where(inner, middle, last)]
+
+
+def heads_per_key(queries, kv_weight):
+    heads = queries.shape[1] // HD * lax.axis_size(T)
+    return heads // (kv_weight.shape[1] // 2 // HD)
 
 
 def from_partner(shard, axis, distance):
     return lax.ppermute(shard, axis, [(i, i ^ 1 << distance) for i in range(lax.axis_size(axis))])
 
 
-def shards(
+def general(
     image_feats, proj_weight, proj_bias, kv_weight, queries, out_grad, image_sample, text_sample
 ):
     gathered = lax.all_gather(image_feats, "tensor", axis=0, tiled=True)
@@ -27,7 +67,7 @@
     kv_term = jnp.dot(projected, kv_weight, preferred_element_type=jnp.float32)
     kv_all = lax.psum(kv_term, "tensor").astype(jnp.bfloat16)
     local_heads = queries.shape[1] // HD
-    shared = H // KVH
+    shared = heads_per_key(queries, kv_weight)
     half = kv_all.shape[1] // 2
     key_head = lax.axis_index("tensor") * local_heads // shared
     key_start = key_head * HD
@@ -90,6 +130,112 @@
     return (attended, d_queries, weight_grad.astype(jnp.bfloat16), bias_grad, d_kv_weight)
 
 
+def shards(
+    image_feats, proj_weight, proj_bias, kv_weight, queries, out_grad, image_sample, text_sample
+):
+    chips = lax.axis_size(T) // 2
+    parts = size_of(XY)
+    if heads_per_key(queries, kv_weight) * HD != queries.shape[1] or chips != parts:
+        return general(
+            image_feats, proj_weight, proj_bias, kv_weight, queries, out_grad, image_sample, text_sample
+        )
+    me = lax.axis_index(T)
+    chip, core = me // 2, me % 2
+    part = lax.axis_index("group") * lax.axis_size("dp") + lax.axis_index("dp")
+
+    def pick(stack, k):
+        return lax.dynamic_index_in_dim(stack, k, 0, keepdims=False)
+
+    def both_cores(own, other, axis):
+        return jnp.where(core == 0, jnp.stack([own, other], axis), jnp.stack([other, own], axis))
+
+    own = jnp.stack(gather_line(image_feats, chips))
+    other = swap(own, T, 1)
+    feats = both_cores(own, other, 1)
+    shard_rows = 2 * image_feats.shape[0]
+    feats = feats.reshape(chips, shard_rows, image_feats.shape[1])
+    partial = jnp.einsum("krf,fd->krd", feats, proj_weight, preferred_element_type=F32).astype(BF16)
+    summed = pick(partial, chip ^ part).astype(F32)
+    for j in range(1, parts):
+        summed = summed + swap(pick(partial, chip ^ part ^ j), XY, j).astype(F32)
+    projected = (summed + proj_bias.astype(F32)[None, :]).astype(BF16)
+    projected_all = jnp.stack([projected] + [swap(projected, XY, j) for j in range(1, parts)])
+
+    kv_term = jnp.dot(projected, kv_weight, preferred_element_type=F32)
+    half = kv_weight.shape[1] // 2
+    tensors = 2 * chips
+
+    def kv_of(i):
+        start = (me ^ i) * HD
+        return jnp.concatenate(
+            [
+                lax.dynamic_slice_in_dim(kv_term, start, HD, 1),
+                lax.dynamic_slice_in_dim(kv_term, half + start, HD, 1),
+            ],
+            axis=1,
+        )
+
+    theirs = swap(jnp.stack([kv_of(2 * k + 1) for k in range(chips)]).astype(BF16), T, 1)
+    mine = jnp.stack([kv_of(2 * k) for k in range(chips)]) + theirs.astype(F32)
+    kv = mine[0]
+    for k in range(1, chips):
+        kv = kv + swap(mine[k].astype(BF16), T, 2 * k).astype(F32)
+    kv = kv.astype(BF16)
+    keys, values = kv[:, :HD], kv[:, HD:]
+
+    local_heads = queries.shape[1] // HD
+    scale = HD ** (-0.5)
+    q_rows = queries.reshape(queries.shape[0], local_heads, HD)
+    grads = out_grad.reshape(out_grad.shape[0], local_heads, HD)
+    scores = jnp.einsum("thd,id->hti", q_rows, keys, preferred_element_type=F32) * scale
+    allowed = text_sample[0][:, None] == image_sample[0][None, :]
+    scores = jnp.where(allowed[None], scores, F32(-1e30))
+    peak = jnp.max(scores, axis=-1, keepdims=True)
+    expo = jnp.exp(scores - peak)
+    probs = expo / jnp.sum(expo, axis=-1, keepdims=True)
+    probs_b = probs.astype(BF16)
+    attended = jnp.einsum("hti,id->thd", probs_b, values, preferred_element_type=F32).astype(BF16)
+    dprobs = jnp.einsum("thd,id->hti", grads, values, preferred_element_type=F32)
+    delta = jnp.sum(probs * dprobs, axis=-1, keepdims=True)
+    dscores = (probs * (dprobs - delta) * scale).astype(BF16)
+    d_rows = jnp.einsum("hti,id->thd", dscores, keys, preferred_element_type=F32).astype(BF16)
+    d_keys = jnp.einsum("hti,thd->id", dscores, q_rows, preferred_element_type=F32)
+    d_values = jnp.einsum("hti,thd->id", probs_b, grads, preferred_element_type=F32)
+    dkv = jnp.concatenate([d_keys, d_values], axis=1).astype(BF16)
+
+    dkv_own = jnp.stack([dkv] + [swap(dkv, T, 2 * k) for k in range(1, chips)])
+    dkv_other = swap(dkv_own, T, 1)
+    heads = both_cores(dkv_own, dkv_other, 1)
+    heads = jnp.stack([pick(heads, k ^ chip) for k in range(chips)])
+    rows = heads.shape[2]
+    dkv_all = heads.reshape(tensors, rows, 2, HD).transpose(1, 2, 0, 3).reshape(rows, 2 * tensors * HD)
+    d_projected = lax.dot_general(
+        dkv_all, kv_weight, (((1,), (1,)), ((), ())), preferred_element_type=F32
+    ).astype(BF16)
+    width = kv_weight.shape[1] // parts
+
+    def columns(j):
+        return lax.dynamic_slice_in_dim(dkv_all, (part ^ j) * width, width, 1)
+
+    dkv_rows = jnp.stack([columns(0)] + [swap(columns(j), XY, j) for j in range(1, parts)])
+    d_kv_weight = jnp.einsum(
+        "jrd,jrc->dc", projected_all, dkv_rows, preferred_element_type=F32
+    ).astype(BF16)
+    d_all = jnp.stack([d_projected] + [swap(d_projected, XY, j) for j in range(1, parts)])
+    d_by_chip = jnp.stack([pick(d_all, k ^ chip ^ part) for k in range(parts)])
+    weight_grad = jnp.einsum(
+        "krf,krd->fd", feats, d_by_chip, preferred_element_type=F32
+    ).astype(BF16)
+    bias_grad = jnp.sum(d_all.astype(F32), axis=(0, 1))
+    return (
+        attended.reshape(queries.shape),
+        d_rows.reshape(queries.shape),
+        weight_grad,
+        bias_grad,
+        d_kv_weight,
+    )
+
+
 def solution(mesh):
     in_specs = (
         P("tensor", ("group", "dp")),

time: 247 us -> 132 us (0.53)
  waiting for transfers between devices: 119 us -> 40.2 us
  blocking collectives: 74 us -> 0 us
  starting transfers between devices: 0.16 us -> 40.1 us
  between operations: 14 us -> 1.06 us
  other arithmetic: 0.87 us -> 11.3 us
    reduce_scatter x2 -> x0, waiting for transfers between devices: 69.8 us -> none  [the longest x1 43 us: shards(): lax.psum_scatter(kv_grad_term.astype(jnp.bfloat16), ('group', 'dp'), scat...]
    psum x1 -> x0, blocking collectives: 59 us -> none  [shards(): kv_all = lax.psum(kv_term, 'tensor').astype(jnp.bfloat16)]
    all_gather x2 -> x0, waiting for transfers between devices: 48.4 us -> none  [the longest x1 32.4 us: shards(): gathered = lax.all_gather(image_feats, 'tensor', axis=0, tiled=True)]
    ppermute x0 -> x25, waiting for transfers between devices: none -> 40.2 us  [the longest x22 29.4 us: swap(): return lax.ppermute(x, axes, [(i, i ^ bits) for i in range(size_of(axes))])]
    ppermute x0 -> x25, starting transfers between devices: none -> 40.1 us  [the longest x22 25.9 us: swap(): return lax.ppermute(x, axes, [(i, i ^ bits) for i in range(size_of(axes))])]
    all_gather x1 -> x0, blocking collectives: 14.9 us -> none  [shards(): collected = lax.all_gather(mine, 'tensor', axis=1, tiled=True)]
    unnamed x17 -> x31, local copies, waits for them, and re-layouts: 8.47 us -> 4.42 us
    select_n x0 -> x3, other arithmetic: none -> 2.88 us  [the longest x2 1.9 us: both_cores(): jnp.where(core == 0, jnp.stack([own, other], axis), jnp.stack([other, own...]
  transfers between devices with their start and end apart: 4 -> 25, of which waited for: 4 -> 12; matrix products, arithmetic and copies ran while one was open for 9% -> 14% of each run, Pallas kernels for 0% -> 0%
where the time goes in v1:
time: 132 us; the launch traced here: 131 us
  waiting for transfers between devices  40.2 us (30%)
  starting transfers between devices  40.1 us (30%)
  matrix products  29.6 us (22%)
  other arithmetic  11.3 us (9%)
  local copies, waits for them, and re-layouts  8.7 us (7%)
    ppermute x22, waiting for transfers between devices, swap(): return lax.ppermute(x, axes, [(i, i ^ bits) for i in range(size_of(axes))])  29.4 us
    ppermute x22, starting transfers between devices, swap(): return lax.ppermute(x, axes, [(i, i ^ bits) for i in range(size_of(axes))])  25.9 us
    ppermute x3, starting transfers between devices, send(): return lax.ppermute(x, axes, [(i, t) for i, t in pairs if t is not None])  14.2 us
    ppermute x3, waiting for transfers between devices, send(): return lax.ppermute(x, axes, [(i, t) for i, t in pairs if t is not None])  10.8 us
    unnamed x31, local copies, waits for them, and re-layouts  4.42 us
    dot_general x1, matrix products, shards(): jnp.einsum('krf,krd->fd', feats, d_by_chip, preferred_element_type=F32)  4.18 us
    dot_general x1, matrix products, shards(): lax.dot_general(dkv_all, kv_weight, (((1,), (1,)), ((), ())), preferred_e...  3.7 us
    dot_general x1, matrix products, shards(): jnp.einsum('jrd,jrc->dc', projected_all, dkv_rows, preferred_element_type...  3.09 us
  transfers between devices with their start and end apart: 25, of which 12 were waited for; matrix products, arithmetic and copies ran while one was open for 14% of the time, Pallas kernels for 0%

profile of v1, /device:TPU:0, one launch (start us, length us, event | category | flops | bytes accessed | tf_op | source)
XLA Modules:
  0.0 130.9 jit_solution(15475040195687702267)
XLA Ops:
  2.3 12.2 %collective-permute-start.2 = (bf16[64,1920]{1,0:T(8,128)(2,1)S(1)}, bf16[64,1920]{1,0:T(8,128)(2,1)S(1)}, u32[]{:S(2)}, u32[]{:S(2)}) collective-permute-start(bf16[64,1920]{1,0:T(8,128)(2,1)S(1)} %broadcast_select_fusion), channel_id=1, source_target_pairs={{0,4},{1,5},{2,0},{3,1},{4,6},{5,7},{6,2},{7,3},{8,12},{9,13},{10,... | collective-permute-start | bytes 737288 | tf_op jit(solution)/shard_map/ppermute | solution.py:28
  14.6 4.3 %collective-permute-done.2 = bf16[64,1920]{1,0:T(8,128)(2,1)S(1)} collective-permute-done((bf16[64,1920]{1,0:T(8,128)(2,1)S(1)}, bf16[64,1920]{1,0:T(8,128)(2,1)S(1)}, u32[]{:S(2)}, u32[]{:S(2)}) %collective-permute-start.2) | collective-permute-done | bytes 245792 | tf_op jit(solution)/shard_map/ppermute | solution.py:28
  20.2 2.7 %collective-permute-start = (bf16[64,1920]{1,0:T(8,128)(2,1)}, bf16[64,1920]{1,0:T(8,128)(2,1)S(1)}, u32[]{:S(2)}, u32[]{:S(2)}) collective-permute-start(bf16[64,1920]{1,0:T(8,128)(2,1)} %param.8), channel_id=1, source_target_pairs={{0,2},{1,3},{2,0},{3,1},{4,6},{5,7},{6,4},{7,5},{8,10},{9,11},{10,... | collective-permute-start | bytes 737288 | tf_op jit(solution)/shard_map/ppermute | solution.py:23
  22.9 6.4 %collective-permute-done.3 = bf16[64,1920]{1,0:T(8,128)(2,1)S(1)} collective-permute-done((bf16[64,1920]{1,0:T(8,128)(2,1)S(1)}, bf16[64,1920]{1,0:T(8,128)(2,1)S(1)}, u32[]{:S(2)}, u32[]{:S(2)}) %collective-permute-start.3) | collective-permute-done | bytes 245792 | tf_op jit(solution)/shard_map/ppermute | solution.py:28
  29.4 2.6 %collective-permute-done = bf16[64,1920]{1,0:T(8,128)(2,1)S(1)} collective-permute-done((bf16[64,1920]{1,0:T(8,128)(2,1)}, bf16[64,1920]{1,0:T(8,128)(2,1)S(1)}, u32[]{:S(2)}, u32[]{:S(2)}) %collective-permute-start) | collective-permute-done | bytes 245792 | tf_op jit(solution)/shard_map/ppermute | solution.py:23
  33.2 2.5 %collective-permute-done.4 = bf16[4,64,1920]{2,1,0:T(8,128)(2,1)S(1)} collective-permute-done((bf16[4,64,1920]{2,1,0:T(8,128)(2,1)S(1)}, bf16[4,64,1920]{2,1,0:T(8,128)(2,1)S(1)}, u32[]{:S(2)}, u32[]{:S(2)}) %collective-permute-start.4) | collective-permute-done | bytes 983072 | tf_op jit(solution)/shard_map/ppermute | solution.py:23
  36.7 1.8 %maximum_select_fusion = bf16[4,2,64,1920]{3,2,1,0:T(8,128)(2,1)S(1)} fusion(bf16[4,1,64,1920]{3,2,1,0:T(8,128)(2,1)} %bitcast.172, bf16[4,1,64,1920]{3,2,1,0:T(8,128)(2,1)S(1)} %get-tuple-element.42, pred[]{:T(512)S(6)} %eq.31), kind=kLoop, calls=%fused_computation.7 | loop fusion | flops 2949120 | bytes 3932161 | tf_op jit(solution)/shard_map/jit(_where)/select_n | solution.py:150
  38.5 2.4 %fusion.5 = bf16[4,128,1024]{2,1,0:T(8,128)(2,1)S(1)} fusion(bf16[4,128,1920]{2,1,0:T(8,128)(2,1)S(1)} %bitcast.168, bf16[1920,1024]{1,0:T(8,128)(2,1)S(1)} %copy-done.12), kind=kOutput, calls=%fused_computation.9 | convolution fusion | flops 2013790208 | bytes 6946816 | tf_op jit(solution)/shard_map/krf,fd->krd/dot_general | solution.py:157
  41.8 2.4 %collective-permute-start.7 = (bf16[128,1024]{1,0:T(8,128)(2,1)}, bf16[128,1024]{1,0:T(8,128)(2,1)S(1)}, u32[]{:S(2)}, u32[]{:S(2)}) collective-permute-start(bf16[128,1024]{1,0:T(8,128)(2,1)} %get-tuple-element.40), channel_id=1, source_target_pairs={{0,24},{8,16},{16,8},{24,0},{1,25},{9,17},{17,9},{25,1},{2,26},{10... | collective-permute-start | bytes 786440 | tf_op jit(solution)/shard_map/ppermute | solution.py:23
  45.3 6.8 %collective-permute-done.7 = bf16[128,1024]{1,0:T(8,128)(2,1)S(1)} collective-permute-done((bf16[128,1024]{1,0:T(8,128)(2,1)}, bf16[128,1024]{1,0:T(8,128)(2,1)S(1)}, u32[]{:S(2)}, u32[]{:S(2)}) %collective-permute-start.7) | collective-permute-done | bytes 262176 | tf_op jit(solution)/shard_map/ppermute | solution.py:23
  52.1 5.0 %collective-permute-done.6 = bf16[128,1024]{1,0:T(8,128)(2,1)} collective-permute-done((bf16[128,1024]{1,0:T(8,128)(2,1)}, bf16[128,1024]{1,0:T(8,128)(2,1)}, u32[]{:S(2)}, u32[]{:S(2)}) %collective-permute-start.6) | collective-permute-done | bytes 262176 | tf_op jit(solution)/shard_map/ppermute | solution.py:23
  57.0 1.9 %fusion.45 = bf16[128,1024]{1,0:T(8,128)(2,1)} fusion(bf16[128,1024]{1,0:T(8,128)(2,1)S(1)} %collective-permute-done.7, bf16[128,1024]{1,0:T(8,128)(2,1)} %collective-permute-done.6, bf16[128,1024]{1,0:T(8,128)(2,1)} %collective-permute-done.5, f32[1024]{0:T(1024)S(1)} %convert_element_type.96, bf16[4,128,1024]{2,1,0:T(8,128)(2,1)S(1)} %fusion.5, ...), kind=kLoop, calls=%fused_computation.60 | loop fusion | flops 1179648 | bytes 1314820 | tf_op jit(solution)/shard_map/convert_element_type | solution.py:161
  58.9 3.0 %fusion.66 = f32[128,2048]{1,0:T(8,128)S(1)} fusion(bf16[128,1024]{1,0:T(8,128)(2,1)} %fusion.45, bf16[1024,2048]{1,0:T(8,128)(2,1)} %param.11), kind=kOutput, calls=%fused_computation.133 | convolution fusion | flops 536870912 | bytes 5505024 | tf_op jit(solution)/shard_map/dot_general | solution.py:164
  64.5 2.5 %collective-permute-start.11 = (bf16[128,256]{1,0:T(8,128)(2,1)}, bf16[128,256]{1,0:T(8,128)(2,1)}, u32[]{:S(2)}, u32[]{:S(2)}) collective-permute-start(bf16[128,256]{1,0:T(8,128)(2,1)} %get-tuple-element.53), channel_id=1, source_target_pairs={{0,6},{1,7},{2,4},{3,5},{4,2},{5,3},{6,0},{7,1},{8,14},{9,15},{10,... | collective-permute-start | bytes 196616 | tf_op jit(solution)/shard_map/ppermute | solution.py:23
  67.0 1.9 %collective-permute-start.9 = (bf16[128,256]{1,0:T(8,128)(2,1)}, bf16[128,256]{1,0:T(8,128)(2,1)}, u32[]{:S(2)}, u32[]{:S(2)}) collective-permute-start(bf16[128,256]{1,0:T(8,128)(2,1)} %get-tuple-element.52), channel_id=1, source_target_pairs={{0,2},{1,3},{2,0},{3,1},{4,6},{5,7},{6,4},{7,5},{8,10},{9,11},{10,... | collective-permute-start | bytes 196616 | tf_op jit(solution)/shard_map/ppermute | solution.py:23
  71.6 2.0 %collective-permute-done.10 = bf16[128,256]{1,0:T(8,128)(2,1)} collective-permute-done((bf16[128,256]{1,0:T(8,128)(2,1)}, bf16[128,256]{1,0:T(8,128)(2,1)}, u32[]{:S(2)}, u32[]{:S(2)}) %collective-permute-start.10) | collective-permute-done | bytes 65568 | tf_op jit(solution)/shard_map/ppermute | solution.py:23
  75.5 2.8 %fusion.65 = (f32[8,256]{1,0:T(8,128)S(1)}, f32[8,256,128]{1,2,0:T(8,128)}) fusion(bf16[256,8,128]{0,2,1:T(8,128)(2,1)} %bitcast.173, pred[256,128]{0,1:T(8,128)(4,1)} %broadcast_compare_fusion, bf16[128,256]{1,0:T(8,128)(2,1)} %copy-done.8), kind=kOutput, calls=%fused_computation.132 | convolution fusion | flops 68157568 | bytes 1646592 | tf_op jit(solution)/shard_map/sub | solution.py:194
  78.3 2.3 %fusion.16 = bf16[128,128]{0,1:T(8,128)(2,1)} fusion(bf16[256,8,128]{0,2,1:T(8,128)(2,1)S(1)} %bitcast.165, f32[8,256]{1,0:T(8,128)S(1)} %get-tuple-element.55, bf16[256,8,128]{0,2,1:T(8,128)(2,1)} %bitcast.174, pred[256,128]{0,1:T(8,128)(4,1)} %broadcast_compare_fusion, bf16[128,256]{1,0:T(8,128)(2,1)} %copy-done.8), kind=kOutput, calls=%fused_computation.25 | convolution fusion | flops 135547008 | bytes 1155072 | tf_op jit(solution)/shard_map/hti,thd->id/dot_general | solution.py:203
  80.6 2.8 %fusion.15 = bf16[128,128]{0,1:T(8,128)(2,1)} fusion(bf16[256,8,128]{0,2,1:T(8,128)(2,1)} %bitcast.175, f32[8,256,128]{1,2,0:T(8,128)S(1)} %convolution_bitcast_fusion, f32[8,256,128]{1,2,0:T(8,128)} %get-tuple-element.56, f32[8,256]{1,0:T(8,128)S(1)} %get-tuple-element.55), kind=kOutput, calls=%fused_computation.24 | convolution fusion | flops 68962432 | bytes 2662400 | tf_op jit(solution)/shard_map/hti,thd->id/dot_general | solution.py:202
  84.2 2.5 %collective-permute-start.14 = (bf16[128,256]{0,1:T(8,128)(2,1)S(1)}, bf16[128,256]{0,1:T(8,128)(2,1)S(1)}, u32[]{:S(2)}, u32[]{:S(2)}) collective-permute-start(bf16[128,256]{0,1:T(8,128)(2,1)S(1)} %pad_maximum_fusion.5), channel_id=1, source_target_pairs={{0,6},{1,7},{2,4},{3,5},{4,2},{5,3},{6,0},{7,1},{8,14},{9,15},{10,... | collective-permute-start | bytes 196616 | tf_op jit(solution)/shard_map/ppermute | solution.py:23
  86.7 1.9 %collective-permute-start.12 = (bf16[128,256]{0,1:T(8,128)(2,1)S(1)}, bf16[128,256]{0,1:T(8,128)(2,1)S(1)}, u32[]{:S(2)}, u32[]{:S(2)}) collective-permute-start(bf16[128,256]{0,1:T(8,128)(2,1)S(1)} %pad_maximum_fusion.5), channel_id=1, source_target_pairs={{0,2},{1,3},{2,0},{3,1},{4,6},{5,7},{6,4},{7,5},{8,10},{9,11},{10,... | collective-permute-start | bytes 196616 | tf_op jit(solution)/shard_map/ppermute | solution.py:23
  88.6 2.3 %collective-permute-start.21 = (bf16[128,1024]{1,0:T(8,128)(2,1)}, bf16[128,1024]{1,0:T(8,128)(2,1)}, u32[]{:S(2)}, u32[]{:S(2)}) collective-permute-start(bf16[128,1024]{1,0:T(8,128)(2,1)} %fusion.45), channel_id=1, source_target_pairs={{0,24},{8,16},{16,8},{24,0},{1,25},{9,17},{17,9},{25,1},{2,26},{10... | collective-permute-start | bytes 786440 | tf_op jit(solution)/shard_map/ppermute | solution.py:23
  93.8 2.3 %convolution_convert_fusion.1 = bf16[128,8,256]{2,0,1:T(8,128)(2,1)} fusion(bf16[128,256]{1,0:T(8,128)(2,1)} %copy-done.8, f32[8,256]{1,0:T(8,128)S(1)} %get-tuple-element.55, bf16[256,8,128]{0,2,1:T(8,128)(2,1)S(1)} %bitcast.176, pred[256,128]{0,1:T(8,128)(4,1)} %broadcast_compare_fusion), kind=kOutput, calls=%fused_computation.19 | convolution fusion | flops 135792768 | bytes 1155072 | tf_op jit(solution)/shard_map/hti,id->thd/dot_general | solution.py:197
  97.7 2.4 %collective-permute-start.24 = (bf16[128,512]{1,0:T(8,128)(2,1)S(1)}, bf16[128,512]{1,0:T(8,128)(2,1)S(1)}, u32[]{:S(2)}, u32[]{:S(2)}) collective-permute-start(bf16[128,512]{1,0:T(8,128)(2,1)S(1)} %get-tuple-element.47), channel_id=1, source_target_pairs={{0,24},{8,16},{16,8},{24,0},{1,25},{9,17},{17,9},{25,1},{2,26},{10... | collective-permute-start | bytes 393224 | tf_op jit(solution)/shard_map/ppermute | solution.py:23
  100.1 3.7 %convolution_convert_fusion.2 = bf16[128,1024]{1,0:T(8,128)(2,1)S(1)} fusion(bf16[1024,2048]{1,0:T(8,128)(2,1)} %param.11, bf16[16,8,16,128]{3,2,1,0:T(8,128)(2,1)S(1)} %bitcast.163), kind=kOutput, calls=%fused_computation.21 | convolution fusion | flops 537001984 | bytes 4980736 | tf_op jit(solution)/shard_map/dot_general | solution.py:212
  104.4 1.5 %collective-permute-start.17 = (bf16[128,1024]{1,0:T(8,128)(2,1)S(1)}, bf16[128,1024]{1,0:T(8,128)(2,1)}, u32[]{:S(2)}, u32[]{:S(2)}) collective-permute-start(bf16[128,1024]{1,0:T(8,128)(2,1)S(1)} %convolution_convert_fusion.2), channel_id=1, source_target_pairs={{0,16},{8,24},{16,0},{24,8},{1,17},{9,25},{17,1},{25,9},{2,18},{10... | collective-permute-start | bytes 786440 | tf_op jit(solution)/shard_map/ppermute | solution.py:23
  105.9 1.4 %collective-permute-start.16 = (bf16[128,1024]{1,0:T(8,128)(2,1)S(1)}, bf16[128,1024]{1,0:T(8,128)(2,1)}, u32[]{:S(2)}, u32[]{:S(2)}) collective-permute-start(bf16[128,1024]{1,0:T(8,128)(2,1)S(1)} %convolution_convert_fusion.2), channel_id=1, source_target_pairs={{0,8},{8,0},{16,24},{24,16},{1,9},{9,1},{17,25},{25,17},{2,10},{10... | collective-permute-start | bytes 786440 | tf_op jit(solution)/shard_map/ppermute | solution.py:23
  109.1 2.7 %convolution_convert_fusion = bf16[128,8,256]{2,0,1:T(8,128)(2,1)S(1)} fusion(f32[8,256,128]{1,2,0:T(8,128)} %copy-done, bf16[128,256]{1,0:T(8,128)(2,1)} %copy-done.8, f32[8,256,128]{1,2,0:T(8,128)} %get-tuple-element.56, f32[8,256]{1,0:T(8,128)S(1)} %get-tuple-element.55), kind=kOutput, calls=%fused_computation.18 | convolution fusion | flops 69208192 | bytes 4767744 | tf_op jit(solution)/shard_map/hti,id->thd/dot_general | solution.py:201
  113.8 7.0 %collective-permute-done.23 = bf16[128,512]{1,0:T(8,128)(2,1)} collective-permute-done((bf16[128,512]{1,0:T(8,128)(2,1)}, bf16[128,512]{1,0:T(8,128)(2,1)}, u32[]{:S(2)}, u32[]{:S(2)}) %collective-permute-start.23) | collective-permute-done | bytes 131104 | tf_op jit(solution)/shard_map/ppermute | solution.py:23
  121.7 3.1 %bitcast_convert_fusion.1 = bf16[1024,512]{1,0:T(8,128)(2,1)} fusion(bf16[1,128,1024]{2,1,0:T(8,128)(2,1)} %bitcast.55, bf16[1,128,1024]{2,1,0:T(8,128)(2,1)} %bitcast.54, bf16[1,128,1024]{2,1,0:T(8,128)(2,1)} %bitcast.53, bf16[1,128,1024]{2,1,0:T(8,128)(2,1)} %bitcast.52, bf16[1,128,512]{2,1,0:T(8,128)(2,1)} %bitcast.195, ...), kind=kOutput, calls=%fused_computation.5 | convolution fusion | flops 539754496 | bytes 2621440 | tf_op jit(solution)/shard_map/jrd,jrc->dc/dot_general | solution.py:221
  124.8 1.9 %convert_reduce_fusion = (f32[1024]{0:T(1024)}, bf16[4,128,1024]{2,1,0:T(8,128)(2,1)S(1)}) fusion(bf16[1,128,1024]{2,1,0:T(8,128)(2,1)S(1)} %bitcast.184, bf16[1,128,1024]{2,1,0:T(8,128)(2,1)} %bitcast.49, bf16[1,128,1024]{2,1,0:T(8,128)(2,1)} %bitcast.48, bf16[1,128,1024]{2,1,0:T(8,128)(2,1)S(1)} %bitcast.170), kind=kLoop, calls=%fused_computation.6 | loop fusion | flops 2620416 | bytes 2101248 | tf_op jit(solution)/shard_map/reduce_sum | solution.py:229
  126.7 4.2 %bitcast_convert_fusion = bf16[1920,1024]{1,0:T(8,128)(2,1)} fusion(bf16[4,128,1920]{2,1,0:T(8,128)(2,1)S(1)} %bitcast.169, bf16[1,128,1024]{2,1,0:T(8,128)(2,1)S(1)} %get-tuple-element.20, bf16[1,128,1024]{2,1,0:T(8,128)(2,1)S(1)} %get-tuple-element.21, bf16[1,128,1024]{2,1,0:T(8,128)(2,1)S(1)} %get-tuple-element.22, ...), kind=kOutput, calls=%fused_computation.2 | convolution fusion | flops 2016804864 | bytes 6946816 | tf_op jit(solution)/shard_map/krf,krd->fd/dot_general | solution.py:226
  (91 shorter events, 24.5 us)
Async XLA Ops:
  0.6 0.7 collective-permute-start.1
  2.3 16.6 %collective-permute-start.2 = (bf16[64,1920]{1,0:T(8,128)(2,1)S(1)}, bf16[64,1920]{1,0:T(8,128)(2,1)S(1)}, u32[]{:S(2)}, u32[]{:S(2)}) collective-permute-start(bf16[64,1920]{1,0:T(8,128)(2,1)S(1)} %broadcast_select_fusion), channel_id=1, source_target_pairs={{0,4},{1,5},{2,0},{3,1},{4,6},{5,7},{6,2},{7,3},{8,12},{9,13},{10,... | collective-permute-start | bytes 737288 | tf_op jit(solution)/shard_map/ppermute | solution.py:28
  18.9 10.4 %collective-permute-start.3 = (bf16[64,1920]{1,0:T(8,128)(2,1)S(1)}, bf16[64,1920]{1,0:T(8,128)(2,1)S(1)}, u32[]{:S(2)}, u32[]{:S(2)}) collective-permute-start(bf16[64,1920]{1,0:T(8,128)(2,1)S(1)} %collective-permute-done.2), channel_id=1, source_target_pairs={{2,0},{3,1},{4,6},{5,7},{10,8},{11,9},{12,14},{13,15},{18,16},{19,... | collective-permute-start | bytes 737288 | tf_op jit(solution)/shard_map/ppermute | solution.py:28
  20.2 11.8 %collective-permute-start = (bf16[64,1920]{1,0:T(8,128)(2,1)}, bf16[64,1920]{1,0:T(8,128)(2,1)S(1)}, u32[]{:S(2)}, u32[]{:S(2)}) collective-permute-start(bf16[64,1920]{1,0:T(8,128)(2,1)} %param.8), channel_id=1, source_target_pairs={{0,2},{1,3},{2,0},{3,1},{4,6},{5,7},{6,4},{7,5},{8,10},{9,11},{10,... | collective-permute-start | bytes 737288 | tf_op jit(solution)/shard_map/ppermute | solution.py:23
  33.1 2.6 %collective-permute-start.4 = (bf16[4,64,1920]{2,1,0:T(8,128)(2,1)S(1)}, bf16[4,64,1920]{2,1,0:T(8,128)(2,1)S(1)}, u32[]{:S(2)}, u32[]{:S(2)}) collective-permute-start(bf16[4,64,1920]{2,1,0:T(8,128)(2,1)S(1)} %get-tuple-element.43), channel_id=1, source_target_pairs={{0,1},{1,0},{2,3},{3,2},{4,5},{5,4},{6,7},{7,6},{8,9},{9,8},{10,11... | collective-permute-start | bytes 2949128 | tf_op jit(solution)/shard_map/ppermute | solution.py:23
  33.2 5.3 %copy-start.12 = (bf16[1920,1024]{1,0:T(8,128)(2,1)S(1)}, bf16[1920,1024]{1,0:T(8,128)(2,1)}, u32[]{:S(2)}) copy-start(bf16[1920,1024]{1,0:T(8,128)(2,1)} %param.9) | copy-start | bytes 11796484
  38.5 6.8 %copy-start.9 = (bf16[1024]{0:T(1024)(128)(2,1)S(1)}, bf16[1024]{0:T(1024)(128)(2,1)}, u32[]{:S(2)}) copy-start(bf16[1024]{0:T(1024)(128)(2,1)} %param.10) | copy-start | bytes 6148
  41.8 10.3 %collective-permute-start.7 = (bf16[128,1024]{1,0:T(8,128)(2,1)}, bf16[128,1024]{1,0:T(8,128)(2,1)S(1)}, u32[]{:S(2)}, u32[]{:S(2)}) collective-permute-start(bf16[128,1024]{1,0:T(8,128)(2,1)} %get-tuple-element.40), channel_id=1, source_target_pairs={{0,24},{8,16},{16,8},{24,0},{1,25},{9,17},{17,9},{25,1},{2,26},{10... | collective-permute-start | bytes 786440 | tf_op jit(solution)/shard_map/ppermute | solution.py:23
  44.2 12.8 %collective-permute-start.6 = (bf16[128,1024]{1,0:T(8,128)(2,1)}, bf16[128,1024]{1,0:T(8,128)(2,1)}, u32[]{:S(2)}, u32[]{:S(2)}) collective-permute-start(bf16[128,1024]{1,0:T(8,128)(2,1)} %get-tuple-element.41), channel_id=1, source_target_pairs={{0,16},{8,24},{16,0},{24,8},{1,17},{9,25},{17,1},{25,9},{2,18},{10... | collective-permute-start | bytes 786440 | tf_op jit(solution)/shard_map/ppermute | solution.py:23
  44.7 12.3 %collective-permute-start.5 = (bf16[128,1024]{1,0:T(8,128)(2,1)S(1)}, bf16[128,1024]{1,0:T(8,128)(2,1)}, u32[]{:S(2)}, u32[]{:S(2)}) collective-permute-start(bf16[128,1024]{1,0:T(8,128)(2,1)S(1)} %get-tuple-element.39), channel_id=1, source_target_pairs={{0,8},{8,0},{16,24},{24,16},{1,9},{9,1},{17,25},{25,17},{2,10},{10... | collective-permute-start | bytes 786440 | tf_op jit(solution)/shard_map/ppermute | solution.py:23
  62.1 6.8 %copy-start.10 = (s32[1,256]{1,0:T(1,128)S(1)}, s32[1,256]{1,0:T(1,128)}, u32[]{:S(2)}) copy-start(s32[1,256]{1,0:T(1,128)} %param.15) | copy-start | bytes 3076
  62.1 6.8 %copy-start.11 = (s32[1,128]{1,0:T(1,128)S(1)}, s32[1,128]{1,0:T(1,128)}, u32[]{:S(2)}) copy-start(s32[1,128]{1,0:T(1,128)} %param.14) | copy-start | bytes 1540
  62.2 7.5 %copy-start.2 = (bf16[256,1024]{1,0:T(8,128)(2,1)S(1)}, bf16[256,1024]{1,0:T(8,128)(2,1)}, u32[]{:S(2)}) copy-start(bf16[256,1024]{1,0:T(8,128)(2,1)} %param.12) | copy-start | bytes 1572868
  62.2 1.6 %collective-permute-start.8 = (bf16[4,128,256]{2,1,0:T(8,128)(2,1)S(1)}, bf16[4,128,256]{2,1,0:T(8,128)(2,1)S(1)}, u32[]{:S(2)}, u32[]{:S(2)}) collective-permute-start(bf16[4,128,256]{2,1,0:T(8,128)(2,1)S(1)} %pad_maximum_fusion.3), channel_id=1, source_target_pairs={{0,1},{1,0},{2,3},{3,2},{4,5},{5,4},{6,7},{7,6},{8,9},{9,8},{10,11... | collective-permute-start | bytes 786440 | tf_op jit(solution)/shard_map/ppermute | solution.py:23
  62.3 8.3 %copy-start.3 = (bf16[256,1024]{1,0:T(8,128)(2,1)S(1)}, bf16[256,1024]{1,0:T(8,128)(2,1)}, u32[]{:S(2)}) copy-start(bf16[256,1024]{1,0:T(8,128)(2,1)} %param.13) | copy-start | bytes 1572868
  64.5 7.0 %collective-permute-start.11 = (bf16[128,256]{1,0:T(8,128)(2,1)}, bf16[128,256]{1,0:T(8,128)(2,1)}, u32[]{:S(2)}, u32[]{:S(2)}) collective-permute-start(bf16[128,256]{1,0:T(8,128)(2,1)} %get-tuple-element.53), channel_id=1, source_target_pairs={{0,6},{1,7},{2,4},{3,5},{4,2},{5,3},{6,0},{7,1},{8,14},{9,15},{10,... | collective-permute-start | bytes 196616 | tf_op jit(solution)/shard_map/ppermute | solution.py:23
  67.0 6.6 %collective-permute-start.10 = (bf16[128,256]{1,0:T(8,128)(2,1)}, bf16[128,256]{1,0:T(8,128)(2,1)}, u32[]{:S(2)}, u32[]{:S(2)}) collective-permute-start(bf16[128,256]{1,0:T(8,128)(2,1)} %get-tuple-element.54), channel_id=1, source_target_pairs={{0,4},{1,5},{2,6},{3,7},{4,0},{5,1},{6,2},{7,3},{8,12},{9,13},{10,... | collective-permute-start | bytes 196616 | tf_op jit(solution)/shard_map/ppermute | solution.py:23
  67.0 6.6 %collective-permute-start.9 = (bf16[128,256]{1,0:T(8,128)(2,1)}, bf16[128,256]{1,0:T(8,128)(2,1)}, u32[]{:S(2)}, u32[]{:S(2)}) collective-permute-start(bf16[128,256]{1,0:T(8,128)(2,1)} %get-tuple-element.52), channel_id=1, source_target_pairs={{0,2},{1,3},{2,0},{3,1},{4,6},{5,7},{6,4},{7,5},{8,10},{9,11},{10,... | collective-permute-start | bytes 196616 | tf_op jit(solution)/shard_map/ppermute | solution.py:23
  80.6 13.2 %copy-start.4 = (bf16[256,1024]{0,1:T(8,128)(2,1)S(1)}, bf16[256,1024]{0,1:T(8,128)(2,1)}, u32[]{:S(2)}) copy-start(bf16[256,1024]{0,1:T(8,128)(2,1)} %copy.53) | copy-start | bytes 1572868
  84.2 7.3 %collective-permute-start.14 = (bf16[128,256]{0,1:T(8,128)(2,1)S(1)}, bf16[128,256]{0,1:T(8,128)(2,1)S(1)}, u32[]{:S(2)}, u32[]{:S(2)}) collective-permute-start(bf16[128,256]{0,1:T(8,128)(2,1)S(1)} %pad_maximum_fusion.5), channel_id=1, source_target_pairs={{0,6},{1,7},{2,4},{3,5},{4,2},{5,3},{6,0},{7,1},{8,14},{9,15},{10,... | collective-permute-start | bytes 196616 | tf_op jit(solution)/shard_map/ppermute | solution.py:23
  86.7 6.1 %collective-permute-start.13 = (bf16[128,256]{0,1:T(8,128)(2,1)S(1)}, bf16[128,256]{0,1:T(8,128)(2,1)S(1)}, u32[]{:S(2)}, u32[]{:S(2)}) collective-permute-start(bf16[128,256]{0,1:T(8,128)(2,1)S(1)} %pad_maximum_fusion.5), channel_id=1, source_target_pairs={{0,4},{1,5},{2,6},{3,7},{4,0},{5,1},{6,2},{7,3},{8,12},{9,13},{10,... | collective-permute-start | bytes 196616 | tf_op jit(solution)/shard_map/ppermute | solution.py:23
  86.7 6.1 %collective-permute-start.12 = (bf16[128,256]{0,1:T(8,128)(2,1)S(1)}, bf16[128,256]{0,1:T(8,128)(2,1)S(1)}, u32[]{:S(2)}, u32[]{:S(2)}) collective-permute-start(bf16[128,256]{0,1:T(8,128)(2,1)S(1)} %pad_maximum_fusion.5), channel_id=1, source_target_pairs={{0,2},{1,3},{2,0},{3,1},{4,6},{5,7},{6,4},{7,5},{8,10},{9,11},{10,... | collective-permute-start | bytes 196616 | tf_op jit(solution)/shard_map/ppermute | solution.py:23
  88.6 15.8 %collective-permute-start.21 = (bf16[128,1024]{1,0:T(8,128)(2,1)}, bf16[128,1024]{1,0:T(8,128)(2,1)}, u32[]{:S(2)}, u32[]{:S(2)}) collective-permute-start(bf16[128,1024]{1,0:T(8,128)(2,1)} %fusion.45), channel_id=1, source_target_pairs={{0,24},{8,16},{16,8},{24,0},{1,25},{9,17},{17,9},{25,1},{2,26},{10... | collective-permute-start | bytes 786440 | tf_op jit(solution)/shard_map/ppermute | solution.py:23
  91.0 14.9 %collective-permute-start.20 = (bf16[128,1024]{1,0:T(8,128)(2,1)}, bf16[128,1024]{1,0:T(8,128)(2,1)}, u32[]{:S(2)}, u32[]{:S(2)}) collective-permute-start(bf16[128,1024]{1,0:T(8,128)(2,1)} %fusion.45), channel_id=1, source_target_pairs={{0,16},{8,24},{16,0},{24,8},{1,17},{9,25},{17,1},{25,9},{2,18},{10... | collective-permute-start | bytes 786440 | tf_op jit(solution)/shard_map/ppermute | solution.py:23
  91.5 15.8 %collective-permute-start.19 = (bf16[128,1024]{1,0:T(8,128)(2,1)}, bf16[128,1024]{1,0:T(8,128)(2,1)}, u32[]{:S(2)}, u32[]{:S(2)}) collective-permute-start(bf16[128,1024]{1,0:T(8,128)(2,1)} %fusion.45), channel_id=1, source_target_pairs={{0,8},{8,0},{16,24},{24,16},{1,9},{9,1},{17,25},{25,17},{2,10},{10... | collective-permute-start | bytes 786440 | tf_op jit(solution)/shard_map/ppermute | solution.py:23
  93.7 2.4 %collective-permute-start.15 = (bf16[4,128,256]{1,2,0:T(8,128)(2,1)S(1)}, bf16[4,128,256]{1,2,0:T(8,128)(2,1)S(1)}, u32[]{:S(2)}, u32[]{:S(2)}) collective-permute-start(bf16[4,128,256]{1,2,0:T(8,128)(2,1)S(1)} %pad_maximum_fusion.4), channel_id=1, source_target_pairs={{0,1},{1,0},{2,3},{3,2},{4,5},{5,4},{6,7},{7,6},{8,9},{9,8},{10,11... | collective-permute-start | bytes 786440 | tf_op jit(solution)/shard_map/ppermute | solution.py:23
  97.7 10.2 %collective-permute-start.24 = (bf16[128,512]{1,0:T(8,128)(2,1)S(1)}, bf16[128,512]{1,0:T(8,128)(2,1)S(1)}, u32[]{:S(2)}, u32[]{:S(2)}) collective-permute-start(bf16[128,512]{1,0:T(8,128)(2,1)S(1)} %get-tuple-element.47), channel_id=1, source_target_pairs={{0,24},{8,16},{16,8},{24,0},{1,25},{9,17},{17,9},{25,1},{2,26},{10... | collective-permute-start | bytes 393224 | tf_op jit(solution)/shard_map/ppermute | solution.py:23
  103.8 21.0 %collective-permute-start.18 = (bf16[128,1024]{1,0:T(8,128)(2,1)S(1)}, bf16[128,1024]{1,0:T(8,128)(2,1)S(1)}, u32[]{:S(2)}, u32[]{:S(2)}) collective-permute-start(bf16[128,1024]{1,0:T(8,128)(2,1)S(1)} %convolution_convert_fusion.2), channel_id=1, source_target_pairs={{0,24},{8,16},{16,8},{24,0},{1,25},{9,17},{17,9},{25,1},{2,26},{10... | collective-permute-start | bytes 786440 | tf_op jit(solution)/shard_map/ppermute | solution.py:23
  104.4 20.4 %collective-permute-start.17 = (bf16[128,1024]{1,0:T(8,128)(2,1)S(1)}, bf16[128,1024]{1,0:T(8,128)(2,1)}, u32[]{:S(2)}, u32[]{:S(2)}) collective-permute-start(bf16[128,1024]{1,0:T(8,128)(2,1)S(1)} %convolution_convert_fusion.2), channel_id=1, source_target_pairs={{0,16},{8,24},{16,0},{24,8},{1,17},{9,25},{17,1},{25,9},{2,18},{10... | collective-permute-start | bytes 786440 | tf_op jit(solution)/shard_map/ppermute | solution.py:23
  105.9 18.9 %collective-permute-start.16 = (bf16[128,1024]{1,0:T(8,128)(2,1)S(1)}, bf16[128,1024]{1,0:T(8,128)(2,1)}, u32[]{:S(2)}, u32[]{:S(2)}) collective-permute-start(bf16[128,1024]{1,0:T(8,128)(2,1)S(1)} %convolution_convert_fusion.2), channel_id=1, source_target_pairs={{0,8},{8,0},{16,24},{24,16},{1,9},{9,1},{17,25},{25,17},{2,10},{10... | collective-permute-start | bytes 786440 | tf_op jit(solution)/shard_map/ppermute | solution.py:23
  107.3 13.5 %collective-permute-start.23 = (bf16[128,512]{1,0:T(8,128)(2,1)}, bf16[128,512]{1,0:T(8,128)(2,1)}, u32[]{:S(2)}, u32[]{:S(2)}) collective-permute-start(bf16[128,512]{1,0:T(8,128)(2,1)} %get-tuple-element.45), channel_id=1, source_target_pairs={{0,16},{8,24},{16,0},{24,8},{1,17},{9,25},{17,1},{25,9},{2,18},{10... | collective-permute-start | bytes 393224 | tf_op jit(solution)/shard_map/ppermute | solution.py:23
  108.5 13.2 %collective-permute-start.22 = (bf16[128,512]{1,0:T(8,128)(2,1)}, bf16[128,512]{1,0:T(8,128)(2,1)}, u32[]{:S(2)}, u32[]{:S(2)}) collective-permute-start(bf16[128,512]{1,0:T(8,128)(2,1)} %get-tuple-element.46), channel_id=1, source_target_pairs={{0,8},{8,0},{16,24},{24,16},{1,9},{9,1},{17,25},{25,17},{2,10},{10... | collective-permute-start | bytes 393224 | tf_op jit(solution)/shard_map/ppermute | solution.py:23
  (7 other events, 15.4 us)

commit v2 on v0

--- a/solution.py
+++ b/solution.py
@@ -1,18 +1,49 @@
+import functools
+
 import jax
 import jax.numpy as jnp
 from jax import lax
+from jax.experimental import pallas as pl
+from jax.experimental.pallas import tpu as pltpu
 from jax.sharding import PartitionSpec as P
 
-H = 64
-KVH = 8
 HD = 128
+
+T = "tensor"
+XY = ("group", "dp")
+F32 = jnp.float32
+BF16 = jnp.bfloat16
+NT = (((1,), (1,)), ((), ()))
+TN = (((0,), (0,)), ((), ()))
+VMEM_LIMIT = 8 * 1024 * 1024
+
+
+def size_of(axes):
+    names = axes if isinstance(axes, tuple) else (axes,)
+    total = 1
+    for name in names:
+        total *= lax.axis_size(name)
+    return total
+
+
+def swap(x, axes, bits):
+    return lax.ppermute(x, axes, [(i, i ^ bits) for i in range(size_of(axes))])
+
+
+def after(x, *others):
+    return lax.optimization_barrier((x,) + others)[0]
+
+
+def heads_per_key(queries, kv_weight):
+    heads = queries.shape[1] // HD * lax.axis_size(T)
+    return heads // (kv_weight.shape[1] // 2 // HD)
 
 
 def from_partner(shard, axis, distance):
     return lax.ppermute(shard, axis, [(i, i ^ 1 << distance) for i in range(lax.axis_size(axis))])
 
 
-def shards(
+def general(
     image_feats, proj_weight, proj_bias, kv_weight, queries, out_grad, image_sample, text_sample
 ):
     gathered = lax.all_gather(image_feats, "tensor", axis=0, tiled=True)
@@ -27,7 +58,7 @@
     kv_term = jnp.dot(projected, kv_weight, preferred_element_type=jnp.float32)
     kv_all = lax.psum(kv_term, "tensor").astype(jnp.bfloat16)
     local_heads = queries.shape[1] // HD
-    shared = H // KVH
+    shared = heads_per_key(queries, kv_weight)
     half = kv_all.shape[1] // 2
     key_head = lax.axis_index("tensor") * local_heads // shared
     key_start = key_head * HD
@@ -90,6 +121,503 @@
     return (attended, d_queries, weight_grad.astype(jnp.bfloat16), bias_grad, d_kv_weight)
 
 
+def params():
+    return pltpu.CompilerParams(vmem_limit_bytes=VMEM_LIMIT)
+
+
+def cost(flops, nbytes):
+    return pl.CostEstimate(flops=flops, bytes_accessed=nbytes, transcendentals=0)
+
+
+def whole(shape):
+    return pl.BlockSpec(shape, lambda *_: (0,) * len(shape))
+
+
+def place_of():
+    me = lax.axis_index(T)
+    part = lax.axis_index("group") * lax.axis_size("dp") + lax.axis_index("dp")
+    return (me // 2) ^ part, me % 2, me, part
+
+
+def pack_kernel(*refs):
+    out = refs[-1]
+    width = out.shape[2]
+    for i, ref in enumerate(refs[:-1]):
+        out[i] = ref[:, ref.shape[1] - width :]
+
+
+def pack(*arrays):
+    rows, width = arrays[0].shape[0], min(x.shape[1] for x in arrays)
+    return pl.pallas_call(
+        pack_kernel,
+        in_specs=in_vmem(len(arrays)),
+        out_shape=jax.ShapeDtypeStruct((len(arrays), rows, width), BF16),
+        compiler_params=params(),
+        cost_estimate=cost(0, 8 * len(arrays) * rows * width),
+        name="pack",
+    )(*arrays)
+
+
+def add_kernel(mine, theirs, first, *rest):
+    first[...] = mine[0] + theirs[0].astype(F32)
+    for k, ref in enumerate(rest):
+        ref[...] = (mine[k + 1] + theirs[k + 1].astype(F32)).astype(BF16)
+
+
+def add(mine, theirs):
+    shape = mine.shape[1:]
+    return pl.pallas_call(
+        add_kernel,
+        in_specs=in_vmem(2),
+        out_shape=[jax.ShapeDtypeStruct(shape, F32)]
+        + [jax.ShapeDtypeStruct(shape, BF16)] * (mine.shape[0] - 1),
+        compiler_params=params(),
+        cost_estimate=cost(0, 16 * mine.size),
+        name="add",
+    )(mine, theirs)
+
+
+def tiles_of(width, tile):
+    return width // tile if width % tile == 0 else 1
+
+
+def project_kernel(groups, *refs):
+    place = place_of()
+    mine, others = refs[:groups], refs[groups : 2 * groups]
+    weight, (partial, feats) = refs[2 * groups], (refs[2 * groups + 1 : -1], refs[-1])
+    own = [ref.at[i] for ref in mine for i in range(ref.shape[0])]
+    others = [ref.at[i] for ref in others for i in range(ref.shape[0])]
+    count = len(own)
+    rows = own[0].shape[0]
+    for k in range(count):
+        j = k ^ place[0]
+
+        @pl.when(place[1] == 0)
+        def _():
+            feats[j, :rows, :] = own[k][...]
+            feats[j, rows:, :] = others[k][...]
+
+        @pl.when(place[1] != 0)
+        def _():
+            feats[j, :rows, :] = others[k][...]
+            feats[j, rows:, :] = own[k][...]
+
+    tiles = tiles_of(weight.shape[1], 256)
+    tile = weight.shape[1] // tiles
+
+    def step(n, _):
+        at = pl.ds(pl.multiple_of(n * tile, tile), tile)
+        lhs = feats[...].reshape(count * 2 * rows, feats.shape[2])
+        out = jnp.dot(lhs, weight[:, at], preferred_element_type=F32).astype(BF16)
+        for j in range(count):
+            partial[j][:, at] = out[j * 2 * rows : (j + 1) * 2 * rows]
+        return 0
+
+    lax.fori_loop(0, tiles, step, 0)
+
+
+def in_vmem(count):
+    return [pl.BlockSpec()] * count
+
+
+def project(own, others, weight):
+    count = sum(x.shape[0] for x in own)
+    rows, depth = own[0].shape[1:]
+    width = weight.shape[1]
+    return pl.pallas_call(
+        functools.partial(project_kernel, len(own)),
+        in_specs=in_vmem(2 * len(own) + 1),
+        out_shape=[jax.ShapeDtypeStruct((2 * rows, width), BF16)] * count
+        + [jax.ShapeDtypeStruct((count, 2 * rows, depth), BF16)],
+        compiler_params=params(),
+        cost_estimate=cost(8 * count * rows * depth * width, 2 * depth * width),
+        name="project",
+    )(*own, *others, weight)
+
+
+def heads_into(x, place, odd, weight, out):
+    half = weight.shape[1] // 2
+    for i in range(out.shape[0]):
+        start = pl.multiple_of((place[2] ^ (2 * i + odd)) * HD, HD)
+        for at, cut in ((start, slice(0, HD)), (half + start, slice(HD, 2 * HD))):
+            value = jnp.dot(x, weight[:, pl.ds(at, HD)], preferred_element_type=F32)
+            out[i, :, cut] = value.astype(out.dtype)
+
+
+def combine_kernel(parts, first, *refs):
+    place = place_of()
+    arrived, (bias, weight, projected, out) = refs[: parts - 1], refs[parts - 1 :]
+    total = first[...].astype(F32)
+    for ref in arrived:
+        total = total + ref[...].astype(F32)
+    x = (total + bias[...].astype(F32)).astype(BF16)
+    projected[...] = x
+    heads_into(x, place, 1, weight, out)
+
+
+def combine(first, arrived, bias, kv_weight, tensors):
+    parts = 1 + len(arrived)
+    rows, depth = first.shape
+    return pl.pallas_call(
+        functools.partial(combine_kernel, parts),
+        in_specs=in_vmem(parts + 2),
+        out_shape=[
+            jax.ShapeDtypeStruct((rows, depth), BF16),
+            jax.ShapeDtypeStruct((tensors // 2, rows, 2 * HD), BF16),
+        ],
+        compiler_params=params(),
+        cost_estimate=cost(24 * rows * depth * tensors * HD, depth * tensors * HD * 2),
+        name="combine",
+    )(first, *arrived, bias, kv_weight)
+
+
+def own_heads_kernel(projected, weight, out):
+    heads_into(projected[...], place_of(), 0, weight, out)
+
+
+def own_heads(projected, kv_weight, tensors):
+    rows, depth = projected.shape
+    return pl.pallas_call(
+        own_heads_kernel,
+        in_specs=in_vmem(2),
+        out_shape=jax.ShapeDtypeStruct((tensors // 2, rows, 2 * HD), F32),
+        compiler_params=params(),
+        cost_estimate=cost(24 * rows * depth * tensors * HD, depth * tensors * HD * 2),
+        name="own_heads",
+    )(projected, kv_weight)
+
+
+def attend_kernel(count, *refs):
+    first, arrived = refs[0], refs[1:count]
+    queries, out_grad, image_ids, text_ids, kv_out, dkv, probs_out, dscores_out = refs[count:]
+    total = first[...]
+    for ref in arrived:
+        total = total + ref[...].astype(F32)
+    kv = total.astype(BF16)
+    kv_out[...] = kv
+    keys, values = kv[:, :HD], kv[:, HD:]
+    scale = HD ** (-0.5)
+    allowed = image_ids[...] == text_ids[...]
+    d_keys = jnp.zeros((kv.shape[0], HD), F32)
+    d_values = jnp.zeros((kv.shape[0], HD), F32)
+    for head in range(queries.shape[1] // HD):
+        at = slice(head * HD, (head + 1) * HD)
+        q, g = queries[:, at], out_grad[:, at]
+        scores = lax.dot_general(keys, q, NT, preferred_element_type=F32) * scale
+        scores = jnp.where(allowed, scores, F32(-1e30))
+        expo = jnp.exp(scores - jnp.max(scores, axis=0, keepdims=True))
+        probs = expo * (1.0 / jnp.sum(expo, axis=0, keepdims=True))
+        probs_b = probs.astype(BF16)
+        dprobs = lax.dot_general(values, g, NT, preferred_element_type=F32)
+        delta = jnp.sum(probs * dprobs, axis=0, keepdims=True)
+        dscores = (probs * (dprobs - delta) * scale).astype(BF16)
+        d_keys = d_keys + jnp.dot(dscores, q, preferred_element_type=F32)
+        d_values = d_values + jnp.dot(probs_b, g, preferred_element_type=F32)
+        probs_out[head] = probs_b
+        dscores_out[head] = dscores
+    dkv[:, :HD] = d_keys.astype(BF16)
+    dkv[:, HD:] = d_values.astype(BF16)
+
+
+def attend(first, arrived, queries, out_grad, image_ids, text_ids):
+    inputs = [first, *arrived, queries, out_grad, image_ids, text_ids]
+    shape = first.shape
+    heads = queries.shape[1] // HD
+    weights = jax.ShapeDtypeStruct((heads, shape[0], queries.shape[0]), BF16)
+    return pl.pallas_call(
+        functools.partial(attend_kernel, 1 + len(arrived)),
+        out_shape=[
+            jax.ShapeDtypeStruct(shape, BF16),
+            jax.ShapeDtypeStruct(shape, BF16),
+            weights,
+            weights,
+        ],
+        compiler_params=params(),
+        cost_estimate=cost(16 * 4 * queries.size * shape[0], 8 * queries.size),
+        name="attend",
+    )(*inputs)
+
+
+def finish_kernel(kv, probs, dscores, attended, d_queries):
+    keys, values = kv[:, :HD], kv[:, HD:]
+    for head in range(probs.shape[0]):
+        at = slice(head * HD, (head + 1) * HD)
+        attended[:, at] = lax.dot_general(
+            probs[head], values, TN, preferred_element_type=F32
+        ).astype(BF16)
+        d_queries[:, at] = lax.dot_general(
+            dscores[head], keys, TN, preferred_element_type=F32
+        ).astype(BF16)
+
+
+def finish(kv, probs, dscores):
+    heads, images, texts = probs.shape
+    out = jax.ShapeDtypeStruct((texts, heads * HD), BF16)
+    return pl.pallas_call(
+        finish_kernel,
+        out_shape=[out, out],
+        compiler_params=params(),
+        cost_estimate=cost(8 * 4 * heads * images * texts * HD, 8 * probs.size),
+        name="finish",
+    )(kv, probs, dscores)
+
+
+def turn_kernel(feats, out):
+    parts, rows, tile = feats.shape
+    out[...] = feats[...].reshape(parts * rows, tile).T
+
+
+def turn(feats):
+    parts, rows, depth = feats.shape
+    tile = depth // tiles_of(depth, 640)
+    total = parts * rows
+    return pl.pallas_call(
+        turn_kernel,
+        grid=(depth // tile,),
+        in_specs=[pl.BlockSpec((parts, rows, tile), lambda n: (0, 0, n))],
+        out_specs=pl.BlockSpec((tile, total), lambda n: (n, 0)),
+        out_shape=jax.ShapeDtypeStruct((depth, total), BF16),
+        compiler_params=params(),
+        cost_estimate=cost(0, 8 * depth * total),
+        name="turn",
+    )(feats)
+
+
+def back_columns(dkv, weight, first, targets):
+    columns = targets[0].shape[1]
+    count = tiles_of(columns, 256)
+    tile = columns // count
+    for n in range(count):
+        value = lax.dot_general(
+            dkv,
+            weight[first + n * tile : first + (n + 1) * tile, :],
+            NT,
+            preferred_element_type=F32,
+        ).astype(BF16)
+        for ref in targets:
+            ref[:, n * tile : (n + 1) * tile] = value
+
+
+def back_kernel(chips, *refs):
+    place = place_of()
+    own, (other, weight, out), refs = refs[:chips], refs[chips : chips + 3], refs[chips + 3 :]
+    sent, (cols, dkv_all) = refs[:-2], refs[-2:]
+    columns = out.shape[1]
+    half = dkv_all.shape[1] // 2
+    for k in range(chips):
+        for block, bits in ((own[k][...], 2 * k), (other[k], 2 * k + 1)):
+            start = pl.multiple_of((place[2] ^ bits) * HD, HD)
+            dkv_all[:, pl.ds(start, HD)] = block[:, :HD]
+            dkv_all[:, pl.ds(half + start, HD)] = block[:, HD:]
+    width = cols.shape[1] * 2
+    for j in range(len(sent) + 1):
+        for m in range(width // HD // 2):
+            start = (place[3] ^ j) * width + (2 * m + place[1]) * HD
+            block = dkv_all[:, pl.ds(pl.multiple_of(start, HD), HD)]
+            at = slice(m * HD, (m + 1) * HD)
+            if j == 0:
+                cols[:, at] = block
+            else:
+                sent[j - 1][:, columns + m * HD : columns + (m + 1) * HD] = block
+    back_columns(dkv_all[...], weight, 0, [out])
+    for ref in sent:
+        ref[:, :columns] = out[...]
+
+
+def back(own, other, kv_weight, parts, chunks):
+    rows = own[0].shape[0]
+    depth, width = kv_weight.shape
+    columns = depth // chunks
+    extra = width // parts // 2
+    full = jax.ShapeDtypeStruct((rows, columns + extra), BF16)
+    return pl.pallas_call(
+        functools.partial(back_kernel, len(own)),
+        in_specs=in_vmem(len(own) + 2),
+        out_shape=[jax.ShapeDtypeStruct((rows, columns), BF16)]
+        + [full] * (parts - 1)
+        + [
+            jax.ShapeDtypeStruct((rows, extra), BF16),
+            jax.ShapeDtypeStruct((rows, width), BF16),
+        ],
+        compiler_params=params(),
+        cost_estimate=cost(8 * rows * columns * width, 2 * columns * width),
+        name="back",
+    )(*own, other, kv_weight)
+
+
+def back_rest_kernel(chunk, dkv_all, weight, out):
+    back_columns(dkv_all[...], weight, chunk * out.shape[1], [out])
+
+
+def back_rest(dkv_all, kv_weight, chunk, chunks):
+    rows = dkv_all.shape[0]
+    depth, width = kv_weight.shape
+    columns = depth // chunks
+    return pl.pallas_call(
+        functools.partial(back_rest_kernel, chunk),
+        in_specs=in_vmem(2),
+        out_shape=jax.ShapeDtypeStruct((rows, columns), BF16),
+        compiler_params=params(),
+        cost_estimate=cost(8 * rows * columns * width, 2 * columns * width),
+        name="back_rest",
+    )(dkv_all, kv_weight)
+
+
+def kv_grad_kernel(count, parts, *refs):
+    place = place_of()
+    left, mine, (theirs, out, right) = refs[:count], refs[count : count + parts], refs[-3:]
+    rows = left[0].shape[0]
+    extra = mine[0].shape[1]
+    for j in range(parts):
+        at = slice(j * rows, (j + 1) * rows)
+        skip = mine[j].shape[1] - extra
+        for m in range(extra // HD):
+            start = pl.multiple_of((2 * m + place[1]) * HD, HD)
+            right[at, pl.ds(start, HD)] = mine[j][:, skip + m * HD : skip + (m + 1) * HD]
+            start = pl.multiple_of((2 * m + 1 - place[1]) * HD, HD)
+            right[at, pl.ds(start, HD)] = theirs[j, :, m * HD : (m + 1) * HD]
+    depth = out.shape[0]
+    count = tiles_of(depth, 256)
+    tile = depth // count
+    for n in range(count):
+        at = slice(n * tile, (n + 1) * tile)
+        lhs = jnp.concatenate([x[:, at] for x in left], axis=0)
+        out[at, :] = lax.dot_general(
+            lhs, right[...], TN, preferred_element_type=F32
+        ).astype(BF16)
+
+
+def kv_grad(left, own, sent, theirs):
+    parts = 1 + len(sent)
+    rows, depth = left[0].shape
+    extra = own.shape[1]
+    return pl.pallas_call(
+        functools.partial(kv_grad_kernel, len(left), parts),
+        in_specs=in_vmem(len(left) + parts + 1),
+        out_shape=jax.ShapeDtypeStruct((depth, 2 * extra), BF16),
+        scratch_shapes=[pltpu.VMEM((parts * rows, 2 * extra), BF16)],
+        compiler_params=params(),
+        cost_estimate=cost(4 * parts * rows * depth * extra, 4 * parts * rows * depth),
+        name="kv_grad",
+    )(*left, own, *sent, theirs)
+
+
+def weight_grad_kernel(parts, feats, *refs):
+    grads, (out, bias, right) = refs[:parts], refs[-3:]
+    columns = out.shape[1]
+    rows = grads[0].shape[0]
+
+    @pl.when(pl.program_id(0) == 0)
+    def _():
+        total = None
+        for j, g in enumerate(grads):
+            value = g[:, :columns]
+            right[j * rows : (j + 1) * rows, :] = value
+            term = jnp.sum(value.astype(F32), axis=0, keepdims=True)
+            total = term if total is None else total + term
+        bias[...] = total
+
+    tile = out.shape[0]
+    at = pl.ds(pl.multiple_of(pl.program_id(0) * tile, tile), tile)
+    out[...] = jnp.dot(feats[at, :], right[...], preferred_element_type=F32).astype(BF16)
+
+
+def weight_grad(feats, grads, held, chunk, chunks):
+    depth, total = feats.shape
+    shard = grads[0].shape
+    columns = shard[1]
+    tile = depth // 3 if depth % 384 == 0 else depth
+    inputs = [feats, *grads]
+    specs = in_vmem(len(inputs))
+    aliases = {}
+    if held is not None:
+        aliases = {len(inputs): 0, len(inputs) + 1: 1}
+        inputs += held
+        specs += [pl.BlockSpec(memory_space=pl.ANY)] * 2
+    return pl.pallas_call(
+        functools.partial(weight_grad_kernel, len(grads)),
+        grid=(depth // tile,),
+        in_specs=specs,
+        out_specs=[
+            pl.BlockSpec((tile, columns), lambda n: (n, chunk)),
+            pl.BlockSpec((1, columns), lambda n: (0, chunk)),
+        ],
+        out_shape=[
+            jax.ShapeDtypeStruct((depth, columns * chunks), BF16),
+            jax.ShapeDtypeStruct((1, columns * chunks), F32),
+        ],
+        scratch_shapes=[pltpu.VMEM((total, columns), BF16)],
+        input_output_aliases=aliases,
+        compiler_params=params(),
+        cost_estimate=cost(2 * total * depth * columns, 2 * depth * (total + columns)),
+        name="weight_grad",
+    )(*inputs)
+
+
+def shards(
+    image_feats, proj_weight, proj_bias, kv_weight, queries, out_grad, image_sample, text_sample
+):
+    tensors = lax.axis_size(T)
+    chips = tensors // 2
+    parts = size_of(XY)
+    if (
+        heads_per_key(queries, kv_weight) * HD != queries.shape[1]
+        or chips != parts
+        or parts != 4
+    ):
+        return general(
+            image_feats, proj_weight, proj_bias, kv_weight, queries, out_grad, image_sample, text_sample
+        )
+    own = [image_feats] + [swap(image_feats, T, 2 * k) for k in range(1, chips)]
+    image_ids = after(image_sample, own[1]).reshape(-1, 1)
+    stacks = [pack(*own[: chips // 2]), pack(*own[chips // 2 :])]
+    *partial, feats = project(stacks, [swap(x, T, 1) for x in stacks], proj_weight)
+    arrived = [swap(partial[j], XY, j) for j in range(1, parts)]
+
+    projected, theirs = combine(
+        partial[0], arrived, proj_bias.reshape(1, -1), kv_weight, tensors
+    )
+    theirs = swap(theirs, T, 1)
+    mine = own_heads(projected, kv_weight, tensors)
+    mine, *kv_sent = add(mine, theirs)
+    kv_parts = [swap(x, T, 2 * k) for k, x in enumerate(kv_sent, 1)]
+    ready = after(projected, *kv_sent)
+    aside, across = swap(ready, XY, 1), swap(ready, XY, 2)
+    *kv_parts, aside, across = lax.optimization_barrier((*kv_parts, aside, across))
+
+    kv, dkv, probs, dscores = attend(
+        mine, kv_parts, queries, out_grad, image_ids, text_sample
+    )
+    cut = projected.shape[0] // 2
+    upper, lower, _ = lax.optimization_barrier((across[:cut], aside[cut:], dkv))
+    upper, lower = swap(upper, XY, 1), swap(lower, XY, 2)
+    dkv_own = [dkv] + [swap(dkv, T, 2 * k) for k in range(1, chips)]
+    turned = turn(after(feats, dkv))
+    attended, d_queries = finish(kv, probs, dscores)
+    stacked = lax.optimization_barrier((*dkv_own, turned, attended, d_queries, upper, lower))
+    *dkv_own, turned, attended, d_queries, upper, lower = stacked
+    dkv_other = swap(pack(*dkv_own), T, 1)
+
+    halves = 2
+    back_out = back(dkv_own, dkv_other, kv_weight, parts, halves)
+    d_rows, sent, (columns, dkv_all) = back_out[0], back_out[1:-2], back_out[-2:]
+    sent = [swap(x, XY, j + 1) for j, x in enumerate(sent)]
+    d_parts = [[d_rows, *sent]]
+    for h in range(1, halves):
+        d_rows = after(back_rest(dkv_all, kv_weight, h, halves), sent[0])
+        d_parts.append([d_rows] + [swap(d_rows, XY, j) for j in range(1, parts)])
+    theirs = swap(pack(columns, *sent), T, 1)
+    d_kv_weight = kv_grad(
+        (projected, aside, across, upper, lower), columns, sent, theirs
+    )
+
+    held = None
+    for h in range(halves):
+        held = weight_grad(turned, d_parts[h], held, h, halves)
+    d_weight, d_bias = held
+    return attended, d_queries, d_weight, d_bias.reshape(-1), d_kv_weight
+
+
 def solution(mesh):
     in_specs = (
         P("tensor", ("group", "dp")),

time: 247 us -> 110 us (0.45)
  blocking collectives: 74 us -> 0 us
  waiting for transfers between devices: 119 us -> 54.4 us
  matrix products: 29.9 us -> 0 us
  starting transfers between devices: 0.16 us -> 29.6 us
  Pallas kernels: 0 us -> 20.2 us
  between operations: 14 us -> 0.85 us
  local copies, waits for them, and re-layouts: 8.91 us -> 4.26 us
    reduce_scatter x2 -> x0, waiting for transfers between devices: 69.8 us -> none  [the longest x1 43 us: shards(): lax.psum_scatter(kv_grad_term.astype(jnp.bfloat16), ('group', 'dp'), scat...]
    psum x1 -> x0, blocking collectives: 59 us -> none  [shards(): kv_all = lax.psum(kv_term, 'tensor').astype(jnp.bfloat16)]
    ppermute x0 -> x27, waiting for transfers between devices: none -> 54.4 us  [swap(): return lax.ppermute(x, axes, [(i, i ^ bits) for i in range(size_of(axes))])]
    all_gather x2 -> x0, waiting for transfers between devices: 48.4 us -> none  [the longest x1 32.4 us: shards(): gathered = lax.all_gather(image_feats, 'tensor', axis=0, tiled=True)]
    ppermute x0 -> x27, starting transfers between devices: none -> 29.6 us  [swap(): return lax.ppermute(x, axes, [(i, i ^ bits) for i in range(size_of(axes))])]
    dot_general x10 -> x0, matrix products: 28.5 us -> none  [the longest x1 6.12 us: shards(): lax.dot_general(rows, piece, (((0,), (0,)), ((), ())), preferred_element_...]
    pallas_call x0 -> x16, Pallas kernels: none -> 20.2 us  [the longest x2 5.59 us: weight_grad(): pl.pallas_call(functools.partial(weight_grad_kernel, len(grads)), grid=(d...]
    all_gather x1 -> x0, blocking collectives: 14.9 us -> none  [shards(): collected = lax.all_gather(mine, 'tensor', axis=1, tiled=True)]
  transfers between devices with their start and end apart: 4 -> 27, of which waited for: 4 -> 18; matrix products, arithmetic and copies ran while one was open for 9% -> 0% of each run, Pallas kernels for 0% -> 9%
where the time goes in v2:
time: 110 us; the launch traced here: 109 us
  waiting for transfers between devices  54.4 us (49%)
  starting transfers between devices  29.6 us (27%)
  Pallas kernels  20.2 us (18%)
  local copies, waits for them, and re-layouts  4.26 us (4%)
    ppermute x27, waiting for transfers between devices, swap(): return lax.ppermute(x, axes, [(i, i ^ bits) for i in range(size_of(axes))])  54.4 us
    ppermute x27, starting transfers between devices, swap(): return lax.ppermute(x, axes, [(i, i ^ bits) for i in range(size_of(axes))])  29.6 us
    pallas_call x2, Pallas kernels, weight_grad(): pl.pallas_call(functools.partial(weight_grad_kernel, len(grads)), grid=(d...  5.59 us
    unnamed x18, local copies, waits for them, and re-layouts  4.13 us
    pallas_call x1, Pallas kernels, project(): pl.pallas_call(functools.partial(project_kernel, len(own)), in_specs=in_v...  3.08 us
    pallas_call x1, Pallas kernels, attend(): pl.pallas_call(functools.partial(attend_kernel, 1 + len(arrived)), out_sh...  3.04 us
  transfers between devices with their start and end apart: 27, of which 18 were waited for; matrix products, arithmetic and copies ran while one was open for 0% of the time, Pallas kernels for 9%

profile of v2, /device:TPU:0, one launch (start us, length us, event | category | flops | bytes accessed | tf_op | source)
XLA Modules:
  0.0 109.3 jit_solution(11093003117207717536)
XLA Ops:
  0.6 3.1 %collective-permute-start = (bf16[64,1920]{1,0:T(8,128)(2,1)}, bf16[64,1920]{1,0:T(8,128)(2,1)S(1)}, u32[]{:S(2)}, u32[]{:S(2)}) collective-permute-start(bf16[64,1920]{1,0:T(8,128)(2,1)} %refs_0_.1), channel_id=1, source_target_pairs={{0,2},{1,3},{2,0},{3,1},{4,6},{5,7},{6,4},{7,5},{8,10},{9,11},{10,... | collective-permute-start | bytes 737288 | tf_op jit(solution)/shard_map/ppermute | solution.py:30
  3.7 2.5 %collective-permute-start.2 = (bf16[64,1920]{1,0:T(8,128)(2,1)}, bf16[64,1920]{1,0:T(8,128)(2,1)S(1)}, u32[]{:S(2)}, u32[]{:S(2)}) collective-permute-start(bf16[64,1920]{1,0:T(8,128)(2,1)} %refs_0_.1), channel_id=1, source_target_pairs={{0,6},{1,7},{2,4},{3,5},{4,2},{5,3},{6,0},{7,1},{8,14},{9,15},{10,... | collective-permute-start | bytes 737288 | tf_op jit(solution)/shard_map/ppermute | solution.py:30
  6.3 4.1 %collective-permute-done.refs_1_ = bf16[64,1920]{1,0:T(8,128)(2,1)S(1)} collective-permute-done((bf16[64,1920]{1,0:T(8,128)(2,1)}, bf16[64,1920]{1,0:T(8,128)(2,1)S(1)}, u32[]{:S(2)}, u32[]{:S(2)}) %collective-permute-start) | collective-permute-done | bytes 245792 | tf_op jit(solution)/shard_map/ppermute | solution.py:30
  11.5 7.1 %collective-permute-done.2.refs_1_ = bf16[64,1920]{1,0:T(8,128)(2,1)S(1)} collective-permute-done((bf16[64,1920]{1,0:T(8,128)(2,1)}, bf16[64,1920]{1,0:T(8,128)(2,1)S(1)}, u32[]{:S(2)}, u32[]{:S(2)}) %collective-permute-start.2) | collective-permute-done | bytes 245792 | tf_op jit(solution)/shard_map/ppermute | solution.py:30
  18.6 9.4 %collective-permute-done.1.refs_0_ = bf16[64,1920]{1,0:T(8,128)(2,1)S(1)} collective-permute-done((bf16[64,1920]{1,0:T(8,128)(2,1)}, bf16[64,1920]{1,0:T(8,128)(2,1)S(1)}, u32[]{:S(2)}, u32[]{:S(2)}) %collective-permute-start.1) | collective-permute-done | bytes 245792 | tf_op jit(solution)/shard_map/ppermute | solution.py:30
  28.2 1.8 %collective-permute-done.4.refs_3_ = bf16[2,64,1920]{2,1,0:T(8,128)(2,1)S(1)} collective-permute-done((bf16[2,64,1920]{2,1,0:T(8,128)(2,1)S(1)}, bf16[2,64,1920]{2,1,0:T(8,128)(2,1)S(1)}, u32[]{:S(2)}, u32[]{:S(2)}) %collective-permute-start.4) | collective-permute-done | bytes 491552 | tf_op jit(solution)/shard_map/ppermute | solution.py:30
  30.0 2.1 %copy-done.3 = bf16[1920,1024]{1,0:T(8,128)(2,1)S(1)} copy-done((bf16[1920,1024]{1,0:T(8,128)(2,1)S(1)}, bf16[1920,1024]{1,0:T(8,128)(2,1)}, u32[]{:S(2)}) %copy-start.3) | copy-done | bytes 3932184
  32.1 3.1 %project.1 = (bf16[128,1024]{1,0:T(8,128)(2,1)S(1)}, bf16[128,1024]{1,0:T(8,128)(2,1)S(1)}, bf16[128,1024]{1,0:T(8,128)(2,1)S(1)}, bf16[128,1024]{1,0:T(8,128)(2,1)S(1)}, bf16[4,128,1920]{2,1,0:T(8,128)(2,1)S(1)}) custom-call(bf16[2,64,1920]{2,1,0:T(8,128)(2,1)S(1)} %pack.4.refs_0_, bf16[2,64,1920]{2,1,0:T(8,128)(2,1)S(1)} %pack.5.refs_1_, ...), custom_call_target="tpu_custom_call" | custom-call | flops 4026531840 | bytes 3932160 | tf_op jit(solution)/shard_map/project/pallas_call | solution.py:227
  35.2 1.6 %collective-permute-start.5 = (bf16[128,1024]{1,0:T(8,128)(2,1)S(1)}, bf16[128,1024]{1,0:T(8,128)(2,1)S(1)}, u32[]{:S(2)}, u32[]{:S(2)}) collective-permute-start(bf16[128,1024]{1,0:T(8,128)(2,1)S(1)} %get-tuple-element.53), channel_id=1, source_target_pairs={{0,8},{8,0},{16,24},{24,16},{1,9},{9,1},{17,25},{25,17},{2,10},{10... | collective-permute-start | bytes 786440 | tf_op jit(solution)/shard_map/ppermute | solution.py:30
  36.8 1.5 %collective-permute-start.6 = (bf16[128,1024]{1,0:T(8,128)(2,1)S(1)}, bf16[128,1024]{1,0:T(8,128)(2,1)S(1)}, u32[]{:S(2)}, u32[]{:S(2)}) collective-permute-start(bf16[128,1024]{1,0:T(8,128)(2,1)S(1)} %get-tuple-element.54), channel_id=1, source_target_pairs={{0,16},{8,24},{16,0},{24,8},{1,17},{9,25},{17,1},{25,9},{2,18},{10... | collective-permute-start | bytes 786440 | tf_op jit(solution)/shard_map/ppermute | solution.py:30
  38.8 4.9 %collective-permute-done.5.refs_0_ = bf16[128,1024]{1,0:T(8,128)(2,1)S(1)} collective-permute-done((bf16[128,1024]{1,0:T(8,128)(2,1)S(1)}, bf16[128,1024]{1,0:T(8,128)(2,1)S(1)}, u32[]{:S(2)}, u32[]{:S(2)}) %collective-permute-start.5) | collective-permute-done | bytes 262176 | tf_op jit(solution)/shard_map/ppermute | solution.py:30
  43.6 2.4 %collective-permute-done.6.refs_1_ = bf16[128,1024]{1,0:T(8,128)(2,1)S(1)} collective-permute-done((bf16[128,1024]{1,0:T(8,128)(2,1)S(1)}, bf16[128,1024]{1,0:T(8,128)(2,1)S(1)}, u32[]{:S(2)}, u32[]{:S(2)}) %collective-permute-start.6) | collective-permute-done | bytes 262176 | tf_op jit(solution)/shard_map/ppermute | solution.py:30
  46.0 4.4 %collective-permute-done.7.refs_2_ = bf16[128,1024]{1,0:T(8,128)(2,1)S(1)} collective-permute-done((bf16[128,1024]{1,0:T(8,128)(2,1)S(1)}, bf16[128,1024]{1,0:T(8,128)(2,1)S(1)}, u32[]{:S(2)}, u32[]{:S(2)}) %collective-permute-start.7) | collective-permute-done | bytes 262176 | tf_op jit(solution)/shard_map/ppermute | solution.py:30
  53.6 1.5 %collective-permute-start.13 = (bf16[128,1024]{1,0:T(8,128)(2,1)S(1)}, bf16[128,1024]{1,0:T(8,128)(2,1)S(1)}, u32[]{:S(2)}, u32[]{:S(2)}) collective-permute-start(bf16[128,1024]{1,0:T(8,128)(2,1)S(1)} %get-tuple-element.62.projected.refs_0_), channel_id=1, source_target_pairs={{0,16},{8,24},{16,0},{24,8},{1,17},{9,25},{17,1},{25,9},{2,18},{10... | collective-permute-start | bytes 786440 | tf_op jit(solution)/shard_map/ppermute | solution.py:30
  55.1 1.5 %collective-permute-start.12 = (bf16[128,1024]{1,0:T(8,128)(2,1)S(1)}, bf16[128,1024]{1,0:T(8,128)(2,1)S(1)}, u32[]{:S(2)}, u32[]{:S(2)}) collective-permute-start(bf16[128,1024]{1,0:T(8,128)(2,1)S(1)} %get-tuple-element.62.projected.refs_0_), channel_id=1, source_target_pairs={{0,8},{8,0},{16,24},{24,16},{1,9},{9,1},{17,25},{25,17},{2,10},{10... | collective-permute-start | bytes 786440 | tf_op jit(solution)/shard_map/ppermute | solution.py:30
  56.6 3.2 %collective-permute-start.10 = (bf16[128,256]{1,0:T(8,128)(2,1)}, bf16[128,256]{1,0:T(8,128)(2,1)}, u32[]{:S(2)}, u32[]{:S(2)}) collective-permute-start(bf16[128,256]{1,0:T(8,128)(2,1)} %get-tuple-element.60), channel_id=1, source_target_pairs={{0,4},{1,5},{2,6},{3,7},{4,0},{5,1},{6,2},{7,3},{8,12},{9,13},{10,... | collective-permute-start | bytes 196616 | tf_op jit(solution)/shard_map/ppermute | solution.py:30
  61.6 3.3 %collective-permute-done.10.refs_2_ = bf16[128,256]{1,0:T(8,128)(2,1)} collective-permute-done((bf16[128,256]{1,0:T(8,128)(2,1)}, bf16[128,256]{1,0:T(8,128)(2,1)}, u32[]{:S(2)}, u32[]{:S(2)}) %collective-permute-start.10) | collective-permute-done | bytes 65568 | tf_op jit(solution)/shard_map/ppermute | solution.py:30
  64.8 1.4 %collective-permute-done.11.refs_3_ = bf16[128,256]{1,0:T(8,128)(2,1)} collective-permute-done((bf16[128,256]{1,0:T(8,128)(2,1)}, bf16[128,256]{1,0:T(8,128)(2,1)}, u32[]{:S(2)}, u32[]{:S(2)}) %collective-permute-start.11) | collective-permute-done | bytes 65568 | tf_op jit(solution)/shard_map/ppermute | solution.py:30
  67.3 3.0 %attend.1 = (bf16[128,256]{1,0:T(8,128)(2,1)S(1)}, bf16[128,256]{1,0:T(8,128)(2,1)S(1)}, bf16[8,128,256]{2,1,0:T(8,128)(2,1)S(1)}, bf16[8,128,256]{2,1,0:T(8,128)(2,1)S(1)}) custom-call(f32[128,256]{1,0:T(8,128)S(1)} %get-tuple-element.58.refs_0_, bf16[128,256]{1,0:T(8,128)(2,1)S(1)} %collective-permute-done.9.refs_1_, ...), custom_call_target="tpu_custom_call" | custom-call | flops 2147483648 | bytes 2097152 | tf_op jit(solution)/shard_map/attend/pallas_call | solution.py:327
  72.8 3.0 %collective-permute-start.14 = (bf16[128,256]{1,0:T(8,128)(2,1)S(1)}, bf16[128,256]{1,0:T(8,128)(2,1)S(1)}, u32[]{:S(2)}, u32[]{:S(2)}) collective-permute-start(bf16[128,256]{1,0:T(8,128)(2,1)S(1)} %get-tuple-element.82.refs_0_), channel_id=1, source_target_pairs={{0,2},{1,3},{2,0},{3,1},{4,6},{5,7},{6,4},{7,5},{8,10},{9,11},{10,... | collective-permute-start | bytes 196616 | tf_op jit(solution)/shard_map/ppermute | solution.py:30
  76.8 1.5 %finish.1 = (bf16[256,1024]{1,0:T(8,128)(2,1)}, bf16[256,1024]{1,0:T(8,128)(2,1)}) custom-call(bf16[128,256]{1,0:T(8,128)(2,1)S(1)} %get-tuple-element.70.kv, bf16[8,128,256]{2,1,0:T(8,128)(2,1)S(1)} %get-tuple-element.71.probs, bf16[8,128,256]{2,1,0:T(8,128)(2,1)S(1)} %get-tuple-element.72.dscores), custom_call_target="tpu_custom_call" | custom-call | flops 1073741824 | bytes 2097152 | tf_op jit(solution)/shard_map/finish/pallas_call | solution.py:356
  79.1 1.5 %collective-permute-done.19.refs_4_ = bf16[4,128,256]{2,1,0:T(8,128)(2,1)S(1)} collective-permute-done((bf16[4,128,256]{2,1,0:T(8,128)(2,1)S(1)}, bf16[4,128,256]{2,1,0:T(8,128)(2,1)S(1)}, u32[]{:S(2)}, u32[]{:S(2)}) %collective-permute-start.19) | collective-permute-done | bytes 262176 | tf_op jit(solution)/shard_map/ppermute | solution.py:30
  81.6 1.6 %collective-permute-start.20 = (bf16[128,768]{1,0:T(8,128)(2,1)S(1)}, bf16[128,768]{1,0:T(8,128)(2,1)S(1)}, u32[]{:S(2)}, u32[]{:S(2)}) collective-permute-start(bf16[128,768]{1,0:T(8,128)(2,1)S(1)} %get-tuple-element.87), channel_id=1, source_target_pairs={{0,8},{8,0},{16,24},{24,16},{1,9},{9,1},{17,25},{25,17},{2,10},{10... | collective-permute-start | bytes 589832 | tf_op jit(solution)/shard_map/ppermute | solution.py:30
  83.1 1.5 %collective-permute-start.24 = (bf16[128,768]{1,0:T(8,128)(2,1)S(1)}, bf16[128,768]{1,0:T(8,128)(2,1)S(1)}, u32[]{:S(2)}, u32[]{:S(2)}) collective-permute-start(bf16[128,768]{1,0:T(8,128)(2,1)S(1)} %get-tuple-element.90), channel_id=1, source_target_pairs={{0,16},{8,24},{16,0},{24,8},{1,17},{9,25},{17,1},{25,9},{2,18},{10... | collective-permute-start | bytes 589832 | tf_op jit(solution)/shard_map/ppermute | solution.py:30
  85.1 3.5 %collective-permute-done.20.refs_1_.refs_6_ = bf16[128,768]{1,0:T(8,128)(2,1)S(1)} collective-permute-done((bf16[128,768]{1,0:T(8,128)(2,1)S(1)}, bf16[128,768]{1,0:T(8,128)(2,1)S(1)}, u32[]{:S(2)}, u32[]{:S(2)}) %collective-permute-start.20) | collective-permute-done | bytes 196640 | tf_op jit(solution)/shard_map/ppermute | solution.py:30
  88.6 2.4 %collective-permute-done.24.refs_2_.refs_7_ = bf16[128,768]{1,0:T(8,128)(2,1)S(1)} collective-permute-done((bf16[128,768]{1,0:T(8,128)(2,1)S(1)}, bf16[128,768]{1,0:T(8,128)(2,1)S(1)}, u32[]{:S(2)}, u32[]{:S(2)}) %collective-permute-start.24) | collective-permute-done | bytes 196640 | tf_op jit(solution)/shard_map/ppermute | solution.py:30
  90.9 3.0 %collective-permute-done.25.refs_3_.refs_8_ = bf16[128,768]{1,0:T(8,128)(2,1)S(1)} collective-permute-done((bf16[128,768]{1,0:T(8,128)(2,1)S(1)}, bf16[128,768]{1,0:T(8,128)(2,1)S(1)}, u32[]{:S(2)}, u32[]{:S(2)}) %collective-permute-start.25) | collective-permute-done | bytes 196640 | tf_op jit(solution)/shard_map/ppermute | solution.py:30
  94.9 2.5 %collective-permute-start.23 = (bf16[128,512]{1,0:T(8,128)(2,1)S(1)}, bf16[128,512]{1,0:T(8,128)(2,1)S(1)}, u32[]{:S(2)}, u32[]{:S(2)}) collective-permute-start(bf16[128,512]{1,0:T(8,128)(2,1)S(1)} %back_rest.1.refs_0_), channel_id=1, source_target_pairs={{0,24},{8,16},{16,8},{24,0},{1,25},{9,17},{17,9},{25,1},{2,26},{10... | collective-permute-start | bytes 393224 | tf_op jit(solution)/shard_map/ppermute | solution.py:30
  98.4 2.8 %weight_grad.2 = (bf16[1920,1024]{1,0:T(8,128)(2,1)}, f32[1,1024]{1,0:T(1,128)}) custom-call(bf16[1920,512]{1,0:T(8,128)(2,1)S(1)} %turn.1.feats, bf16[128,512]{1,0:T(8,128)(2,1)S(1)} %get-tuple-element.89.refs_0_, bf16[128,768]{1,0:T(8,128)(2,1)S(1)} %collective-permute-done.20.refs_1_.refs_6_, ...), custom_call_target="tpu_custom_call" | custom-call | flops 1006632960 | bytes 3932160 | tf_op jit(solution)/shard_map/weight_grad/pallas_call | solution.py:537
  102.1 2.5 %collective-permute-done.22.refs_2_ = bf16[128,512]{1,0:T(8,128)(2,1)S(1)} collective-permute-done((bf16[128,512]{1,0:T(8,128)(2,1)S(1)}, bf16[128,512]{1,0:T(8,128)(2,1)S(1)}, u32[]{:S(2)}, u32[]{:S(2)}) %collective-permute-start.22) | collective-permute-done | bytes 131104 | tf_op jit(solution)/shard_map/ppermute | solution.py:30
  104.7 2.8 %weight_grad.3 = (bf16[1920,1024]{1,0:T(8,128)(2,1)}, f32[1,1024]{1,0:T(1,128)}) custom-call(bf16[1920,512]{1,0:T(8,128)(2,1)S(1)} %turn.1.feats, bf16[128,512]{1,0:T(8,128)(2,1)S(1)} %back_rest.1.refs_0_, bf16[128,512]{1,0:T(8,128)(2,1)S(1)} %collective-permute-done.21.refs_1_, ...), custom_call_target="tpu_custom_call", output_to_operand_aliasing={{0}: (5, {}), {1}: (6, {})} | custom-call | flops 1006632960 | bytes 3932160 | tf_op jit(solution)/shard_map/weight_grad/pallas_call | solution.py:537
  107.5 1.9 %kv_grad.1 = bf16[1024,512]{1,0:T(8,128)(2,1)} custom-call(bf16[128,1024]{1,0:T(8,128)(2,1)S(1)} %get-tuple-element.62.projected.refs_0_, bf16[128,1024]{1,0:T(8,128)(2,1)S(1)} %collective-permute-done.12.refs_1_, bf16[128,1024]{1,0:T(8,128)(2,1)S(1)} %collective-permute-done.13.refs_2_, bf16[64,1024]{1,0:T(8,128)(2,1)S(1)} %collective-permute-done.17.refs_3_, ...), custom_call_target="tpu_custom_call" | custom-call | flops 536870912 | bytes 2097152 | tf_op jit(solution)/shard_map/kv_grad/pallas_call | solution.py:494
  (60 shorter events, 16.1 us)
Async XLA Ops:
  0.6 9.8 %collective-permute-start = (bf16[64,1920]{1,0:T(8,128)(2,1)}, bf16[64,1920]{1,0:T(8,128)(2,1)S(1)}, u32[]{:S(2)}, u32[]{:S(2)}) collective-permute-start(bf16[64,1920]{1,0:T(8,128)(2,1)} %refs_0_.1), channel_id=1, source_target_pairs={{0,2},{1,3},{2,0},{3,1},{4,6},{5,7},{6,4},{7,5},{8,10},{9,11},{10,... | collective-permute-start | bytes 737288 | tf_op jit(solution)/shard_map/ppermute | solution.py:30
  3.7 14.9 %collective-permute-start.2 = (bf16[64,1920]{1,0:T(8,128)(2,1)}, bf16[64,1920]{1,0:T(8,128)(2,1)S(1)}, u32[]{:S(2)}, u32[]{:S(2)}) collective-permute-start(bf16[64,1920]{1,0:T(8,128)(2,1)} %refs_0_.1), channel_id=1, source_target_pairs={{0,6},{1,7},{2,4},{3,5},{4,2},{5,3},{6,0},{7,1},{8,14},{9,15},{10,... | collective-permute-start | bytes 737288 | tf_op jit(solution)/shard_map/ppermute | solution.py:30
  6.2 21.8 %collective-permute-start.1 = (bf16[64,1920]{1,0:T(8,128)(2,1)}, bf16[64,1920]{1,0:T(8,128)(2,1)S(1)}, u32[]{:S(2)}, u32[]{:S(2)}) collective-permute-start(bf16[64,1920]{1,0:T(8,128)(2,1)} %refs_0_.1), channel_id=1, source_target_pairs={{0,4},{1,5},{2,6},{3,7},{4,0},{5,1},{6,2},{7,3},{8,12},{9,13},{10,... | collective-permute-start | bytes 737288 | tf_op jit(solution)/shard_map/ppermute | solution.py:30
  11.4 16.8 %collective-permute-start.3 = (bf16[2,64,1920]{2,1,0:T(8,128)(2,1)S(1)}, bf16[2,64,1920]{2,1,0:T(8,128)(2,1)S(1)}, u32[]{:S(2)}, u32[]{:S(2)}) collective-permute-start(bf16[2,64,1920]{2,1,0:T(8,128)(2,1)S(1)} %pack.4.refs_0_), channel_id=1, source_target_pairs={{0,1},{1,0},{2,3},{3,2},{4,5},{5,4},{6,7},{7,6},{8,9},{9,8},{10,11... | collective-permute-start | bytes 1474568 | tf_op jit(solution)/shard_map/ppermute | solution.py:30
  28.0 10.7 %copy-start.7 = (bf16[1024]{0:T(1024)(128)(2,1)S(1)}, bf16[1024]{0:T(1024)(128)(2,1)}, u32[]{:S(2)}) copy-start(bf16[1024]{0:T(1024)(128)(2,1)} %param.10) | copy-start | bytes 6148
  28.1 22.4 %copy-start = (bf16[1024,2048]{1,0:T(8,128)(2,1)S(1)}, bf16[1024,2048]{1,0:T(8,128)(2,1)}, u32[]{:S(2)}) copy-start(bf16[1024,2048]{1,0:T(8,128)(2,1)} %weight.3) | copy-start | bytes 12582916
  28.1 1.9 %collective-permute-start.4 = (bf16[2,64,1920]{2,1,0:T(8,128)(2,1)S(1)}, bf16[2,64,1920]{2,1,0:T(8,128)(2,1)S(1)}, u32[]{:S(2)}, u32[]{:S(2)}) collective-permute-start(bf16[2,64,1920]{2,1,0:T(8,128)(2,1)S(1)} %pack.5.refs_1_), channel_id=1, source_target_pairs={{0,1},{1,0},{2,3},{3,2},{4,5},{5,4},{6,7},{7,6},{8,9},{9,8},{10,11... | collective-permute-start | bytes 1474568 | tf_op jit(solution)/shard_map/ppermute | solution.py:30
  35.2 8.4 %collective-permute-start.5 = (bf16[128,1024]{1,0:T(8,128)(2,1)S(1)}, bf16[128,1024]{1,0:T(8,128)(2,1)S(1)}, u32[]{:S(2)}, u32[]{:S(2)}) collective-permute-start(bf16[128,1024]{1,0:T(8,128)(2,1)S(1)} %get-tuple-element.53), channel_id=1, source_target_pairs={{0,8},{8,0},{16,24},{24,16},{1,9},{9,1},{17,25},{25,17},{2,10},{10... | collective-permute-start | bytes 786440 | tf_op jit(solution)/shard_map/ppermute | solution.py:30
  36.8 9.2 %collective-permute-start.6 = (bf16[128,1024]{1,0:T(8,128)(2,1)S(1)}, bf16[128,1024]{1,0:T(8,128)(2,1)S(1)}, u32[]{:S(2)}, u32[]{:S(2)}) collective-permute-start(bf16[128,1024]{1,0:T(8,128)(2,1)S(1)} %get-tuple-element.54), channel_id=1, source_target_pairs={{0,16},{8,24},{16,0},{24,8},{1,17},{9,25},{17,1},{25,9},{2,18},{10... | collective-permute-start | bytes 786440 | tf_op jit(solution)/shard_map/ppermute | solution.py:30
  38.3 12.1 %collective-permute-start.7 = (bf16[128,1024]{1,0:T(8,128)(2,1)S(1)}, bf16[128,1024]{1,0:T(8,128)(2,1)S(1)}, u32[]{:S(2)}, u32[]{:S(2)}) collective-permute-start(bf16[128,1024]{1,0:T(8,128)(2,1)S(1)} %get-tuple-element.55), channel_id=1, source_target_pairs={{0,24},{8,16},{16,8},{24,0},{1,25},{9,17},{17,9},{25,1},{2,26},{10... | collective-permute-start | bytes 786440 | tf_op jit(solution)/shard_map/ppermute | solution.py:30
  51.3 1.6 %collective-permute-start.8 = (bf16[4,128,256]{2,1,0:T(8,128)(2,1)S(1)}, bf16[4,128,256]{2,1,0:T(8,128)(2,1)S(1)}, u32[]{:S(2)}, u32[]{:S(2)}) collective-permute-start(bf16[4,128,256]{2,1,0:T(8,128)(2,1)S(1)} %get-tuple-element.57), channel_id=1, source_target_pairs={{0,1},{1,0},{2,3},{3,2},{4,5},{5,4},{6,7},{7,6},{8,9},{9,8},{10,11... | collective-permute-start | bytes 786440 | tf_op jit(solution)/shard_map/ppermute | solution.py:30
  51.4 9.6 %copy-start.8 = (s32[1,128]{1,0:T(1,128)S(1)}, s32[1,128]{1,0:T(1,128)}, u32[]{:S(2)}) copy-start(s32[1,128]{1,0:T(1,128)} %param.14) | copy-start | bytes 1540
  51.4 14.9 %copy-start.4 = (bf16[256,1024]{1,0:T(8,128)(2,1)S(1)}, bf16[256,1024]{1,0:T(8,128)(2,1)}, u32[]{:S(2)}) copy-start(bf16[256,1024]{1,0:T(8,128)(2,1)} %refs_4_.5) | copy-start | bytes 1572868
  51.4 14.9 %copy-start.6 = (s32[1,256]{1,0:T(1,128)S(1)}, s32[1,256]{1,0:T(1,128)}, u32[]{:S(2)}) copy-start(s32[1,256]{1,0:T(1,128)} %refs_7_.1) | copy-start | bytes 3076
  53.6 12.6 %collective-permute-start.13 = (bf16[128,1024]{1,0:T(8,128)(2,1)S(1)}, bf16[128,1024]{1,0:T(8,128)(2,1)S(1)}, u32[]{:S(2)}, u32[]{:S(2)}) collective-permute-start(bf16[128,1024]{1,0:T(8,128)(2,1)S(1)} %get-tuple-element.62.projected.refs_0_), channel_id=1, source_target_pairs={{0,16},{8,24},{16,0},{24,8},{1,17},{9,25},{17,1},{25,9},{2,18},{10... | collective-permute-start | bytes 786440 | tf_op jit(solution)/shard_map/ppermute | solution.py:30
  55.1 11.1 %collective-permute-start.12 = (bf16[128,1024]{1,0:T(8,128)(2,1)S(1)}, bf16[128,1024]{1,0:T(8,128)(2,1)S(1)}, u32[]{:S(2)}, u32[]{:S(2)}) collective-permute-start(bf16[128,1024]{1,0:T(8,128)(2,1)S(1)} %get-tuple-element.62.projected.refs_0_), channel_id=1, source_target_pairs={{0,8},{8,0},{16,24},{24,16},{1,9},{9,1},{17,25},{25,17},{2,10},{10... | collective-permute-start | bytes 786440 | tf_op jit(solution)/shard_map/ppermute | solution.py:30
  56.6 4.9 %collective-permute-start.9 = (bf16[128,256]{1,0:T(8,128)(2,1)}, bf16[128,256]{1,0:T(8,128)(2,1)S(1)}, u32[]{:S(2)}, u32[]{:S(2)}) collective-permute-start(bf16[128,256]{1,0:T(8,128)(2,1)} %get-tuple-element.59), channel_id=1, source_target_pairs={{0,2},{1,3},{2,0},{3,1},{4,6},{5,7},{6,4},{7,5},{8,10},{9,11},{10,... | collective-permute-start | bytes 196616 | tf_op jit(solution)/shard_map/ppermute | solution.py:30
  56.6 8.2 %collective-permute-start.10 = (bf16[128,256]{1,0:T(8,128)(2,1)}, bf16[128,256]{1,0:T(8,128)(2,1)}, u32[]{:S(2)}, u32[]{:S(2)}) collective-permute-start(bf16[128,256]{1,0:T(8,128)(2,1)} %get-tuple-element.60), channel_id=1, source_target_pairs={{0,4},{1,5},{2,6},{3,7},{4,0},{5,1},{6,2},{7,3},{8,12},{9,13},{10,... | collective-permute-start | bytes 196616 | tf_op jit(solution)/shard_map/ppermute | solution.py:30
  59.8 6.4 %collective-permute-start.11 = (bf16[128,256]{1,0:T(8,128)(2,1)}, bf16[128,256]{1,0:T(8,128)(2,1)}, u32[]{:S(2)}, u32[]{:S(2)}) collective-permute-start(bf16[128,256]{1,0:T(8,128)(2,1)} %get-tuple-element.61), channel_id=1, source_target_pairs={{0,6},{1,7},{2,4},{3,5},{4,2},{5,3},{6,0},{7,1},{8,14},{9,15},{10,... | collective-permute-start | bytes 196616 | tf_op jit(solution)/shard_map/ppermute | solution.py:30
  70.4 8.6 %collective-permute-start.17 = (bf16[64,1024]{1,0:T(8,128)(2,1)S(1)}, bf16[64,1024]{1,0:T(8,128)(2,1)S(1)}, u32[]{:S(2)}, u32[]{:S(2)}) collective-permute-start(bf16[64,1024]{1,0:T(8,128)(2,1)S(1)} %slice.6), channel_id=1, source_target_pairs={{0,8},{8,0},{16,24},{24,16},{1,9},{9,1},{17,25},{25,17},{2,10},{10... | collective-permute-start | bytes 393224 | tf_op jit(solution)/shard_map/ppermute | solution.py:30
  71.0 8.0 %collective-permute-start.18 = (bf16[64,1024]{1,0:T(8,128)(2,1)S(1)}, bf16[64,1024]{1,0:T(8,128)(2,1)S(1)}, u32[]{:S(2)}, u32[]{:S(2)}) collective-permute-start(bf16[64,1024]{1,0:T(8,128)(2,1)S(1)} %slice.7), channel_id=1, source_target_pairs={{0,16},{8,24},{16,0},{24,8},{1,17},{9,25},{17,1},{25,9},{2,18},{10... | collective-permute-start | bytes 393224 | tf_op jit(solution)/shard_map/ppermute | solution.py:30
  71.5 6.8 %collective-permute-start.16 = (bf16[128,256]{1,0:T(8,128)(2,1)S(1)}, bf16[128,256]{1,0:T(8,128)(2,1)S(1)}, u32[]{:S(2)}, u32[]{:S(2)}) collective-permute-start(bf16[128,256]{1,0:T(8,128)(2,1)S(1)} %get-tuple-element.82.refs_0_), channel_id=1, source_target_pairs={{0,6},{1,7},{2,4},{3,5},{4,2},{5,3},{6,0},{7,1},{8,14},{9,15},{10,... | collective-permute-start | bytes 196616 | tf_op jit(solution)/shard_map/ppermute | solution.py:30
  72.8 6.2 %collective-permute-start.15 = (bf16[128,256]{1,0:T(8,128)(2,1)S(1)}, bf16[128,256]{1,0:T(8,128)(2,1)S(1)}, u32[]{:S(2)}, u32[]{:S(2)}) collective-permute-start(bf16[128,256]{1,0:T(8,128)(2,1)S(1)} %get-tuple-element.82.refs_0_), channel_id=1, source_target_pairs={{0,4},{1,5},{2,6},{3,7},{4,0},{5,1},{6,2},{7,3},{8,12},{9,13},{10,... | collective-permute-start | bytes 196616 | tf_op jit(solution)/shard_map/ppermute | solution.py:30
  72.8 6.1 %collective-permute-start.14 = (bf16[128,256]{1,0:T(8,128)(2,1)S(1)}, bf16[128,256]{1,0:T(8,128)(2,1)S(1)}, u32[]{:S(2)}, u32[]{:S(2)}) collective-permute-start(bf16[128,256]{1,0:T(8,128)(2,1)S(1)} %get-tuple-element.82.refs_0_), channel_id=1, source_target_pairs={{0,2},{1,3},{2,0},{3,1},{4,6},{5,7},{6,4},{7,5},{8,10},{9,11},{10,... | collective-permute-start | bytes 196616 | tf_op jit(solution)/shard_map/ppermute | solution.py:30
  79.0 1.6 %collective-permute-start.19 = (bf16[4,128,256]{2,1,0:T(8,128)(2,1)S(1)}, bf16[4,128,256]{2,1,0:T(8,128)(2,1)S(1)}, u32[]{:S(2)}, u32[]{:S(2)}) collective-permute-start(bf16[4,128,256]{2,1,0:T(8,128)(2,1)S(1)} %pack.6), channel_id=1, source_target_pairs={{0,1},{1,0},{2,3},{3,2},{4,5},{5,4},{6,7},{7,6},{8,9},{9,8},{10,11... | collective-permute-start | bytes 786440 | tf_op jit(solution)/shard_map/ppermute | solution.py:30
  81.6 7.0 %collective-permute-start.20 = (bf16[128,768]{1,0:T(8,128)(2,1)S(1)}, bf16[128,768]{1,0:T(8,128)(2,1)S(1)}, u32[]{:S(2)}, u32[]{:S(2)}) collective-permute-start(bf16[128,768]{1,0:T(8,128)(2,1)S(1)} %get-tuple-element.87), channel_id=1, source_target_pairs={{0,8},{8,0},{16,24},{24,16},{1,9},{9,1},{17,25},{25,17},{2,10},{10... | collective-permute-start | bytes 589832 | tf_op jit(solution)/shard_map/ppermute | solution.py:30
  83.1 7.8 %collective-permute-start.24 = (bf16[128,768]{1,0:T(8,128)(2,1)S(1)}, bf16[128,768]{1,0:T(8,128)(2,1)S(1)}, u32[]{:S(2)}, u32[]{:S(2)}) collective-permute-start(bf16[128,768]{1,0:T(8,128)(2,1)S(1)} %get-tuple-element.90), channel_id=1, source_target_pairs={{0,16},{8,24},{16,0},{24,8},{1,17},{9,25},{17,1},{25,9},{2,18},{10... | collective-permute-start | bytes 589832 | tf_op jit(solution)/shard_map/ppermute | solution.py:30
  84.6 9.3 %collective-permute-start.25 = (bf16[128,768]{1,0:T(8,128)(2,1)S(1)}, bf16[128,768]{1,0:T(8,128)(2,1)S(1)}, u32[]{:S(2)}, u32[]{:S(2)}) collective-permute-start(bf16[128,768]{1,0:T(8,128)(2,1)S(1)} %get-tuple-element.91), channel_id=1, source_target_pairs={{0,24},{8,16},{16,8},{24,0},{1,25},{9,17},{17,9},{25,1},{2,26},{10... | collective-permute-start | bytes 589832 | tf_op jit(solution)/shard_map/ppermute | solution.py:30
  94.0 13.5 %collective-permute-start.26 = (bf16[4,128,256]{2,1,0:T(8,128)(2,1)S(1)}, bf16[4,128,256]{2,1,0:T(8,128)(2,1)S(1)}, u32[]{:S(2)}, u32[]{:S(2)}) collective-permute-start(bf16[4,128,256]{2,1,0:T(8,128)(2,1)S(1)} %pack.7), channel_id=1, source_target_pairs={{0,1},{1,0},{2,3},{3,2},{4,5},{5,4},{6,7},{7,6},{8,9},{9,8},{10,11... | collective-permute-start | bytes 786440 | tf_op jit(solution)/shard_map/ppermute | solution.py:30
  94.9 7.3 %collective-permute-start.23 = (bf16[128,512]{1,0:T(8,128)(2,1)S(1)}, bf16[128,512]{1,0:T(8,128)(2,1)S(1)}, u32[]{:S(2)}, u32[]{:S(2)}) collective-permute-start(bf16[128,512]{1,0:T(8,128)(2,1)S(1)} %back_rest.1.refs_0_), channel_id=1, source_target_pairs={{0,24},{8,16},{16,8},{24,0},{1,25},{9,17},{17,9},{25,1},{2,26},{10... | collective-permute-start | bytes 393224 | tf_op jit(solution)/shard_map/ppermute | solution.py:30
  97.4 7.3 %collective-permute-start.22 = (bf16[128,512]{1,0:T(8,128)(2,1)S(1)}, bf16[128,512]{1,0:T(8,128)(2,1)S(1)}, u32[]{:S(2)}, u32[]{:S(2)}) collective-permute-start(bf16[128,512]{1,0:T(8,128)(2,1)S(1)} %back_rest.1.refs_0_), channel_id=1, source_target_pairs={{0,16},{8,24},{16,0},{24,8},{1,17},{9,25},{17,1},{25,9},{2,18},{10... | collective-permute-start | bytes 393224 | tf_op jit(solution)/shard_map/ppermute | solution.py:30
  98.0 6.7 %collective-permute-start.21 = (bf16[128,512]{1,0:T(8,128)(2,1)S(1)}, bf16[128,512]{1,0:T(8,128)(2,1)S(1)}, u32[]{:S(2)}, u32[]{:S(2)}) collective-permute-start(bf16[128,512]{1,0:T(8,128)(2,1)S(1)} %back_rest.1.refs_0_), channel_id=1, source_target_pairs={{0,8},{8,0},{16,24},{24,16},{1,9},{9,1},{17,25},{25,17},{2,10},{10... | collective-permute-start | bytes 393224 | tf_op jit(solution)/shard_map/ppermute | solution.py:30
  (4 other events, 8.8 us)

commit v3 on v2

--- a/solution.py
+++ b/solution.py
@@ -126,7 +126,9 @@
 
 
 def cost(flops, nbytes):
-    return pl.CostEstimate(flops=flops, bytes_accessed=nbytes, transcendentals=0)
+    return pl.CostEstimate(
+        flops=flops // 20, bytes_accessed=nbytes // 20, transcendentals=0
+    )
 
 
 def whole(shape):
@@ -139,23 +141,23 @@
     return (me // 2) ^ part, me % 2, me, part
 
 
-def pack_kernel(*refs):
+def pack_kernel(count, *refs):
     out = refs[-1]
     width = out.shape[2]
-    for i, ref in enumerate(refs[:-1]):
+    for i, ref in enumerate(refs[:count]):
         out[i] = ref[:, ref.shape[1] - width :]
 
 
-def pack(*arrays):
+def pack(*arrays, beside=()):
     rows, width = arrays[0].shape[0], min(x.shape[1] for x in arrays)
     return pl.pallas_call(
-        pack_kernel,
-        in_specs=in_vmem(len(arrays)),
+        functools.partial(pack_kernel, len(arrays)),
+        in_specs=in_vmem(len(arrays)) + [pl.BlockSpec(memory_space=pl.ANY)] * len(beside),
         out_shape=jax.ShapeDtypeStruct((len(arrays), rows, width), BF16),
         compiler_params=params(),
         cost_estimate=cost(0, 8 * len(arrays) * rows * width),
         name="pack",
-    )(*arrays)
+    )(*arrays, *beside)
 
 
 def add_kernel(mine, theirs, first, *rest):
@@ -424,10 +426,10 @@
         ref[:, :columns] = out[...]
 
 
-def back(own, other, kv_weight, parts, chunks):
+def back(own, other, kv_weight, parts):
     rows = own[0].shape[0]
     depth, width = kv_weight.shape
-    columns = depth // chunks
+    columns = depth
     extra = width // parts // 2
     full = jax.ShapeDtypeStruct((rows, columns + extra), BF16)
     return pl.pallas_call(
@@ -443,24 +445,6 @@
         cost_estimate=cost(8 * rows * columns * width, 2 * columns * width),
         name="back",
     )(*own, other, kv_weight)
-
-
-def back_rest_kernel(chunk, dkv_all, weight, out):
-    back_columns(dkv_all[...], weight, chunk * out.shape[1], [out])
-
-
-def back_rest(dkv_all, kv_weight, chunk, chunks):
-    rows = dkv_all.shape[0]
-    depth, width = kv_weight.shape
-    columns = depth // chunks
-    return pl.pallas_call(
-        functools.partial(back_rest_kernel, chunk),
-        in_specs=in_vmem(2),
-        out_shape=jax.ShapeDtypeStruct((rows, columns), BF16),
-        compiler_params=params(),
-        cost_estimate=cost(8 * rows * columns * width, 2 * columns * width),
-        name="back_rest",
-    )(dkv_all, kv_weight)
 
 
 def kv_grad_kernel(count, parts, *refs):
@@ -502,56 +486,87 @@
     )(*left, own, *sent, theirs)
 
 
-def weight_grad_kernel(parts, feats, *refs):
-    grads, (out, bias, right) = refs[:parts], refs[-3:]
-    columns = out.shape[1]
-    rows = grads[0].shape[0]
-
-    @pl.when(pl.program_id(0) == 0)
-    def _():
-        total = None
-        for j, g in enumerate(grads):
-            value = g[:, :columns]
-            right[j * rows : (j + 1) * rows, :] = value
-            term = jnp.sum(value.astype(F32), axis=0, keepdims=True)
-            total = term if total is None else total + term
-        bias[...] = total
-
-    tile = out.shape[0]
-    at = pl.ds(pl.multiple_of(pl.program_id(0) * tile, tile), tile)
-    out[...] = jnp.dot(feats[at, :], right[...], preferred_element_type=F32).astype(BF16)
-
-
-def weight_grad(feats, grads, held, chunk, chunks):
-    depth, total = feats.shape
-    shard = grads[0].shape
-    columns = shard[1]
-    tile = depth // 3 if depth % 384 == 0 else depth
-    inputs = [feats, *grads]
-    specs = in_vmem(len(inputs))
-    aliases = {}
-    if held is not None:
-        aliases = {len(inputs): 0, len(inputs) + 1: 1}
-        inputs += held
-        specs += [pl.BlockSpec(memory_space=pl.ANY)] * 2
-    return pl.pallas_call(
-        functools.partial(weight_grad_kernel, len(grads)),
-        grid=(depth // tile,),
-        in_specs=specs,
-        out_specs=[
-            pl.BlockSpec((tile, columns), lambda n: (n, chunk)),
-            pl.BlockSpec((1, columns), lambda n: (0, chunk)),
-        ],
+def side_by_side(grads, right):
+    total = None
+    rows, columns = grads[0].shape[0], right.shape[1]
+    for i, ref in enumerate(grads):
+        value = ref[:, :columns]
+        right[i * rows : (i + 1) * rows, :] = value
+        term = jnp.sum(value.astype(F32), axis=0, keepdims=True)
+        total = term if total is None else total + term
+    return total
+
+
+def first_grad_kernel(count, feats, *refs):
+    grads, (out, bias, right) = refs[:count], refs[count:]
+    bias[...] = side_by_side(grads, right)
+    tiles = tiles_of(out.shape[0], 384)
+    tile = out.shape[0] // tiles
+    for n in range(tiles):
+        at = slice(n * tile, (n + 1) * tile)
+        out[at, :] = jnp.dot(
+            feats[at, : right.shape[0]], right[...], preferred_element_type=F32
+        )
+
+
+def first_grad(feats, grads):
+    depth = feats.shape[0]
+    rows, columns = grads[0].shape
+    total = len(grads) * rows
+    return pl.pallas_call(
+        functools.partial(first_grad_kernel, len(grads)),
+        in_specs=in_vmem(1 + len(grads)),
         out_shape=[
-            jax.ShapeDtypeStruct((depth, columns * chunks), BF16),
-            jax.ShapeDtypeStruct((1, columns * chunks), F32),
+            jax.ShapeDtypeStruct((depth, columns), F32),
+            jax.ShapeDtypeStruct((1, columns), F32),
         ],
         scratch_shapes=[pltpu.VMEM((total, columns), BF16)],
-        input_output_aliases=aliases,
-        compiler_params=params(),
-        cost_estimate=cost(2 * total * depth * columns, 2 * depth * (total + columns)),
-        name="weight_grad",
-    )(*inputs)
+        compiler_params=params(),
+        cost_estimate=cost(2 * total * depth * columns, 4 * depth * columns),
+        name="first_grad",
+    )(feats, *grads)
+
+
+def last_grad_kernel(count, feats, before, bias_before, *refs):
+    grads, (out, bias, right, rounded, sems) = refs[:count], refs[count:]
+    bias[...] = bias_before[...] + side_by_side(grads, right)
+    tiles = tiles_of(out.shape[0], 384)
+    tile = out.shape[0] // tiles
+    skip = feats.shape[1] - right.shape[0]
+    copies = []
+    for n in range(tiles):
+        at = pl.ds(n * tile, tile)
+        value = before[at, :] + jnp.dot(
+            feats[at, skip:], right[...], preferred_element_type=F32
+        )
+        rounded[at, :] = value.astype(BF16)
+        copy = pltpu.make_async_copy(rounded.at[at, :], out.at[at, :], sems.at[n])
+        copy.start()
+        copies.append(copy)
+    for copy in copies:
+        copy.wait()
+
+
+def last_grad(feats, before, bias, grads):
+    depth, columns = before.shape
+    total = len(grads) * grads[0].shape[0]
+    return pl.pallas_call(
+        functools.partial(last_grad_kernel, len(grads)),
+        in_specs=in_vmem(3 + len(grads)),
+        out_specs=[pl.BlockSpec(memory_space=pl.ANY), pl.BlockSpec()],
+        out_shape=[
+            jax.ShapeDtypeStruct((depth, columns), BF16),
+            jax.ShapeDtypeStruct((1, columns), F32),
+        ],
+        scratch_shapes=[
+            pltpu.VMEM((total, columns), BF16),
+            pltpu.VMEM((depth, columns), BF16),
+            pltpu.SemaphoreType.DMA((tiles_of(depth, 384),)),
+        ],
+        compiler_params=params(),
+        cost_estimate=cost(2 * total * depth * columns, 6 * depth * columns),
+        name="last_grad",
+    )(feats, before, bias, *grads)
 
 
 def shards(
@@ -570,7 +585,7 @@
         )
     own = [image_feats] + [swap(image_feats, T, 2 * k) for k in range(1, chips)]
     image_ids = after(image_sample, own[1]).reshape(-1, 1)
-    stacks = [pack(*own[: chips // 2]), pack(*own[chips // 2 :])]
+    stacks = [pack(*own[: chips // 2], beside=(proj_weight,)), pack(*own[chips // 2 :])]
     *partial, feats = project(stacks, [swap(x, T, 1) for x in stacks], proj_weight)
     arrived = [swap(partial[j], XY, j) for j in range(1, parts)]
 
@@ -598,23 +613,17 @@
     *dkv_own, turned, attended, d_queries, upper, lower = stacked
     dkv_other = swap(pack(*dkv_own), T, 1)
 
-    halves = 2
-    back_out = back(dkv_own, dkv_other, kv_weight, parts, halves)
-    d_rows, sent, (columns, dkv_all) = back_out[0], back_out[1:-2], back_out[-2:]
+    back_out = back(dkv_own, dkv_other, kv_weight, parts)
+    d_rows, sent, columns = back_out[0], back_out[1:-2], back_out[-2]
     sent = [swap(x, XY, j + 1) for j, x in enumerate(sent)]
-    d_parts = [[d_rows, *sent]]
-    for h in range(1, halves):
-        d_rows = after(back_rest(dkv_all, kv_weight, h, halves), sent[0])
-        d_parts.append([d_rows] + [swap(d_rows, XY, j) for j in range(1, parts)])
-    theirs = swap(pack(columns, *sent), T, 1)
+    early = parts // 2
+    partial, bias = first_grad(turned, [d_rows] + sent[: early - 1])
+    d_weight, d_bias = last_grad(turned, partial, bias, sent[early - 1 :])
+    ours = lax.optimization_barrier((columns, *sent, bias))[:-1]
+    theirs = swap(pack(*ours), T, 1)
     d_kv_weight = kv_grad(
         (projected, aside, across, upper, lower), columns, sent, theirs
     )
-
-    held = None
-    for h in range(halves):
-        held = weight_grad(turned, d_parts[h], held, h, halves)
-    d_weight, d_bias = held
     return attended, d_queries, d_weight, d_bias.reshape(-1), d_kv_weight
 
 

time: 110 us -> 104 us (0.945)
  waiting for transfers between devices: 54.4 us -> 50.8 us
  starting transfers between devices: 29.6 us -> 28.4 us
    ppermute x27 -> x24, waiting for transfers between devices: 54.4 us -> 50.8 us  [swap(): return lax.ppermute(x, axes, [(i, i ^ bits) for i in range(size_of(axes))])]
    pallas_call x7 -> x6, Pallas kernels: 6.52 us -> 4.26 us  [the longest x1 2.95 us: last_grad(): pl.pallas_call(functools.partial(last_grad_kernel, len(grads)), in_specs=...]
    pallas_call x1, Pallas kernels: 0.94 us -> 2.2 us  [back(): pl.pallas_call(functools.partial(back_kernel, len(own)), in_specs=in_vmem...]
    ppermute x27 -> x24, starting transfers between devices: 29.6 us -> 28.4 us  [swap(): return lax.ppermute(x, axes, [(i, i ^ bits) for i in range(size_of(axes))])]
    unnamed x18 -> x20, local copies, waits for them, and re-layouts: 4.13 us -> 4.13 us
  transfers between devices with their start and end apart: 27 -> 24, of which waited for: 18 -> 15; matrix products, arithmetic and copies ran while one was open for 0% -> 0% of each run, Pallas kernels for 9% -> 7%
where the time goes in v3:
time: 104 us
  waiting for transfers between devices  50.8 us (49%)
  starting transfers between devices  28.4 us (27%)
  Pallas kernels  19.3 us (19%)
  local copies, waits for them, and re-layouts  4.27 us (4%)
    ppermute x24, waiting for transfers between devices, swap(): return lax.ppermute(x, axes, [(i, i ^ bits) for i in range(size_of(axes))])  50.8 us
    ppermute x24, starting transfers between devices, swap(): return lax.ppermute(x, axes, [(i, i ^ bits) for i in range(size_of(axes))])  28.4 us
    unnamed x20, local copies, waits for them, and re-layouts  4.13 us
    pallas_call x1, Pallas kernels, project(): pl.pallas_call(functools.partial(project_kernel, len(own)), in_specs=in_v...  3.09 us
    pallas_call x1, Pallas kernels, attend(): pl.pallas_call(functools.partial(attend_kernel, 1 + len(arrived)), out_sh...  3.03 us
    pallas_call x1, Pallas kernels, last_grad(): pl.pallas_call(functools.partial(last_grad_kernel, len(grads)), in_specs=...  2.95 us
    pallas_call x1, Pallas kernels, back(): pl.pallas_call(functools.partial(back_kernel, len(own)), in_specs=in_vmem...  2.2 us
  transfers between devices with their start and end apart: 24, of which 15 were waited for; matrix products, arithmetic and copies ran while one was open for 0% of the time, Pallas kernels for 7%

profile of v3, /device:TPU:0, one launch (start us, length us, event | category | flops | bytes accessed | tf_op | source)
XLA Modules:
  0.0 103.6 jit_solution(3127825694468194232)
XLA Ops:
  0.6 3.1 %collective-permute-start = (bf16[64,1920]{1,0:T(8,128)(2,1)}, bf16[64,1920]{1,0:T(8,128)(2,1)S(1)}, u32[]{:S(2)}, u32[]{:S(2)}) collective-permute-start(bf16[64,1920]{1,0:T(8,128)(2,1)} %refs_0_.1), channel_id=1, source_target_pairs={{0,2},{1,3},{2,0},{3,1},{4,6},{5,7},{6,4},{7,5},{8,10},{9,11},{10,... | collective-permute-start | bytes 737288 | tf_op jit(solution)/shard_map/ppermute | solution.py:30
  3.7 2.6 %collective-permute-start.1 = (bf16[64,1920]{1,0:T(8,128)(2,1)}, bf16[64,1920]{1,0:T(8,128)(2,1)S(1)}, u32[]{:S(2)}, u32[]{:S(2)}) collective-permute-start(bf16[64,1920]{1,0:T(8,128)(2,1)} %refs_0_.1), channel_id=1, source_target_pairs={{0,4},{1,5},{2,6},{3,7},{4,0},{5,1},{6,2},{7,3},{8,12},{9,13},{10,... | collective-permute-start | bytes 737288 | tf_op jit(solution)/shard_map/ppermute | solution.py:30
  6.3 8.1 %collective-permute-done.refs_1_ = bf16[64,1920]{1,0:T(8,128)(2,1)S(1)} collective-permute-done((bf16[64,1920]{1,0:T(8,128)(2,1)}, bf16[64,1920]{1,0:T(8,128)(2,1)S(1)}, u32[]{:S(2)}, u32[]{:S(2)}) %collective-permute-start) | collective-permute-done | bytes 245792 | tf_op jit(solution)/shard_map/ppermute | solution.py:30
  14.4 2.1 %copy-done.2 = bf16[1920,1024]{1,0:T(8,128)(2,1)S(1)} copy-done((bf16[1920,1024]{1,0:T(8,128)(2,1)S(1)}, bf16[1920,1024]{1,0:T(8,128)(2,1)}, u32[]{:S(2)}) %copy-start.2) | copy-done | bytes 3932184
  17.6 6.7 %collective-permute-done.1.refs_0_ = bf16[64,1920]{1,0:T(8,128)(2,1)S(1)} collective-permute-done((bf16[64,1920]{1,0:T(8,128)(2,1)}, bf16[64,1920]{1,0:T(8,128)(2,1)S(1)}, u32[]{:S(2)}, u32[]{:S(2)}) %collective-permute-start.1) | collective-permute-done | bytes 245792 | tf_op jit(solution)/shard_map/ppermute | solution.py:30
  24.4 1.8 %collective-permute-done.4.refs_3_ = bf16[2,64,1920]{2,1,0:T(8,128)(2,1)S(1)} collective-permute-done((bf16[2,64,1920]{2,1,0:T(8,128)(2,1)S(1)}, bf16[2,64,1920]{2,1,0:T(8,128)(2,1)S(1)}, u32[]{:S(2)}, u32[]{:S(2)}) %collective-permute-start.4) | collective-permute-done | bytes 491552 | tf_op jit(solution)/shard_map/ppermute | solution.py:30
  26.2 3.1 %project.1 = (bf16[128,1024]{1,0:T(8,128)(2,1)S(1)}, bf16[128,1024]{1,0:T(8,128)(2,1)S(1)}, bf16[128,1024]{1,0:T(8,128)(2,1)S(1)}, bf16[128,1024]{1,0:T(8,128)(2,1)S(1)}, bf16[4,128,1920]{2,1,0:T(8,128)(2,1)S(1)}) custom-call(bf16[2,64,1920]{2,1,0:T(8,128)(2,1)S(1)} %pack.4.refs_0_, bf16[2,64,1920]{2,1,0:T(8,128)(2,1)S(1)} %pack.5.refs_1_, ...), custom_call_target="tpu_custom_call" | custom-call | flops 201326592 | bytes 196608 | tf_op jit(solution)/shard_map/project/pallas_call | solution.py:229
  29.3 1.6 %collective-permute-start.5 = (bf16[128,1024]{1,0:T(8,128)(2,1)S(1)}, bf16[128,1024]{1,0:T(8,128)(2,1)S(1)}, u32[]{:S(2)}, u32[]{:S(2)}) collective-permute-start(bf16[128,1024]{1,0:T(8,128)(2,1)S(1)} %get-tuple-element.55), channel_id=1, source_target_pairs={{0,8},{8,0},{16,24},{24,16},{1,9},{9,1},{17,25},{25,17},{2,10},{10... | collective-permute-start | bytes 786440 | tf_op jit(solution)/shard_map/ppermute | solution.py:30
  30.9 1.5 %collective-permute-start.6 = (bf16[128,1024]{1,0:T(8,128)(2,1)S(1)}, bf16[128,1024]{1,0:T(8,128)(2,1)S(1)}, u32[]{:S(2)}, u32[]{:S(2)}) collective-permute-start(bf16[128,1024]{1,0:T(8,128)(2,1)S(1)} %get-tuple-element.56), channel_id=1, source_target_pairs={{0,16},{8,24},{16,0},{24,8},{1,17},{9,25},{17,1},{25,9},{2,18},{10... | collective-permute-start | bytes 786440 | tf_op jit(solution)/shard_map/ppermute | solution.py:30
  32.9 4.8 %collective-permute-done.5.refs_0_ = bf16[128,1024]{1,0:T(8,128)(2,1)S(1)} collective-permute-done((bf16[128,1024]{1,0:T(8,128)(2,1)S(1)}, bf16[128,1024]{1,0:T(8,128)(2,1)S(1)}, u32[]{:S(2)}, u32[]{:S(2)}) %collective-permute-start.5) | collective-permute-done | bytes 262176 | tf_op jit(solution)/shard_map/ppermute | solution.py:30
  37.7 2.4 %collective-permute-done.6.refs_1_ = bf16[128,1024]{1,0:T(8,128)(2,1)S(1)} collective-permute-done((bf16[128,1024]{1,0:T(8,128)(2,1)S(1)}, bf16[128,1024]{1,0:T(8,128)(2,1)S(1)}, u32[]{:S(2)}, u32[]{:S(2)}) %collective-permute-start.6) | collective-permute-done | bytes 262176 | tf_op jit(solution)/shard_map/ppermute | solution.py:30
  40.1 4.4 %collective-permute-done.7.refs_2_ = bf16[128,1024]{1,0:T(8,128)(2,1)S(1)} collective-permute-done((bf16[128,1024]{1,0:T(8,128)(2,1)S(1)}, bf16[128,1024]{1,0:T(8,128)(2,1)S(1)}, u32[]{:S(2)}, u32[]{:S(2)}) %collective-permute-start.7) | collective-permute-done | bytes 262176 | tf_op jit(solution)/shard_map/ppermute | solution.py:30
  47.8 1.5 %collective-permute-start.12 = (bf16[128,1024]{1,0:T(8,128)(2,1)S(1)}, bf16[128,1024]{1,0:T(8,128)(2,1)S(1)}, u32[]{:S(2)}, u32[]{:S(2)}) collective-permute-start(bf16[128,1024]{1,0:T(8,128)(2,1)S(1)} %get-tuple-element.64.projected.refs_0_), channel_id=1, source_target_pairs={{0,8},{8,0},{16,24},{24,16},{1,9},{9,1},{17,25},{25,17},{2,10},{10... | collective-permute-start | bytes 786440 | tf_op jit(solution)/shard_map/ppermute | solution.py:30
  49.3 1.5 %collective-permute-start.13 = (bf16[128,1024]{1,0:T(8,128)(2,1)S(1)}, bf16[128,1024]{1,0:T(8,128)(2,1)S(1)}, u32[]{:S(2)}, u32[]{:S(2)}) collective-permute-start(bf16[128,1024]{1,0:T(8,128)(2,1)S(1)} %get-tuple-element.64.projected.refs_0_), channel_id=1, source_target_pairs={{0,16},{8,24},{16,0},{24,8},{1,17},{9,25},{17,1},{25,9},{2,18},{10... | collective-permute-start | bytes 786440 | tf_op jit(solution)/shard_map/ppermute | solution.py:30
  50.8 5.4 %collective-permute-start.10 = (bf16[128,256]{1,0:T(8,128)(2,1)}, bf16[128,256]{1,0:T(8,128)(2,1)S(1)}, u32[]{:S(2)}, u32[]{:S(2)}) collective-permute-start(bf16[128,256]{1,0:T(8,128)(2,1)} %get-tuple-element.62), channel_id=1, source_target_pairs={{0,4},{1,5},{2,6},{3,7},{4,0},{5,1},{6,2},{7,3},{8,12},{9,13},{10,... | collective-permute-start | bytes 196616 | tf_op jit(solution)/shard_map/ppermute | solution.py:30
  56.2 1.4 %collective-permute-start.11 = (bf16[128,256]{1,0:T(8,128)(2,1)}, bf16[128,256]{1,0:T(8,128)(2,1)}, u32[]{:S(2)}, u32[]{:S(2)}) collective-permute-start(bf16[128,256]{1,0:T(8,128)(2,1)} %get-tuple-element.63), channel_id=1, source_target_pairs={{0,6},{1,7},{2,4},{3,5},{4,2},{5,3},{6,0},{7,1},{8,14},{9,15},{10,... | collective-permute-start | bytes 196616 | tf_op jit(solution)/shard_map/ppermute | solution.py:30
  57.7 3.4 %collective-permute-done.10.refs_2_ = bf16[128,256]{1,0:T(8,128)(2,1)S(1)} collective-permute-done((bf16[128,256]{1,0:T(8,128)(2,1)}, bf16[128,256]{1,0:T(8,128)(2,1)S(1)}, u32[]{:S(2)}, u32[]{:S(2)}) %collective-permute-start.10) | collective-permute-done | bytes 65568 | tf_op jit(solution)/shard_map/ppermute | solution.py:30
  61.0 1.6 %collective-permute-done.11.refs_3_ = bf16[128,256]{1,0:T(8,128)(2,1)} collective-permute-done((bf16[128,256]{1,0:T(8,128)(2,1)}, bf16[128,256]{1,0:T(8,128)(2,1)}, u32[]{:S(2)}, u32[]{:S(2)}) %collective-permute-start.11) | collective-permute-done | bytes 65568 | tf_op jit(solution)/shard_map/ppermute | solution.py:30
  63.9 3.0 %attend.1 = (bf16[128,256]{1,0:T(8,128)(2,1)S(1)}, bf16[128,256]{1,0:T(8,128)(2,1)S(1)}, bf16[8,128,256]{2,1,0:T(8,128)(2,1)S(1)}, bf16[8,128,256]{2,1,0:T(8,128)(2,1)S(1)}) custom-call(f32[128,256]{1,0:T(8,128)S(1)} %get-tuple-element.60.refs_0_, bf16[128,256]{1,0:T(8,128)(2,1)} %collective-permute-done.9.refs_1_, ...), custom_call_target="tpu_custom_call" | custom-call | flops 107374184 | bytes 104857 | tf_op jit(solution)/shard_map/attend/pallas_call | solution.py:329
  68.5 2.3 %collective-permute-start.15 = (bf16[128,256]{1,0:T(8,128)(2,1)S(1)}, bf16[128,256]{1,0:T(8,128)(2,1)S(1)}, u32[]{:S(2)}, u32[]{:S(2)}) collective-permute-start(bf16[128,256]{1,0:T(8,128)(2,1)S(1)} %get-tuple-element.84.refs_0_), channel_id=1, source_target_pairs={{0,4},{1,5},{2,6},{3,7},{4,0},{5,1},{6,2},{7,3},{8,12},{9,13},{10,... | collective-permute-start | bytes 196616 | tf_op jit(solution)/shard_map/ppermute | solution.py:30
  70.8 1.7 %collective-permute-start.16 = (bf16[128,256]{1,0:T(8,128)(2,1)S(1)}, bf16[128,256]{1,0:T(8,128)(2,1)S(1)}, u32[]{:S(2)}, u32[]{:S(2)}) collective-permute-start(bf16[128,256]{1,0:T(8,128)(2,1)S(1)} %get-tuple-element.84.refs_0_), channel_id=1, source_target_pairs={{0,6},{1,7},{2,4},{3,5},{4,2},{5,3},{6,0},{7,1},{8,14},{9,15},{10,... | collective-permute-start | bytes 196616 | tf_op jit(solution)/shard_map/ppermute | solution.py:30
  73.4 1.5 %finish.1 = (bf16[256,1024]{1,0:T(8,128)(2,1)}, bf16[256,1024]{1,0:T(8,128)(2,1)}) custom-call(bf16[128,256]{1,0:T(8,128)(2,1)S(1)} %get-tuple-element.72.kv, bf16[8,128,256]{2,1,0:T(8,128)(2,1)S(1)} %get-tuple-element.73.probs, bf16[8,128,256]{2,1,0:T(8,128)(2,1)S(1)} %get-tuple-element.74.dscores), custom_call_target="tpu_custom_call" | custom-call | flops 53687092 | bytes 104857 | tf_op jit(solution)/shard_map/finish/pallas_call | solution.py:358
  74.9 2.0 %collective-permute-done.16.refs_3_ = bf16[128,256]{1,0:T(8,128)(2,1)S(1)} collective-permute-done((bf16[128,256]{1,0:T(8,128)(2,1)S(1)}, bf16[128,256]{1,0:T(8,128)(2,1)S(1)}, u32[]{:S(2)}, u32[]{:S(2)}) %collective-permute-start.16) | collective-permute-done | bytes 65568 | tf_op jit(solution)/shard_map/ppermute | solution.py:30
  77.0 1.5 %collective-permute-done.19.refs_4_ = bf16[4,128,256]{2,1,0:T(8,128)(2,1)S(1)} collective-permute-done((bf16[4,128,256]{2,1,0:T(8,128)(2,1)S(1)}, bf16[4,128,256]{2,1,0:T(8,128)(2,1)S(1)}, u32[]{:S(2)}, u32[]{:S(2)}) %collective-permute-start.19) | collective-permute-done | bytes 262176 | tf_op jit(solution)/shard_map/ppermute | solution.py:30
  78.5 2.2 %back.1 = (bf16[128,1024]{1,0:T(8,128)(2,1)S(1)}, bf16[128,1280]{1,0:T(8,128)(2,1)S(1)}, bf16[128,1280]{1,0:T(8,128)(2,1)S(1)}, bf16[128,1280]{1,0:T(8,128)(2,1)...) custom-call(bf16[128,256]{1,0:T(8,128)(2,1)S(1)} %get-tuple-element.84.refs_0_, ...), custom_call_target="tpu_custom_call" | custom-call | flops 107374184 | bytes 209715 | tf_op jit(solution)/shard_map/back/pallas_call | solution.py:435
  80.7 1.5 %collective-permute-start.20 = (bf16[128,1280]{1,0:T(8,128)(2,1)S(1)}, bf16[128,1280]{1,0:T(8,128)(2,1)S(1)}, u32[]{:S(2)}, u32[]{:S(2)}) collective-permute-start(bf16[128,1280]{1,0:T(8,128)(2,1)S(1)} %get-tuple-element.89), channel_id=1, source_target_pairs={{0,8},{8,0},{16,24},{24,16},{1,9},{9,1},{17,25},{25,17},{2,10},{10... | collective-permute-start | bytes 983048 | tf_op jit(solution)/shard_map/ppermute | solution.py:30
  82.2 1.5 %collective-permute-start.21 = (bf16[128,1280]{1,0:T(8,128)(2,1)S(1)}, bf16[128,1280]{1,0:T(8,128)(2,1)S(1)}, u32[]{:S(2)}, u32[]{:S(2)}) collective-permute-start(bf16[128,1280]{1,0:T(8,128)(2,1)S(1)} %get-tuple-element.92), channel_id=1, source_target_pairs={{0,16},{8,24},{16,0},{24,8},{1,17},{9,25},{17,1},{25,9},{2,18},{10... | collective-permute-start | bytes 983048 | tf_op jit(solution)/shard_map/ppermute | solution.py:30
  84.2 6.3 %collective-permute-done.20.refs_1_.refs_6_ = bf16[128,1280]{1,0:T(8,128)(2,1)S(1)} collective-permute-done((bf16[128,1280]{1,0:T(8,128)(2,1)S(1)}, bf16[128,1280]{1,0:T(8,128)(2,1)S(1)}, u32[]{:S(2)}, u32[]{:S(2)}) %collective-permute-start.20) | collective-permute-done | bytes 327712 | tf_op jit(solution)/shard_map/ppermute | solution.py:30
  90.5 1.2 %first_grad.1 = (f32[1920,1024]{1,0:T(8,128)S(1)}, f32[1,1024]{1,0:T(1,128)S(1)}) custom-call(bf16[1920,512]{1,0:T(8,128)(2,1)S(1)} %turn.1.feats, bf16[128,1024]{1,0:T(8,128)(2,1)S(1)} %get-tuple-element.88.refs_0_, bf16[128,1280]{1,0:T(8,128)(2,1)S(1)} %collective-permute-done.20.refs_1_.refs_6_), custom_call_target="tpu_custom_call" | custom-call | flops 50331648 | bytes 393216 | tf_op jit(solution)/shard_map/first_grad/pallas_call | solution.py:516
  92.8 5.8 %collective-permute-done.22.refs_1_.refs_3_.refs_8_ = bf16[128,1280]{1,0:T(8,128)(2,1)S(1)} collective-permute-done((bf16[128,1280]{1,0:T(8,128)(2,1)S(1)}, bf16[128,1280]{1,0:T(8,128)(2,1)S(1)}, u32[]{:S(2)}, u32[]{:S(2)}) %collective-permute-start.22) | collective-permute-done | bytes 327712 | tf_op jit(solution)/shard_map/ppermute | solution.py:30
  98.8 2.9 %last_grad.1 = (bf16[1920,1024]{1,0:T(8,128)(2,1)}, f32[1,1024]{1,0:T(1,128)}) custom-call(bf16[1920,512]{1,0:T(8,128)(2,1)S(1)} %turn.1.feats, f32[1920,1024]{1,0:T(8,128)S(1)} %get-tuple-element.90.before, f32[1,1024]{1,0:T(1,128)S(1)} %get-tuple-element.91.bias_before, bf16[128,1280]{1,0:T(8,128)(2,1)S(1)} %collective-permute-done.21.refs_0_.refs_2_.refs_7_, ...), custom_call_target="tpu_custom_call" | custom-call | flops 50331648 | bytes 589824 | tf_op jit(solution)/shard_map/last_grad/pallas_call | solution.py:553
  101.7 1.9 %kv_grad.1 = bf16[1024,512]{1,0:T(8,128)(2,1)} custom-call(bf16[128,1024]{1,0:T(8,128)(2,1)S(1)} %get-tuple-element.64.projected.refs_0_, bf16[128,1024]{1,0:T(8,128)(2,1)S(1)} %collective-permute-done.12.refs_1_, bf16[128,1024]{1,0:T(8,128)(2,1)S(1)} %collective-permute-done.13.refs_2_, bf16[64,1024]{1,0:T(8,128)(2,1)S(1)} %collective-permute-done.17.refs_3_, ...), custom_call_target="tpu_custom_call" | custom-call | flops 26843544 | bytes 104857 | tf_op jit(solution)/shard_map/kv_grad/pallas_call | solution.py:478
  (55 shorter events, 10.5 us)
Async XLA Ops:
  0.6 13.8 %collective-permute-start = (bf16[64,1920]{1,0:T(8,128)(2,1)}, bf16[64,1920]{1,0:T(8,128)(2,1)S(1)}, u32[]{:S(2)}, u32[]{:S(2)}) collective-permute-start(bf16[64,1920]{1,0:T(8,128)(2,1)} %refs_0_.1), channel_id=1, source_target_pairs={{0,2},{1,3},{2,0},{3,1},{4,6},{5,7},{6,4},{7,5},{8,10},{9,11},{10,... | collective-permute-start | bytes 737288 | tf_op jit(solution)/shard_map/ppermute | solution.py:30
  3.7 20.5 %collective-permute-start.1 = (bf16[64,1920]{1,0:T(8,128)(2,1)}, bf16[64,1920]{1,0:T(8,128)(2,1)S(1)}, u32[]{:S(2)}, u32[]{:S(2)}) collective-permute-start(bf16[64,1920]{1,0:T(8,128)(2,1)} %refs_0_.1), channel_id=1, source_target_pairs={{0,4},{1,5},{2,6},{3,7},{4,0},{5,1},{6,2},{7,3},{8,12},{9,13},{10,... | collective-permute-start | bytes 737288 | tf_op jit(solution)/shard_map/ppermute | solution.py:30
  6.3 17.9 %collective-permute-start.2 = (bf16[64,1920]{1,0:T(8,128)(2,1)}, bf16[64,1920]{1,0:T(8,128)(2,1)S(1)}, u32[]{:S(2)}, u32[]{:S(2)}) collective-permute-start(bf16[64,1920]{1,0:T(8,128)(2,1)} %refs_0_.1), channel_id=1, source_target_pairs={{0,6},{1,7},{2,4},{3,5},{4,2},{5,3},{6,0},{7,1},{8,14},{9,15},{10,... | collective-permute-start | bytes 737288 | tf_op jit(solution)/shard_map/ppermute | solution.py:30
  14.4 2.1 %copy-start.2 = (bf16[1920,1024]{1,0:T(8,128)(2,1)S(1)}, bf16[1920,1024]{1,0:T(8,128)(2,1)}, u32[]{:S(2)}) copy-start(bf16[1920,1024]{1,0:T(8,128)(2,1)} %refs_4_.3) | copy-start | bytes 11796484
  17.4 8.8 %copy-start.3 = (bf16[1920,1024]{1,0:T(8,128)(2,1)S(1)}, bf16[1920,1024]{1,0:T(8,128)(2,1)}, u32[]{:S(2)}) copy-start(bf16[1920,1024]{1,0:T(8,128)(2,1)} %refs_4_.3) | copy-start | bytes 11796484
  17.5 15.4 %copy-start.8 = (bf16[1024]{0:T(1024)(128)(2,1)S(1)}, bf16[1024]{0:T(1024)(128)(2,1)}, u32[]{:S(2)}) copy-start(bf16[1024]{0:T(1024)(128)(2,1)} %param.10) | copy-start | bytes 6148
  17.5 27.0 %copy-start = (bf16[1024,2048]{1,0:T(8,128)(2,1)S(1)}, bf16[1024,2048]{1,0:T(8,128)(2,1)}, u32[]{:S(2)}) copy-start(bf16[1024,2048]{1,0:T(8,128)(2,1)} %refs_5_.3) | copy-start | bytes 12582916
  17.5 6.9 %collective-permute-start.3 = (bf16[2,64,1920]{2,1,0:T(8,128)(2,1)S(1)}, bf16[2,64,1920]{2,1,0:T(8,128)(2,1)S(1)}, u32[]{:S(2)}, u32[]{:S(2)}) collective-permute-start(bf16[2,64,1920]{2,1,0:T(8,128)(2,1)S(1)} %pack.4.refs_0_), channel_id=1, source_target_pairs={{0,1},{1,0},{2,3},{3,2},{4,5},{5,4},{6,7},{7,6},{8,9},{9,8},{10,11... | collective-permute-start | bytes 1474568 | tf_op jit(solution)/shard_map/ppermute | solution.py:30
  24.3 1.9 %collective-permute-start.4 = (bf16[2,64,1920]{2,1,0:T(8,128)(2,1)S(1)}, bf16[2,64,1920]{2,1,0:T(8,128)(2,1)S(1)}, u32[]{:S(2)}, u32[]{:S(2)}) collective-permute-start(bf16[2,64,1920]{2,1,0:T(8,128)(2,1)S(1)} %pack.5.refs_1_), channel_id=1, source_target_pairs={{0,1},{1,0},{2,3},{3,2},{4,5},{5,4},{6,7},{7,6},{8,9},{9,8},{10,11... | collective-permute-start | bytes 1474568 | tf_op jit(solution)/shard_map/ppermute | solution.py:30
  29.3 8.4 %collective-permute-start.5 = (bf16[128,1024]{1,0:T(8,128)(2,1)S(1)}, bf16[128,1024]{1,0:T(8,128)(2,1)S(1)}, u32[]{:S(2)}, u32[]{:S(2)}) collective-permute-start(bf16[128,1024]{1,0:T(8,128)(2,1)S(1)} %get-tuple-element.55), channel_id=1, source_target_pairs={{0,8},{8,0},{16,24},{24,16},{1,9},{9,1},{17,25},{25,17},{2,10},{10... | collective-permute-start | bytes 786440 | tf_op jit(solution)/shard_map/ppermute | solution.py:30
  30.9 9.2 %collective-permute-start.6 = (bf16[128,1024]{1,0:T(8,128)(2,1)S(1)}, bf16[128,1024]{1,0:T(8,128)(2,1)S(1)}, u32[]{:S(2)}, u32[]{:S(2)}) collective-permute-start(bf16[128,1024]{1,0:T(8,128)(2,1)S(1)} %get-tuple-element.56), channel_id=1, source_target_pairs={{0,16},{8,24},{16,0},{24,8},{1,17},{9,25},{17,1},{25,9},{2,18},{10... | collective-permute-start | bytes 786440 | tf_op jit(solution)/shard_map/ppermute | solution.py:30
  32.4 12.1 %collective-permute-start.7 = (bf16[128,1024]{1,0:T(8,128)(2,1)S(1)}, bf16[128,1024]{1,0:T(8,128)(2,1)S(1)}, u32[]{:S(2)}, u32[]{:S(2)}) collective-permute-start(bf16[128,1024]{1,0:T(8,128)(2,1)S(1)} %get-tuple-element.57), channel_id=1, source_target_pairs={{0,24},{8,16},{16,8},{24,0},{1,25},{9,17},{17,9},{25,1},{2,26},{10... | collective-permute-start | bytes 786440 | tf_op jit(solution)/shard_map/ppermute | solution.py:30
  45.4 12.1 %copy-start.9 = (s32[1,128]{1,0:T(1,128)S(1)}, s32[1,128]{1,0:T(1,128)}, u32[]{:S(2)}) copy-start(s32[1,128]{1,0:T(1,128)} %param.14) | copy-start | bytes 1540
  45.4 17.4 %copy-start.4 = (bf16[256,1024]{1,0:T(8,128)(2,1)S(1)}, bf16[256,1024]{1,0:T(8,128)(2,1)}, u32[]{:S(2)}) copy-start(bf16[256,1024]{1,0:T(8,128)(2,1)} %refs_4_.5) | copy-start | bytes 1572868
  45.5 17.4 %copy-start.7 = (s32[1,256]{1,0:T(1,128)S(1)}, s32[1,256]{1,0:T(1,128)}, u32[]{:S(2)}) copy-start(s32[1,256]{1,0:T(1,128)} %refs_7_.1) | copy-start | bytes 3076
  45.5 1.6 %collective-permute-start.8 = (bf16[4,128,256]{2,1,0:T(8,128)(2,1)S(1)}, bf16[4,128,256]{2,1,0:T(8,128)(2,1)S(1)}, u32[]{:S(2)}, u32[]{:S(2)}) collective-permute-start(bf16[4,128,256]{2,1,0:T(8,128)(2,1)S(1)} %get-tuple-element.59), channel_id=1, source_target_pairs={{0,1},{1,0},{2,3},{3,2},{4,5},{5,4},{6,7},{7,6},{8,9},{9,8},{10,11... | collective-permute-start | bytes 786440 | tf_op jit(solution)/shard_map/ppermute | solution.py:30
  47.8 15.1 %collective-permute-start.12 = (bf16[128,1024]{1,0:T(8,128)(2,1)S(1)}, bf16[128,1024]{1,0:T(8,128)(2,1)S(1)}, u32[]{:S(2)}, u32[]{:S(2)}) collective-permute-start(bf16[128,1024]{1,0:T(8,128)(2,1)S(1)} %get-tuple-element.64.projected.refs_0_), channel_id=1, source_target_pairs={{0,8},{8,0},{16,24},{24,16},{1,9},{9,1},{17,25},{25,17},{2,10},{10... | collective-permute-start | bytes 786440 | tf_op jit(solution)/shard_map/ppermute | solution.py:30
  49.3 13.6 %collective-permute-start.13 = (bf16[128,1024]{1,0:T(8,128)(2,1)S(1)}, bf16[128,1024]{1,0:T(8,128)(2,1)S(1)}, u32[]{:S(2)}, u32[]{:S(2)}) collective-permute-start(bf16[128,1024]{1,0:T(8,128)(2,1)S(1)} %get-tuple-element.64.projected.refs_0_), channel_id=1, source_target_pairs={{0,16},{8,24},{16,0},{24,8},{1,17},{9,25},{17,1},{25,9},{2,18},{10... | collective-permute-start | bytes 786440 | tf_op jit(solution)/shard_map/ppermute | solution.py:30
  50.8 10.3 %collective-permute-start.10 = (bf16[128,256]{1,0:T(8,128)(2,1)}, bf16[128,256]{1,0:T(8,128)(2,1)S(1)}, u32[]{:S(2)}, u32[]{:S(2)}) collective-permute-start(bf16[128,256]{1,0:T(8,128)(2,1)} %get-tuple-element.62), channel_id=1, source_target_pairs={{0,4},{1,5},{2,6},{3,7},{4,0},{5,1},{6,2},{7,3},{8,12},{9,13},{10,... | collective-permute-start | bytes 196616 | tf_op jit(solution)/shard_map/ppermute | solution.py:30
  56.2 6.5 %collective-permute-start.11 = (bf16[128,256]{1,0:T(8,128)(2,1)}, bf16[128,256]{1,0:T(8,128)(2,1)}, u32[]{:S(2)}, u32[]{:S(2)}) collective-permute-start(bf16[128,256]{1,0:T(8,128)(2,1)} %get-tuple-element.63), channel_id=1, source_target_pairs={{0,6},{1,7},{2,4},{3,5},{4,2},{5,3},{6,0},{7,1},{8,14},{9,15},{10,... | collective-permute-start | bytes 196616 | tf_op jit(solution)/shard_map/ppermute | solution.py:30
  57.6 5.3 %collective-permute-start.9 = (bf16[128,256]{1,0:T(8,128)(2,1)}, bf16[128,256]{1,0:T(8,128)(2,1)}, u32[]{:S(2)}, u32[]{:S(2)}) collective-permute-start(bf16[128,256]{1,0:T(8,128)(2,1)} %get-tuple-element.61), channel_id=1, source_target_pairs={{0,2},{1,3},{2,0},{3,1},{4,6},{5,7},{6,4},{7,5},{8,10},{9,11},{10,... | collective-permute-start | bytes 196616 | tf_op jit(solution)/shard_map/ppermute | solution.py:30
  57.7 20.8 %copy-start.1 = (bf16[1024,2048]{1,0:T(8,128)(2,1)S(1)}, bf16[1024,2048]{1,0:T(8,128)(2,1)}, u32[]{:S(2)}) copy-start(bf16[1024,2048]{1,0:T(8,128)(2,1)} %refs_5_.3) | copy-start | bytes 12582916
  67.0 9.9 %collective-permute-start.17 = (bf16[64,1024]{1,0:T(8,128)(2,1)S(1)}, bf16[64,1024]{1,0:T(8,128)(2,1)S(1)}, u32[]{:S(2)}, u32[]{:S(2)}) collective-permute-start(bf16[64,1024]{1,0:T(8,128)(2,1)S(1)} %slice.6), channel_id=1, source_target_pairs={{0,8},{8,0},{16,24},{24,16},{1,9},{9,1},{17,25},{25,17},{2,10},{10... | collective-permute-start | bytes 393224 | tf_op jit(solution)/shard_map/ppermute | solution.py:30
  67.6 9.3 %collective-permute-start.18 = (bf16[64,1024]{1,0:T(8,128)(2,1)S(1)}, bf16[64,1024]{1,0:T(8,128)(2,1)S(1)}, u32[]{:S(2)}, u32[]{:S(2)}) collective-permute-start(bf16[64,1024]{1,0:T(8,128)(2,1)S(1)} %slice.7), channel_id=1, source_target_pairs={{0,16},{8,24},{16,0},{24,8},{1,17},{9,25},{17,1},{25,9},{2,18},{10... | collective-permute-start | bytes 393224 | tf_op jit(solution)/shard_map/ppermute | solution.py:30
  68.1 6.8 %collective-permute-start.14 = (bf16[128,256]{1,0:T(8,128)(2,1)S(1)}, bf16[128,256]{1,0:T(8,128)(2,1)S(1)}, u32[]{:S(2)}, u32[]{:S(2)}) collective-permute-start(bf16[128,256]{1,0:T(8,128)(2,1)S(1)} %get-tuple-element.84.refs_0_), channel_id=1, source_target_pairs={{0,2},{1,3},{2,0},{3,1},{4,6},{5,7},{6,4},{7,5},{8,10},{9,11},{10,... | collective-permute-start | bytes 196616 | tf_op jit(solution)/shard_map/ppermute | solution.py:30
  68.5 6.4 %collective-permute-start.15 = (bf16[128,256]{1,0:T(8,128)(2,1)S(1)}, bf16[128,256]{1,0:T(8,128)(2,1)S(1)}, u32[]{:S(2)}, u32[]{:S(2)}) collective-permute-start(bf16[128,256]{1,0:T(8,128)(2,1)S(1)} %get-tuple-element.84.refs_0_), channel_id=1, source_target_pairs={{0,4},{1,5},{2,6},{3,7},{4,0},{5,1},{6,2},{7,3},{8,12},{9,13},{10,... | collective-permute-start | bytes 196616 | tf_op jit(solution)/shard_map/ppermute | solution.py:30
  70.8 6.1 %collective-permute-start.16 = (bf16[128,256]{1,0:T(8,128)(2,1)S(1)}, bf16[128,256]{1,0:T(8,128)(2,1)S(1)}, u32[]{:S(2)}, u32[]{:S(2)}) collective-permute-start(bf16[128,256]{1,0:T(8,128)(2,1)S(1)} %get-tuple-element.84.refs_0_), channel_id=1, source_target_pairs={{0,6},{1,7},{2,4},{3,5},{4,2},{5,3},{6,0},{7,1},{8,14},{9,15},{10,... | collective-permute-start | bytes 196616 | tf_op jit(solution)/shard_map/ppermute | solution.py:30
  76.9 1.6 %collective-permute-start.19 = (bf16[4,128,256]{2,1,0:T(8,128)(2,1)S(1)}, bf16[4,128,256]{2,1,0:T(8,128)(2,1)S(1)}, u32[]{:S(2)}, u32[]{:S(2)}) collective-permute-start(bf16[4,128,256]{2,1,0:T(8,128)(2,1)S(1)} %pack.6), channel_id=1, source_target_pairs={{0,1},{1,0},{2,3},{3,2},{4,5},{5,4},{6,7},{7,6},{8,9},{9,8},{10,11... | collective-permute-start | bytes 786440 | tf_op jit(solution)/shard_map/ppermute | solution.py:30
  80.7 9.8 %collective-permute-start.20 = (bf16[128,1280]{1,0:T(8,128)(2,1)S(1)}, bf16[128,1280]{1,0:T(8,128)(2,1)S(1)}, u32[]{:S(2)}, u32[]{:S(2)}) collective-permute-start(bf16[128,1280]{1,0:T(8,128)(2,1)S(1)} %get-tuple-element.89), channel_id=1, source_target_pairs={{0,8},{8,0},{16,24},{24,16},{1,9},{9,1},{17,25},{25,17},{2,10},{10... | collective-permute-start | bytes 983048 | tf_op jit(solution)/shard_map/ppermute | solution.py:30
  82.2 10.6 %collective-permute-start.21 = (bf16[128,1280]{1,0:T(8,128)(2,1)S(1)}, bf16[128,1280]{1,0:T(8,128)(2,1)S(1)}, u32[]{:S(2)}, u32[]{:S(2)}) collective-permute-start(bf16[128,1280]{1,0:T(8,128)(2,1)S(1)} %get-tuple-element.92), channel_id=1, source_target_pairs={{0,16},{8,24},{16,0},{24,8},{1,17},{9,25},{17,1},{25,9},{2,18},{10... | collective-permute-start | bytes 983048 | tf_op jit(solution)/shard_map/ppermute | solution.py:30
  83.7 15.0 %collective-permute-start.22 = (bf16[128,1280]{1,0:T(8,128)(2,1)S(1)}, bf16[128,1280]{1,0:T(8,128)(2,1)S(1)}, u32[]{:S(2)}, u32[]{:S(2)}) collective-permute-start(bf16[128,1280]{1,0:T(8,128)(2,1)S(1)} %get-tuple-element.93), channel_id=1, source_target_pairs={{0,24},{8,16},{16,8},{24,0},{1,25},{9,17},{17,9},{25,1},{2,26},{10... | collective-permute-start | bytes 983048 | tf_op jit(solution)/shard_map/ppermute | solution.py:30
  98.7 3.0 %collective-permute-start.23 = (bf16[4,128,256]{2,1,0:T(8,128)(2,1)S(1)}, bf16[4,128,256]{2,1,0:T(8,128)(2,1)S(1)}, u32[]{:S(2)}, u32[]{:S(2)}) collective-permute-start(bf16[4,128,256]{2,1,0:T(8,128)(2,1)S(1)} %pack.7), channel_id=1, source_target_pairs={{0,1},{1,0},{2,3},{3,2},{4,5},{5,4},{6,7},{7,6},{8,9},{9,8},{10,11... | collective-permute-start | bytes 786440 | tf_op jit(solution)/shard_map/ppermute | solution.py:30
  (2 other events, 2.0 us)

commit v4 on v3

--- a/solution.py
+++ b/solution.py
@@ -449,7 +449,8 @@
 
 def kv_grad_kernel(count, parts, *refs):
     place = place_of()
-    left, mine, (theirs, out, right) = refs[:count], refs[count : count + parts], refs[-3:]
+    left, mine = refs[:count], refs[count : count + parts]
+    theirs, out, right, rounded, sems = refs[count + parts :]
     rows = left[0].shape[0]
     extra = mine[0].shape[1]
     for j in range(parts):
@@ -463,12 +464,21 @@
     depth = out.shape[0]
     count = tiles_of(depth, 256)
     tile = depth // count
+    copies = []
     for n in range(count):
         at = slice(n * tile, (n + 1) * tile)
         lhs = jnp.concatenate([x[:, at] for x in left], axis=0)
-        out[at, :] = lax.dot_general(
+        rounded[at, :] = lax.dot_general(
             lhs, right[...], TN, preferred_element_type=F32
         ).astype(BF16)
+        rows_at = pl.ds(n * tile, tile)
+        copy = pltpu.make_async_copy(
+            rounded.at[rows_at, :], out.at[rows_at, :], sems.at[n]
+        )
+        copy.start()
+        copies.append(copy)
+    for copy in copies:
+        copy.wait()
 
 
 def kv_grad(left, own, sent, theirs):
@@ -479,7 +489,12 @@
         functools.partial(kv_grad_kernel, len(left), parts),
         in_specs=in_vmem(len(left) + parts + 1),
         out_shape=jax.ShapeDtypeStruct((depth, 2 * extra), BF16),
-        scratch_shapes=[pltpu.VMEM((parts * rows, 2 * extra), BF16)],
+        out_specs=pl.BlockSpec(memory_space=pl.ANY),
+        scratch_shapes=[
+            pltpu.VMEM((parts * rows, 2 * extra), BF16),
+            pltpu.VMEM((depth, 2 * extra), BF16),
+            pltpu.SemaphoreType.DMA((tiles_of(depth, 256),)),
+        ],
         compiler_params=params(),
         cost_estimate=cost(4 * parts * rows * depth * extra, 4 * parts * rows * depth),
         name="kv_grad",

time: 104 us -> 104 us (level)
  no operation moved by 1% of the time
where the time goes in v4:
time: 104 us; the launch traced here: 103 us
  waiting for transfers between devices  50.8 us (49%)
  starting transfers between devices  28.4 us (27%)
  Pallas kernels  19 us (18%)
  local copies, waits for them, and re-layouts  4.27 us (4%)
    ppermute x24, waiting for transfers between devices, swap(): return lax.ppermute(x, axes, [(i, i ^ bits) for i in range(size_of(axes))])  50.8 us
    ppermute x24, starting transfers between devices, swap(): return lax.ppermute(x, axes, [(i, i ^ bits) for i in range(size_of(axes))])  28.4 us
    unnamed x20, local copies, waits for them, and re-layouts  4.13 us
    pallas_call x1, Pallas kernels, project(): pl.pallas_call(functools.partial(project_kernel, len(own)), in_specs=in_v...  3.09 us
    pallas_call x1, Pallas kernels, attend(): pl.pallas_call(functools.partial(attend_kernel, 1 + len(arrived)), out_sh...  3.03 us
    pallas_call x1, Pallas kernels, last_grad(): pl.pallas_call(functools.partial(last_grad_kernel, len(grads)), in_specs=...  2.95 us
    pallas_call x1, Pallas kernels, back(): pl.pallas_call(functools.partial(back_kernel, len(own)), in_specs=in_vmem...  2.2 us
  transfers between devices with their start and end apart: 24, of which 15 were waited for; matrix products, arithmetic and copies ran while one was open for 0% of the time, Pallas kernels for 7%

profile of v4, /device:TPU:0, one launch (start us, length us, event | category | flops | bytes accessed | tf_op | source)
XLA Modules:
  0.0 103.4 jit_solution(17533055693450155724)
XLA Ops:
  0.6 3.1 %collective-permute-start = (bf16[64,1920]{1,0:T(8,128)(2,1)}, bf16[64,1920]{1,0:T(8,128)(2,1)S(1)}, u32[]{:S(2)}, u32[]{:S(2)}) collective-permute-start(bf16[64,1920]{1,0:T(8,128)(2,1)} %refs_0_.1), channel_id=1, source_target_pairs={{0,2},{1,3},{2,0},{3,1},{4,6},{5,7},{6,4},{7,5},{8,10},{9,11},{10,... | collective-permute-start | bytes 737288 | tf_op jit(solution)/shard_map/ppermute | solution.py:30
  3.7 2.6 %collective-permute-start.1 = (bf16[64,1920]{1,0:T(8,128)(2,1)}, bf16[64,1920]{1,0:T(8,128)(2,1)S(1)}, u32[]{:S(2)}, u32[]{:S(2)}) collective-permute-start(bf16[64,1920]{1,0:T(8,128)(2,1)} %refs_0_.1), channel_id=1, source_target_pairs={{0,4},{1,5},{2,6},{3,7},{4,0},{5,1},{6,2},{7,3},{8,12},{9,13},{10,... | collective-permute-start | bytes 737288 | tf_op jit(solution)/shard_map/ppermute | solution.py:30
  6.3 8.1 %collective-permute-done.refs_1_ = bf16[64,1920]{1,0:T(8,128)(2,1)S(1)} collective-permute-done((bf16[64,1920]{1,0:T(8,128)(2,1)}, bf16[64,1920]{1,0:T(8,128)(2,1)S(1)}, u32[]{:S(2)}, u32[]{:S(2)}) %collective-permute-start) | collective-permute-done | bytes 245792 | tf_op jit(solution)/shard_map/ppermute | solution.py:30
  14.4 2.1 %copy-done.2 = bf16[1920,1024]{1,0:T(8,128)(2,1)S(1)} copy-done((bf16[1920,1024]{1,0:T(8,128)(2,1)S(1)}, bf16[1920,1024]{1,0:T(8,128)(2,1)}, u32[]{:S(2)}) %copy-start.2) | copy-done | bytes 3932184
  17.6 6.7 %collective-permute-done.1.refs_0_ = bf16[64,1920]{1,0:T(8,128)(2,1)S(1)} collective-permute-done((bf16[64,1920]{1,0:T(8,128)(2,1)}, bf16[64,1920]{1,0:T(8,128)(2,1)S(1)}, u32[]{:S(2)}, u32[]{:S(2)}) %collective-permute-start.1) | collective-permute-done | bytes 245792 | tf_op jit(solution)/shard_map/ppermute | solution.py:30
  24.4 1.8 %collective-permute-done.4.refs_3_ = bf16[2,64,1920]{2,1,0:T(8,128)(2,1)S(1)} collective-permute-done((bf16[2,64,1920]{2,1,0:T(8,128)(2,1)S(1)}, bf16[2,64,1920]{2,1,0:T(8,128)(2,1)S(1)}, u32[]{:S(2)}, u32[]{:S(2)}) %collective-permute-start.4) | collective-permute-done | bytes 491552 | tf_op jit(solution)/shard_map/ppermute | solution.py:30
  26.2 3.1 %project.1 = (bf16[128,1024]{1,0:T(8,128)(2,1)S(1)}, bf16[128,1024]{1,0:T(8,128)(2,1)S(1)}, bf16[128,1024]{1,0:T(8,128)(2,1)S(1)}, bf16[128,1024]{1,0:T(8,128)(2,1)S(1)}, bf16[4,128,1920]{2,1,0:T(8,128)(2,1)S(1)}) custom-call(bf16[2,64,1920]{2,1,0:T(8,128)(2,1)S(1)} %pack.4.refs_0_, bf16[2,64,1920]{2,1,0:T(8,128)(2,1)S(1)} %pack.5.refs_1_, ...), custom_call_target="tpu_custom_call" | custom-call | flops 201326592 | bytes 196608 | tf_op jit(solution)/shard_map/project/pallas_call | solution.py:229
  29.3 1.6 %collective-permute-start.5 = (bf16[128,1024]{1,0:T(8,128)(2,1)S(1)}, bf16[128,1024]{1,0:T(8,128)(2,1)S(1)}, u32[]{:S(2)}, u32[]{:S(2)}) collective-permute-start(bf16[128,1024]{1,0:T(8,128)(2,1)S(1)} %get-tuple-element.55), channel_id=1, source_target_pairs={{0,8},{8,0},{16,24},{24,16},{1,9},{9,1},{17,25},{25,17},{2,10},{10... | collective-permute-start | bytes 786440 | tf_op jit(solution)/shard_map/ppermute | solution.py:30
  30.9 1.5 %collective-permute-start.6 = (bf16[128,1024]{1,0:T(8,128)(2,1)S(1)}, bf16[128,1024]{1,0:T(8,128)(2,1)S(1)}, u32[]{:S(2)}, u32[]{:S(2)}) collective-permute-start(bf16[128,1024]{1,0:T(8,128)(2,1)S(1)} %get-tuple-element.56), channel_id=1, source_target_pairs={{0,16},{8,24},{16,0},{24,8},{1,17},{9,25},{17,1},{25,9},{2,18},{10... | collective-permute-start | bytes 786440 | tf_op jit(solution)/shard_map/ppermute | solution.py:30
  32.9 4.8 %collective-permute-done.5.refs_0_ = bf16[128,1024]{1,0:T(8,128)(2,1)S(1)} collective-permute-done((bf16[128,1024]{1,0:T(8,128)(2,1)S(1)}, bf16[128,1024]{1,0:T(8,128)(2,1)S(1)}, u32[]{:S(2)}, u32[]{:S(2)}) %collective-permute-start.5) | collective-permute-done | bytes 262176 | tf_op jit(solution)/shard_map/ppermute | solution.py:30
  37.7 2.4 %collective-permute-done.6.refs_1_ = bf16[128,1024]{1,0:T(8,128)(2,1)S(1)} collective-permute-done((bf16[128,1024]{1,0:T(8,128)(2,1)S(1)}, bf16[128,1024]{1,0:T(8,128)(2,1)S(1)}, u32[]{:S(2)}, u32[]{:S(2)}) %collective-permute-start.6) | collective-permute-done | bytes 262176 | tf_op jit(solution)/shard_map/ppermute | solution.py:30
  40.1 4.4 %collective-permute-done.7.refs_2_ = bf16[128,1024]{1,0:T(8,128)(2,1)S(1)} collective-permute-done((bf16[128,1024]{1,0:T(8,128)(2,1)S(1)}, bf16[128,1024]{1,0:T(8,128)(2,1)S(1)}, u32[]{:S(2)}, u32[]{:S(2)}) %collective-permute-start.7) | collective-permute-done | bytes 262176 | tf_op jit(solution)/shard_map/ppermute | solution.py:30
  47.8 1.5 %collective-permute-start.12 = (bf16[128,1024]{1,0:T(8,128)(2,1)S(1)}, bf16[128,1024]{1,0:T(8,128)(2,1)S(1)}, u32[]{:S(2)}, u32[]{:S(2)}) collective-permute-start(bf16[128,1024]{1,0:T(8,128)(2,1)S(1)} %get-tuple-element.64.projected.refs_0_), channel_id=1, source_target_pairs={{0,8},{8,0},{16,24},{24,16},{1,9},{9,1},{17,25},{25,17},{2,10},{10... | collective-permute-start | bytes 786440 | tf_op jit(solution)/shard_map/ppermute | solution.py:30
  49.3 1.5 %collective-permute-start.13 = (bf16[128,1024]{1,0:T(8,128)(2,1)S(1)}, bf16[128,1024]{1,0:T(8,128)(2,1)S(1)}, u32[]{:S(2)}, u32[]{:S(2)}) collective-permute-start(bf16[128,1024]{1,0:T(8,128)(2,1)S(1)} %get-tuple-element.64.projected.refs_0_), channel_id=1, source_target_pairs={{0,16},{8,24},{16,0},{24,8},{1,17},{9,25},{17,1},{25,9},{2,18},{10... | collective-permute-start | bytes 786440 | tf_op jit(solution)/shard_map/ppermute | solution.py:30
  50.8 5.4 %collective-permute-start.10 = (bf16[128,256]{1,0:T(8,128)(2,1)}, bf16[128,256]{1,0:T(8,128)(2,1)S(1)}, u32[]{:S(2)}, u32[]{:S(2)}) collective-permute-start(bf16[128,256]{1,0:T(8,128)(2,1)} %get-tuple-element.62), channel_id=1, source_target_pairs={{0,4},{1,5},{2,6},{3,7},{4,0},{5,1},{6,2},{7,3},{8,12},{9,13},{10,... | collective-permute-start | bytes 196616 | tf_op jit(solution)/shard_map/ppermute | solution.py:30
  56.2 1.4 %collective-permute-start.11 = (bf16[128,256]{1,0:T(8,128)(2,1)}, bf16[128,256]{1,0:T(8,128)(2,1)}, u32[]{:S(2)}, u32[]{:S(2)}) collective-permute-start(bf16[128,256]{1,0:T(8,128)(2,1)} %get-tuple-element.63), channel_id=1, source_target_pairs={{0,6},{1,7},{2,4},{3,5},{4,2},{5,3},{6,0},{7,1},{8,14},{9,15},{10,... | collective-permute-start | bytes 196616 | tf_op jit(solution)/shard_map/ppermute | solution.py:30
  57.7 3.4 %collective-permute-done.10.refs_2_ = bf16[128,256]{1,0:T(8,128)(2,1)S(1)} collective-permute-done((bf16[128,256]{1,0:T(8,128)(2,1)}, bf16[128,256]{1,0:T(8,128)(2,1)S(1)}, u32[]{:S(2)}, u32[]{:S(2)}) %collective-permute-start.10) | collective-permute-done | bytes 65568 | tf_op jit(solution)/shard_map/ppermute | solution.py:30
  61.0 1.6 %collective-permute-done.11.refs_3_ = bf16[128,256]{1,0:T(8,128)(2,1)} collective-permute-done((bf16[128,256]{1,0:T(8,128)(2,1)}, bf16[128,256]{1,0:T(8,128)(2,1)}, u32[]{:S(2)}, u32[]{:S(2)}) %collective-permute-start.11) | collective-permute-done | bytes 65568 | tf_op jit(solution)/shard_map/ppermute | solution.py:30
  63.9 3.0 %attend.1 = (bf16[128,256]{1,0:T(8,128)(2,1)S(1)}, bf16[128,256]{1,0:T(8,128)(2,1)S(1)}, bf16[8,128,256]{2,1,0:T(8,128)(2,1)S(1)}, bf16[8,128,256]{2,1,0:T(8,128)(2,1)S(1)}) custom-call(f32[128,256]{1,0:T(8,128)S(1)} %get-tuple-element.60.refs_0_, bf16[128,256]{1,0:T(8,128)(2,1)} %collective-permute-done.9.refs_1_, ...), custom_call_target="tpu_custom_call" | custom-call | flops 107374184 | bytes 104857 | tf_op jit(solution)/shard_map/attend/pallas_call | solution.py:329
  68.5 2.3 %collective-permute-start.15 = (bf16[128,256]{1,0:T(8,128)(2,1)S(1)}, bf16[128,256]{1,0:T(8,128)(2,1)S(1)}, u32[]{:S(2)}, u32[]{:S(2)}) collective-permute-start(bf16[128,256]{1,0:T(8,128)(2,1)S(1)} %get-tuple-element.84.refs_0_), channel_id=1, source_target_pairs={{0,4},{1,5},{2,6},{3,7},{4,0},{5,1},{6,2},{7,3},{8,12},{9,13},{10,... | collective-permute-start | bytes 196616 | tf_op jit(solution)/shard_map/ppermute | solution.py:30
  70.8 1.7 %collective-permute-start.16 = (bf16[128,256]{1,0:T(8,128)(2,1)S(1)}, bf16[128,256]{1,0:T(8,128)(2,1)S(1)}, u32[]{:S(2)}, u32[]{:S(2)}) collective-permute-start(bf16[128,256]{1,0:T(8,128)(2,1)S(1)} %get-tuple-element.84.refs_0_), channel_id=1, source_target_pairs={{0,6},{1,7},{2,4},{3,5},{4,2},{5,3},{6,0},{7,1},{8,14},{9,15},{10,... | collective-permute-start | bytes 196616 | tf_op jit(solution)/shard_map/ppermute | solution.py:30
  73.4 1.5 %finish.1 = (bf16[256,1024]{1,0:T(8,128)(2,1)}, bf16[256,1024]{1,0:T(8,128)(2,1)}) custom-call(bf16[128,256]{1,0:T(8,128)(2,1)S(1)} %get-tuple-element.72.kv, bf16[8,128,256]{2,1,0:T(8,128)(2,1)S(1)} %get-tuple-element.73.probs, bf16[8,128,256]{2,1,0:T(8,128)(2,1)S(1)} %get-tuple-element.74.dscores), custom_call_target="tpu_custom_call" | custom-call | flops 53687092 | bytes 104857 | tf_op jit(solution)/shard_map/finish/pallas_call | solution.py:358
  74.9 2.0 %collective-permute-done.16.refs_3_ = bf16[128,256]{1,0:T(8,128)(2,1)S(1)} collective-permute-done((bf16[128,256]{1,0:T(8,128)(2,1)S(1)}, bf16[128,256]{1,0:T(8,128)(2,1)S(1)}, u32[]{:S(2)}, u32[]{:S(2)}) %collective-permute-start.16) | collective-permute-done | bytes 65568 | tf_op jit(solution)/shard_map/ppermute | solution.py:30
  77.0 1.5 %collective-permute-done.19.refs_4_ = bf16[4,128,256]{2,1,0:T(8,128)(2,1)S(1)} collective-permute-done((bf16[4,128,256]{2,1,0:T(8,128)(2,1)S(1)}, bf16[4,128,256]{2,1,0:T(8,128)(2,1)S(1)}, u32[]{:S(2)}, u32[]{:S(2)}) %collective-permute-start.19) | collective-permute-done | bytes 262176 | tf_op jit(solution)/shard_map/ppermute | solution.py:30
  78.5 2.2 %back.1 = (bf16[128,1024]{1,0:T(8,128)(2,1)S(1)}, bf16[128,1280]{1,0:T(8,128)(2,1)S(1)}, bf16[128,1280]{1,0:T(8,128)(2,1)S(1)}, bf16[128,1280]{1,0:T(8,128)(2,1)...) custom-call(bf16[128,256]{1,0:T(8,128)(2,1)S(1)} %get-tuple-element.84.refs_0_, ...), custom_call_target="tpu_custom_call" | custom-call | flops 107374184 | bytes 209715 | tf_op jit(solution)/shard_map/back/pallas_call | solution.py:435
  80.7 1.5 %collective-permute-start.20 = (bf16[128,1280]{1,0:T(8,128)(2,1)S(1)}, bf16[128,1280]{1,0:T(8,128)(2,1)S(1)}, u32[]{:S(2)}, u32[]{:S(2)}) collective-permute-start(bf16[128,1280]{1,0:T(8,128)(2,1)S(1)} %get-tuple-element.89), channel_id=1, source_target_pairs={{0,8},{8,0},{16,24},{24,16},{1,9},{9,1},{17,25},{25,17},{2,10},{10... | collective-permute-start | bytes 983048 | tf_op jit(solution)/shard_map/ppermute | solution.py:30
  82.2 1.5 %collective-permute-start.21 = (bf16[128,1280]{1,0:T(8,128)(2,1)S(1)}, bf16[128,1280]{1,0:T(8,128)(2,1)S(1)}, u32[]{:S(2)}, u32[]{:S(2)}) collective-permute-start(bf16[128,1280]{1,0:T(8,128)(2,1)S(1)} %get-tuple-element.92), channel_id=1, source_target_pairs={{0,16},{8,24},{16,0},{24,8},{1,17},{9,25},{17,1},{25,9},{2,18},{10... | collective-permute-start | bytes 983048 | tf_op jit(solution)/shard_map/ppermute | solution.py:30
  84.2 6.3 %collective-permute-done.20.refs_1_.refs_6_ = bf16[128,1280]{1,0:T(8,128)(2,1)S(1)} collective-permute-done((bf16[128,1280]{1,0:T(8,128)(2,1)S(1)}, bf16[128,1280]{1,0:T(8,128)(2,1)S(1)}, u32[]{:S(2)}, u32[]{:S(2)}) %collective-permute-start.20) | collective-permute-done | bytes 327712 | tf_op jit(solution)/shard_map/ppermute | solution.py:30
  90.5 1.2 %first_grad.1 = (f32[1920,1024]{1,0:T(8,128)S(1)}, f32[1,1024]{1,0:T(1,128)S(1)}) custom-call(bf16[1920,512]{1,0:T(8,128)(2,1)S(1)} %turn.1.feats, bf16[128,1024]{1,0:T(8,128)(2,1)S(1)} %get-tuple-element.88.refs_0_, bf16[128,1280]{1,0:T(8,128)(2,1)S(1)} %collective-permute-done.20.refs_1_.refs_6_), custom_call_target="tpu_custom_call" | custom-call | flops 50331648 | bytes 393216 | tf_op jit(solution)/shard_map/first_grad/pallas_call | solution.py:531
  92.8 5.8 %collective-permute-done.22.refs_1_.refs_3_.refs_8_ = bf16[128,1280]{1,0:T(8,128)(2,1)S(1)} collective-permute-done((bf16[128,1280]{1,0:T(8,128)(2,1)S(1)}, bf16[128,1280]{1,0:T(8,128)(2,1)S(1)}, u32[]{:S(2)}, u32[]{:S(2)}) %collective-permute-start.22) | collective-permute-done | bytes 327712 | tf_op jit(solution)/shard_map/ppermute | solution.py:30
  98.8 2.9 %last_grad.1 = (bf16[1920,1024]{1,0:T(8,128)(2,1)}, f32[1,1024]{1,0:T(1,128)}) custom-call(bf16[1920,512]{1,0:T(8,128)(2,1)S(1)} %turn.1.feats, f32[1920,1024]{1,0:T(8,128)S(1)} %get-tuple-element.90.before, f32[1,1024]{1,0:T(1,128)S(1)} %get-tuple-element.91.bias_before, bf16[128,1280]{1,0:T(8,128)(2,1)S(1)} %collective-permute-done.21.refs_0_.refs_2_.refs_7_, ...), custom_call_target="tpu_custom_call" | custom-call | flops 50331648 | bytes 589824 | tf_op jit(solution)/shard_map/last_grad/pallas_call | solution.py:568
  101.7 1.6 %kv_grad.1 = bf16[1024,512]{1,0:T(8,128)(2,1)} custom-call(bf16[128,1024]{1,0:T(8,128)(2,1)S(1)} %get-tuple-element.64.projected.refs_0_, bf16[128,1024]{1,0:T(8,128)(2,1)S(1)} %collective-permute-done.12.refs_1_, bf16[128,1024]{1,0:T(8,128)(2,1)S(1)} %collective-permute-done.13.refs_2_, bf16[64,1024]{1,0:T(8,128)(2,1)S(1)} %collective-permute-done.17.refs_3_, ...), custom_call_target="tpu_custom_call" | custom-call | flops 26843544 | bytes 104857 | tf_op jit(solution)/shard_map/kv_grad/pallas_call | solution.py:488
  (55 shorter events, 10.5 us)
Async XLA Ops:
  0.6 13.8 %collective-permute-start = (bf16[64,1920]{1,0:T(8,128)(2,1)}, bf16[64,1920]{1,0:T(8,128)(2,1)S(1)}, u32[]{:S(2)}, u32[]{:S(2)}) collective-permute-start(bf16[64,1920]{1,0:T(8,128)(2,1)} %refs_0_.1), channel_id=1, source_target_pairs={{0,2},{1,3},{2,0},{3,1},{4,6},{5,7},{6,4},{7,5},{8,10},{9,11},{10,... | collective-permute-start | bytes 737288 | tf_op jit(solution)/shard_map/ppermute | solution.py:30
  3.7 20.5 %collective-permute-start.1 = (bf16[64,1920]{1,0:T(8,128)(2,1)}, bf16[64,1920]{1,0:T(8,128)(2,1)S(1)}, u32[]{:S(2)}, u32[]{:S(2)}) collective-permute-start(bf16[64,1920]{1,0:T(8,128)(2,1)} %refs_0_.1), channel_id=1, source_target_pairs={{0,4},{1,5},{2,6},{3,7},{4,0},{5,1},{6,2},{7,3},{8,12},{9,13},{10,... | collective-permute-start | bytes 737288 | tf_op jit(solution)/shard_map/ppermute | solution.py:30
  6.3 17.9 %collective-permute-start.2 = (bf16[64,1920]{1,0:T(8,128)(2,1)}, bf16[64,1920]{1,0:T(8,128)(2,1)S(1)}, u32[]{:S(2)}, u32[]{:S(2)}) collective-permute-start(bf16[64,1920]{1,0:T(8,128)(2,1)} %refs_0_.1), channel_id=1, source_target_pairs={{0,6},{1,7},{2,4},{3,5},{4,2},{5,3},{6,0},{7,1},{8,14},{9,15},{10,... | collective-permute-start | bytes 737288 | tf_op jit(solution)/shard_map/ppermute | solution.py:30
  14.4 2.1 %copy-start.2 = (bf16[1920,1024]{1,0:T(8,128)(2,1)S(1)}, bf16[1920,1024]{1,0:T(8,128)(2,1)}, u32[]{:S(2)}) copy-start(bf16[1920,1024]{1,0:T(8,128)(2,1)} %refs_4_.3) | copy-start | bytes 11796484
  17.4 8.8 %copy-start.3 = (bf16[1920,1024]{1,0:T(8,128)(2,1)S(1)}, bf16[1920,1024]{1,0:T(8,128)(2,1)}, u32[]{:S(2)}) copy-start(bf16[1920,1024]{1,0:T(8,128)(2,1)} %refs_4_.3) | copy-start | bytes 11796484
  17.5 15.4 %copy-start.8 = (bf16[1024]{0:T(1024)(128)(2,1)S(1)}, bf16[1024]{0:T(1024)(128)(2,1)}, u32[]{:S(2)}) copy-start(bf16[1024]{0:T(1024)(128)(2,1)} %param.10) | copy-start | bytes 6148
  17.5 27.0 %copy-start = (bf16[1024,2048]{1,0:T(8,128)(2,1)S(1)}, bf16[1024,2048]{1,0:T(8,128)(2,1)}, u32[]{:S(2)}) copy-start(bf16[1024,2048]{1,0:T(8,128)(2,1)} %refs_5_.3) | copy-start | bytes 12582916
  17.5 6.9 %collective-permute-start.3 = (bf16[2,64,1920]{2,1,0:T(8,128)(2,1)S(1)}, bf16[2,64,1920]{2,1,0:T(8,128)(2,1)S(1)}, u32[]{:S(2)}, u32[]{:S(2)}) collective-permute-start(bf16[2,64,1920]{2,1,0:T(8,128)(2,1)S(1)} %pack.4.refs_0_), channel_id=1, source_target_pairs={{0,1},{1,0},{2,3},{3,2},{4,5},{5,4},{6,7},{7,6},{8,9},{9,8},{10,11... | collective-permute-start | bytes 1474568 | tf_op jit(solution)/shard_map/ppermute | solution.py:30
  24.3 1.9 %collective-permute-start.4 = (bf16[2,64,1920]{2,1,0:T(8,128)(2,1)S(1)}, bf16[2,64,1920]{2,1,0:T(8,128)(2,1)S(1)}, u32[]{:S(2)}, u32[]{:S(2)}) collective-permute-start(bf16[2,64,1920]{2,1,0:T(8,128)(2,1)S(1)} %pack.5.refs_1_), channel_id=1, source_target_pairs={{0,1},{1,0},{2,3},{3,2},{4,5},{5,4},{6,7},{7,6},{8,9},{9,8},{10,11... | collective-permute-start | bytes 1474568 | tf_op jit(solution)/shard_map/ppermute | solution.py:30
  29.3 8.4 %collective-permute-start.5 = (bf16[128,1024]{1,0:T(8,128)(2,1)S(1)}, bf16[128,1024]{1,0:T(8,128)(2,1)S(1)}, u32[]{:S(2)}, u32[]{:S(2)}) collective-permute-start(bf16[128,1024]{1,0:T(8,128)(2,1)S(1)} %get-tuple-element.55), channel_id=1, source_target_pairs={{0,8},{8,0},{16,24},{24,16},{1,9},{9,1},{17,25},{25,17},{2,10},{10... | collective-permute-start | bytes 786440 | tf_op jit(solution)/shard_map/ppermute | solution.py:30
  30.9 9.2 %collective-permute-start.6 = (bf16[128,1024]{1,0:T(8,128)(2,1)S(1)}, bf16[128,1024]{1,0:T(8,128)(2,1)S(1)}, u32[]{:S(2)}, u32[]{:S(2)}) collective-permute-start(bf16[128,1024]{1,0:T(8,128)(2,1)S(1)} %get-tuple-element.56), channel_id=1, source_target_pairs={{0,16},{8,24},{16,0},{24,8},{1,17},{9,25},{17,1},{25,9},{2,18},{10... | collective-permute-start | bytes 786440 | tf_op jit(solution)/shard_map/ppermute | solution.py:30
  32.4 12.1 %collective-permute-start.7 = (bf16[128,1024]{1,0:T(8,128)(2,1)S(1)}, bf16[128,1024]{1,0:T(8,128)(2,1)S(1)}, u32[]{:S(2)}, u32[]{:S(2)}) collective-permute-start(bf16[128,1024]{1,0:T(8,128)(2,1)S(1)} %get-tuple-element.57), channel_id=1, source_target_pairs={{0,24},{8,16},{16,8},{24,0},{1,25},{9,17},{17,9},{25,1},{2,26},{10... | collective-permute-start | bytes 786440 | tf_op jit(solution)/shard_map/ppermute | solution.py:30
  45.4 12.1 %copy-start.9 = (s32[1,128]{1,0:T(1,128)S(1)}, s32[1,128]{1,0:T(1,128)}, u32[]{:S(2)}) copy-start(s32[1,128]{1,0:T(1,128)} %param.14) | copy-start | bytes 1540
  45.4 17.4 %copy-start.4 = (bf16[256,1024]{1,0:T(8,128)(2,1)S(1)}, bf16[256,1024]{1,0:T(8,128)(2,1)}, u32[]{:S(2)}) copy-start(bf16[256,1024]{1,0:T(8,128)(2,1)} %refs_4_.5) | copy-start | bytes 1572868
  45.5 17.4 %copy-start.7 = (s32[1,256]{1,0:T(1,128)S(1)}, s32[1,256]{1,0:T(1,128)}, u32[]{:S(2)}) copy-start(s32[1,256]{1,0:T(1,128)} %refs_7_.1) | copy-start | bytes 3076
  45.5 1.6 %collective-permute-start.8 = (bf16[4,128,256]{2,1,0:T(8,128)(2,1)S(1)}, bf16[4,128,256]{2,1,0:T(8,128)(2,1)S(1)}, u32[]{:S(2)}, u32[]{:S(2)}) collective-permute-start(bf16[4,128,256]{2,1,0:T(8,128)(2,1)S(1)} %get-tuple-element.59), channel_id=1, source_target_pairs={{0,1},{1,0},{2,3},{3,2},{4,5},{5,4},{6,7},{7,6},{8,9},{9,8},{10,11... | collective-permute-start | bytes 786440 | tf_op jit(solution)/shard_map/ppermute | solution.py:30
  47.8 15.1 %collective-permute-start.12 = (bf16[128,1024]{1,0:T(8,128)(2,1)S(1)}, bf16[128,1024]{1,0:T(8,128)(2,1)S(1)}, u32[]{:S(2)}, u32[]{:S(2)}) collective-permute-start(bf16[128,1024]{1,0:T(8,128)(2,1)S(1)} %get-tuple-element.64.projected.refs_0_), channel_id=1, source_target_pairs={{0,8},{8,0},{16,24},{24,16},{1,9},{9,1},{17,25},{25,17},{2,10},{10... | collective-permute-start | bytes 786440 | tf_op jit(solution)/shard_map/ppermute | solution.py:30
  49.3 13.6 %collective-permute-start.13 = (bf16[128,1024]{1,0:T(8,128)(2,1)S(1)}, bf16[128,1024]{1,0:T(8,128)(2,1)S(1)}, u32[]{:S(2)}, u32[]{:S(2)}) collective-permute-start(bf16[128,1024]{1,0:T(8,128)(2,1)S(1)} %get-tuple-element.64.projected.refs_0_), channel_id=1, source_target_pairs={{0,16},{8,24},{16,0},{24,8},{1,17},{9,25},{17,1},{25,9},{2,18},{10... | collective-permute-start | bytes 786440 | tf_op jit(solution)/shard_map/ppermute | solution.py:30
  50.8 10.3 %collective-permute-start.10 = (bf16[128,256]{1,0:T(8,128)(2,1)}, bf16[128,256]{1,0:T(8,128)(2,1)S(1)}, u32[]{:S(2)}, u32[]{:S(2)}) collective-permute-start(bf16[128,256]{1,0:T(8,128)(2,1)} %get-tuple-element.62), channel_id=1, source_target_pairs={{0,4},{1,5},{2,6},{3,7},{4,0},{5,1},{6,2},{7,3},{8,12},{9,13},{10,... | collective-permute-start | bytes 196616 | tf_op jit(solution)/shard_map/ppermute | solution.py:30
  56.2 6.5 %collective-permute-start.11 = (bf16[128,256]{1,0:T(8,128)(2,1)}, bf16[128,256]{1,0:T(8,128)(2,1)}, u32[]{:S(2)}, u32[]{:S(2)}) collective-permute-start(bf16[128,256]{1,0:T(8,128)(2,1)} %get-tuple-element.63), channel_id=1, source_target_pairs={{0,6},{1,7},{2,4},{3,5},{4,2},{5,3},{6,0},{7,1},{8,14},{9,15},{10,... | collective-permute-start | bytes 196616 | tf_op jit(solution)/shard_map/ppermute | solution.py:30
  57.6 5.3 %collective-permute-start.9 = (bf16[128,256]{1,0:T(8,128)(2,1)}, bf16[128,256]{1,0:T(8,128)(2,1)}, u32[]{:S(2)}, u32[]{:S(2)}) collective-permute-start(bf16[128,256]{1,0:T(8,128)(2,1)} %get-tuple-element.61), channel_id=1, source_target_pairs={{0,2},{1,3},{2,0},{3,1},{4,6},{5,7},{6,4},{7,5},{8,10},{9,11},{10,... | collective-permute-start | bytes 196616 | tf_op jit(solution)/shard_map/ppermute | solution.py:30
  57.7 20.8 %copy-start.1 = (bf16[1024,2048]{1,0:T(8,128)(2,1)S(1)}, bf16[1024,2048]{1,0:T(8,128)(2,1)}, u32[]{:S(2)}) copy-start(bf16[1024,2048]{1,0:T(8,128)(2,1)} %refs_5_.3) | copy-start | bytes 12582916
  67.0 9.9 %collective-permute-start.17 = (bf16[64,1024]{1,0:T(8,128)(2,1)S(1)}, bf16[64,1024]{1,0:T(8,128)(2,1)S(1)}, u32[]{:S(2)}, u32[]{:S(2)}) collective-permute-start(bf16[64,1024]{1,0:T(8,128)(2,1)S(1)} %slice.6), channel_id=1, source_target_pairs={{0,8},{8,0},{16,24},{24,16},{1,9},{9,1},{17,25},{25,17},{2,10},{10... | collective-permute-start | bytes 393224 | tf_op jit(solution)/shard_map/ppermute | solution.py:30
  67.6 9.3 %collective-permute-start.18 = (bf16[64,1024]{1,0:T(8,128)(2,1)S(1)}, bf16[64,1024]{1,0:T(8,128)(2,1)S(1)}, u32[]{:S(2)}, u32[]{:S(2)}) collective-permute-start(bf16[64,1024]{1,0:T(8,128)(2,1)S(1)} %slice.7), channel_id=1, source_target_pairs={{0,16},{8,24},{16,0},{24,8},{1,17},{9,25},{17,1},{25,9},{2,18},{10... | collective-permute-start | bytes 393224 | tf_op jit(solution)/shard_map/ppermute | solution.py:30
  68.1 6.8 %collective-permute-start.14 = (bf16[128,256]{1,0:T(8,128)(2,1)S(1)}, bf16[128,256]{1,0:T(8,128)(2,1)S(1)}, u32[]{:S(2)}, u32[]{:S(2)}) collective-permute-start(bf16[128,256]{1,0:T(8,128)(2,1)S(1)} %get-tuple-element.84.refs_0_), channel_id=1, source_target_pairs={{0,2},{1,3},{2,0},{3,1},{4,6},{5,7},{6,4},{7,5},{8,10},{9,11},{10,... | collective-permute-start | bytes 196616 | tf_op jit(solution)/shard_map/ppermute | solution.py:30
  68.5 6.4 %collective-permute-start.15 = (bf16[128,256]{1,0:T(8,128)(2,1)S(1)}, bf16[128,256]{1,0:T(8,128)(2,1)S(1)}, u32[]{:S(2)}, u32[]{:S(2)}) collective-permute-start(bf16[128,256]{1,0:T(8,128)(2,1)S(1)} %get-tuple-element.84.refs_0_), channel_id=1, source_target_pairs={{0,4},{1,5},{2,6},{3,7},{4,0},{5,1},{6,2},{7,3},{8,12},{9,13},{10,... | collective-permute-start | bytes 196616 | tf_op jit(solution)/shard_map/ppermute | solution.py:30
  70.8 6.1 %collective-permute-start.16 = (bf16[128,256]{1,0:T(8,128)(2,1)S(1)}, bf16[128,256]{1,0:T(8,128)(2,1)S(1)}, u32[]{:S(2)}, u32[]{:S(2)}) collective-permute-start(bf16[128,256]{1,0:T(8,128)(2,1)S(1)} %get-tuple-element.84.refs_0_), channel_id=1, source_target_pairs={{0,6},{1,7},{2,4},{3,5},{4,2},{5,3},{6,0},{7,1},{8,14},{9,15},{10,... | collective-permute-start | bytes 196616 | tf_op jit(solution)/shard_map/ppermute | solution.py:30
  76.9 1.6 %collective-permute-start.19 = (bf16[4,128,256]{2,1,0:T(8,128)(2,1)S(1)}, bf16[4,128,256]{2,1,0:T(8,128)(2,1)S(1)}, u32[]{:S(2)}, u32[]{:S(2)}) collective-permute-start(bf16[4,128,256]{2,1,0:T(8,128)(2,1)S(1)} %pack.6), channel_id=1, source_target_pairs={{0,1},{1,0},{2,3},{3,2},{4,5},{5,4},{6,7},{7,6},{8,9},{9,8},{10,11... | collective-permute-start | bytes 786440 | tf_op jit(solution)/shard_map/ppermute | solution.py:30
  80.7 9.8 %collective-permute-start.20 = (bf16[128,1280]{1,0:T(8,128)(2,1)S(1)}, bf16[128,1280]{1,0:T(8,128)(2,1)S(1)}, u32[]{:S(2)}, u32[]{:S(2)}) collective-permute-start(bf16[128,1280]{1,0:T(8,128)(2,1)S(1)} %get-tuple-element.89), channel_id=1, source_target_pairs={{0,8},{8,0},{16,24},{24,16},{1,9},{9,1},{17,25},{25,17},{2,10},{10... | collective-permute-start | bytes 983048 | tf_op jit(solution)/shard_map/ppermute | solution.py:30
  82.2 10.6 %collective-permute-start.21 = (bf16[128,1280]{1,0:T(8,128)(2,1)S(1)}, bf16[128,1280]{1,0:T(8,128)(2,1)S(1)}, u32[]{:S(2)}, u32[]{:S(2)}) collective-permute-start(bf16[128,1280]{1,0:T(8,128)(2,1)S(1)} %get-tuple-element.92), channel_id=1, source_target_pairs={{0,16},{8,24},{16,0},{24,8},{1,17},{9,25},{17,1},{25,9},{2,18},{10... | collective-permute-start | bytes 983048 | tf_op jit(solution)/shard_map/ppermute | solution.py:30
  83.7 15.0 %collective-permute-start.22 = (bf16[128,1280]{1,0:T(8,128)(2,1)S(1)}, bf16[128,1280]{1,0:T(8,128)(2,1)S(1)}, u32[]{:S(2)}, u32[]{:S(2)}) collective-permute-start(bf16[128,1280]{1,0:T(8,128)(2,1)S(1)} %get-tuple-element.93), channel_id=1, source_target_pairs={{0,24},{8,16},{16,8},{24,0},{1,25},{9,17},{17,9},{25,1},{2,26},{10... | collective-permute-start | bytes 983048 | tf_op jit(solution)/shard_map/ppermute | solution.py:30
  98.7 3.0 %collective-permute-start.23 = (bf16[4,128,256]{2,1,0:T(8,128)(2,1)S(1)}, bf16[4,128,256]{2,1,0:T(8,128)(2,1)S(1)}, u32[]{:S(2)}, u32[]{:S(2)}) collective-permute-start(bf16[4,128,256]{2,1,0:T(8,128)(2,1)S(1)} %pack.7), channel_id=1, source_target_pairs={{0,1},{1,0},{2,3},{3,2},{4,5},{5,4},{6,7},{7,6},{8,9},{9,8},{10,11... | collective-permute-start | bytes 786440 | tf_op jit(solution)/shard_map/ppermute | solution.py:30
  (2 other events, 2.0 us)
